TPU v7x, 32 devices: a whole 2x2x4 slice. The times are simulated.
32 devices in a mesh: section: 2 (over core), seq: 4 (over z), head: 4 (over y, x).
Axes of the slice: x: 2, y: 2, z: 4, core: 2. Of those that a mesh axis runs over, the one named last changes fastest.
Arguments:
- tokens: bfloat16 [4, 1024, 1024], P(None, 'seq'), may hold values from -6 to 6
- slot_order: int32 [4], replicated, may hold values from 0 to 3, each once
- log_decay: float32 [2, 4, 32, 1024], P('section', None, 'head', 'seq'), may hold values from -0.6 to 0, as said below
- grad_out: bfloat16 [4, 1024, 1024], P(None, 'seq'), may hold values from -6 to 6
- in_gain: float32 [2, 1024], P('section'), may hold values from 0.1 to 1.9
- w_gate: bfloat16 [2, 1024, 2048], P('section', None, 'head'), may hold values from -0.1875 to 0.1875
- w_inner: bfloat16 [2, 1024, 2048], P('section', None, 'head'), may hold values from -0.1875 to 0.1875
- w_shared: bfloat16 [2, 1024, 256], P('section'), may hold values from -0.1875 to 0.1875
- conv_inner: float32 [2, 4, 2048], P('section', None, 'head'), may hold values from -3 to 3
- conv_shared: float32 [2, 4, 256], P('section'), may hold values from -3 to 3
- d_skip: float32 [2, 32], P('section', 'head'), may hold values from 0.1 to 1
- norm_gain: float32 [2, 2048], P('section', 'head'), may hold values from 0.1 to 1.9
- w_out: bfloat16 [2, 2048, 1024], P('section'), may hold values from -0.125 to 0.125
Outputs:
- section_out: float32 [2, 4, 1024, 1024], P('section', None, 'seq', 'head')
- input_grad: float32 [2, 4, 1024, 1024], P('section', None, 'seq', 'head')
- grad_in_gain: float32 [2, 1024], P('section', ('seq', 'head'))
- grad_w_gate: float32 [2, 1024, 2048], P('section', 'seq', 'head')
- grad_w_inner: float32 [2, 1024, 2048], P('section', 'seq', 'head')
- grad_w_shared: float32 [2, 1024, 256], P('section', ('seq', 'head'))
- grad_conv_inner: float32 [2, 4, 2048], P('section', None, 'head')
- grad_conv_shared: float32 [2, 4, 256], P('section', None, ('seq', 'head'))
- grad_d_skip: float32 [2, 32], P('section', 'head')
- grad_norm_gain: float32 [2, 2048], P('section', 'head')
- grad_w_out: float32 [2, 2048, 1024], P('section', 'head', 'seq')
Inputs may be any that keep to these rules, and one draw needn't show every extreme that they name: `log_decay`: every value is below zero. `slot_order`: names every micro-batch once.
All inputs are finite; a program needn't handle non-finite values.
Results may differ from a plain program's by a relative error of at most 0.03.
Values may be sent and summed in bfloat16 or wider, within the bound.
No kernel may reach another device: no remote copies, remote signals or barrier semaphores. Data moves between devices by JAX's collectives and lax.ppermute only.
A program may use at most 128 MiB of HBM per device.

v0:
```python
import functools

import jax
import jax.numpy as jnp
from jax import lax
from jax.experimental import pallas as pl
from jax.experimental.pallas import tpu as pltpu
from jax.sharding import PartitionSpec as P

BLOCK = 256
HALF = BLOCK // 2
PAD = 16
EPS = 1e-05
F32 = jnp.float32
LOW = jnp.bfloat16
HIDDEN = -1e30
NN = ((1,), (0,))
NT = ((1,), (1,))
TN = ((0,), (0,))
VMEM_BYTES = 50 * 1024 * 1024
ALL_VMEM_BYTES = 63 * 1024 * 1024


def dot(a, b, dims):
    return lax.dot_general(a, b, (dims, ((), ())), preferred_element_type=F32)


def aligned(start, size):
    return pl.ds(pl.multiple_of(start, size), size)


def spread(cols, first, count, width):
    rows = cols.shape[0]
    lane = lax.broadcasted_iota(jnp.int32, (rows, count * width), 1)
    out = jnp.broadcast_to(cols[:, first : first + 1], (rows, count * width))
    for h in range(1, count):
        out = jnp.where(lane >= h * width, cols[:, first + h : first + h + 1], out)
    return out


def per_head(array, h, width):
    lane = lax.broadcasted_iota(jnp.int32, array.shape, 1)
    inside = (lane >= h * width) & (lane < (h + 1) * width)
    return jnp.where(inside, array, jnp.zeros_like(array))


def split_low(value):
    high = value.astype(LOW).astype(F32)
    return high, value - high


def column_of(row, size):
    return jnp.transpose(jnp.broadcast_to(row, (128, size)))


def sigmoid(v):
    return 0.5 * jnp.tanh(0.5 * v) + 0.5


def pick(flag, a, b):
    return jnp.where(flag, a, b)


class Sizes:
    def __init__(self, blocks, width, channels, heads, states, taps, head_axis, inner):
        self.blocks = blocks
        self.width = width
        self.channels = channels
        self.heads = heads
        self.head_width = channels // heads
        self.states = states
        self.lin = channels + 2 * states
        self.taps = taps
        self.head_axis = head_axis
        self.chunk = width // head_axis
        self.rows = blocks * HALF
        self.tokens = blocks * BLOCK
        self.inner = inner


def weight_copies(sz, layer, c, h, given, dst, sems):
    ch = sz.channels
    cols = aligned(c * ch, ch)
    places = [dst.at[:, :ch], dst.at[:, ch : 2 * ch], dst.at[:, 2 * ch :]]
    own = [given[0].at[0, :, cols], given[1].at[0, :, cols], given[2].at[0]]
    return copies_for(layer, c, own, given[3:], places, sems)


def out_copies(sz, layer, c, h, given, dst, sems):
    rows = aligned((h * 2 + c) * sz.channels, sz.channels)
    return copies_for(layer, c, [given[0].at[0, rows, :]], given[1:], [dst], sems)


def copies_for(layer, c, own, sent, places, sems):
    both = []
    for flag, sources in ((c == layer, own), (c != layer, sent)):
        copies = [
            pltpu.make_async_copy(p, q, sems.at[i]) for i, (p, q) in enumerate(zip(sources, places))
        ]
        both.append((flag, copies))
    return both


def run_copies(choices, start, wait):
    for flag, copies in choices:

        @pl.when(flag)
        def _(copies=copies):
            if start:
                for copy in copies:
                    copy.start()
            if wait:
                for copy in copies:
                    copy.wait()


def put_ordered(sz, dst, c, k, b, own, other):
    for r in range(len(own)):

        @pl.when(lax.rem(k - b + len(own), len(own)) == r)
        def _(r=r):
            put_pair(dst, c, own[r][:HALF, :], other[r][:HALF, :])


def put_pair(dst, c, own, other):
    dst[aligned(c * HALF, HALF), :] = own
    dst[aligned((1 - c) * HALF, HALF), :] = other


def far_first(count):
    return [0] + list(range(count - 1, 0, -1))


def put_pieces(sz, dst, c, h, own, other):
    own, other = (dict(zip(far_first(sz.head_axis), side)) for side in (own, other))
    for d in range(sz.head_axis):
        cols = aligned((h ^ d) * sz.chunk, sz.chunk)
        dst[aligned(c * HALF, HALF), cols] = own[d]
        dst[aligned((1 - c) * HALF, HALF), cols] = other[d]


def line_of(table, at):
    line = lax.broadcasted_iota(jnp.int32, table.shape, 0)
    return jnp.sum(jnp.where(line == at, table, 0.0), axis=0, keepdims=True)


def conv_forward(sz, ext, taps):
    pre = taps[0:1] * ext[5 : 5 + BLOCK, :]
    for j in range(1, sz.taps):
        pre = pre + taps[j : j + 1] * ext[5 + j : 5 + j + BLOCK, :]
    return pre


def decay_of(sz, cols, rp, h, mask):
    rows = cols[:, h : h + 1] + rp[12 + h : 13 + h, :]
    return jnp.exp(jnp.where(mask, rows, HIDDEN))


def lower_mask():
    t = lax.broadcasted_iota(jnp.int32, (BLOCK, BLOCK), 0)
    s = lax.broadcasted_iota(jnp.int32, (BLOCK, BLOCK), 1)
    return t >= s


def forward_kernel(sz, layer, slots, sc, *refs):
    n = sz.head_axis
    sources = 2 * slots if layer == 0 else 2 * n + 2 * slots
    src, refs = refs[:sources], refs[sources:]
    if layer == 1:
        table, refs = refs[0], refs[1:]
    gains, given, halo, begin = refs[0:2], refs[2:8], refs[8], refs[9]
    refs = refs[10:]
    if layer == 1:
        ov, refs = refs[0], refs[1:]
    normed_o, gl_o, lin_o, ssd_o, inc_o, inv_o, part_o, unit_o, fin_o, sc_o, base_o = refs[:11]
    refs = refs[11:]
    if layer == 1:
        mixed_o, refs = refs[0], refs[1:]
    else:
        tables_o, refs = refs[0:2], refs[2:]
    xs, ms, wv, ext, state, sems = refs
    b = pl.program_id(0)
    c, h, k = sc[0], sc[1], sc[3]
    ch, st = sz.channels, sz.states
    copies = weight_copies(sz, layer, c, h, given, wv, sems)

    @pl.when(b == 0)
    def _():
        run_copies(copies, True, False)
        ext[0:8, :] = halo[...]
        state[...] = begin[...]
        for i in range(4):
            sc_o[i] = sc[i]

    mine = aligned(c * HALF, HALF)
    cols = aligned(h * sz.chunk, sz.chunk)
    if layer == 0:
        put_ordered(sz, xs, c, k, b, src[:slots], src[slots:])
        base_o[...] = xs[mine, cols]
        for r in range(slots):

            @pl.when(lax.rem(k - b + slots, slots) == r)
            def _(r=r):
                own = decay_table(rates_of(src[r]), c, sz.heads)
                other = decay_table(rates_of(src[slots + r]), c, sz.heads)
                tables_o[0][...] = pick(c == 0, own, other)
                tables_o[1][...] = pick(c == 0, other, own)

        rp = tables_o[0][...]
    else:
        put_pieces(sz, xs, c, h, [r[...] for r in src[:n]], [r[...] for r in src[n : 2 * n]])
        put_ordered(sz, ms, c, k, b, src[2 * n : 2 * n + slots], src[2 * n + slots :])
        base_o[...] = ms[mine, cols]
        mixed_o[...] = ms[...]
        rp = table[...]

    pv = pick(c == layer, gains[0][...], gains[1][...])
    x = xs[...].astype(F32)
    inv_in = lax.rsqrt(jnp.mean(x * x, axis=1, keepdims=True) + EPS)
    normed = (x * inv_in * pv[0:1, : sz.width]).astype(LOW)
    normed_o[...] = normed

    @pl.when(b == 0)
    def _():
        run_copies(copies, False, True)

    proj = dot(normed, wv[...], NN)
    gl = proj[:, :ch]
    gl_o[...] = gl
    lin = proj[:, ch:].astype(LOW)
    lin_o[...] = lin
    ext[8 : 8 + BLOCK, :] = lin.astype(F32)
    pre = conv_forward(sz, ext, pv[1:5, : sz.lin])
    ext[0:8, :] = ext[BLOCK : BLOCK + 8, :]
    act = (pre * sigmoid(pre)).astype(LOW)
    values, bm, cm = act[:, :ch], act[:, ch : ch + st], act[:, ch + st :]

    cols = jnp.transpose(rp)
    mask = lower_mask()
    gram = dot(cm, bm, NT)
    mixes, parts = [], []
    for i in range(sz.heads):
        mixes.append((gram * decay_of(sz, cols, rp, i, mask)).astype(LOW))
        parts.append(per_head(values, i, sz.head_width))
    intra = dot(jnp.concatenate(mixes, axis=1), jnp.concatenate(parts, axis=0), NN)

    low_state = state[...].astype(LOW)
    inc_o[0] = low_state
    ecum = spread(cols, sz.heads, sz.heads, sz.head_width)
    inter = dot(cm, low_state, NT) * ecum
    vf = values.astype(F32)
    carried = (vf * spread(cols, 2 * sz.heads, sz.heads, sz.head_width)).astype(LOW)
    local = dot(carried, bm, TN)
    for i in range(sz.heads):
        rows = slice(i * sz.head_width, (i + 1) * sz.head_width)
        total = cols[BLOCK - 1 : BLOCK, sz.heads + i : sz.heads + i + 1]
        state[rows, :] = total * state[rows, :] + local[rows]
    ssd = intra + inter + pv[6:7, :ch] * vf
    ssd_o[...] = ssd
    gated = ssd * (gl * sigmoid(gl))
    weighty = gated * pv[5:6, :ch]
    unit_o[...] = weighty.astype(LOW)

    lane = lax.broadcasted_iota(jnp.int32, (BLOCK, 128), 1)
    square = jnp.sum(gated * gated, axis=1, keepdims=True)
    if layer == 0:
        project = jnp.zeros_like(square)
    else:
        scaled_grad = dot(ms[...], ov[...], NN)
        project = jnp.sum(scaled_grad * weighty, axis=1, keepdims=True)
    stats = jnp.where(lane == 0, square, jnp.where(lane == 1, project, inv_in))
    stats = jnp.transpose(stats)
    part_o[...] = stats[0:2, :]
    inv_o[...] = stats[2:3, :]

    @pl.when(b == sz.blocks - 1)
    def _():
        fin_o[...] = state[...]


def scalar_lines(sz, lines):
    fill = [jnp.zeros((8 - sz.blocks, HALF), F32)] if sz.blocks < 8 else []
    high, low = split_low(jnp.concatenate(lines + fill, axis=0))
    table = jnp.concatenate([high, low], axis=0).astype(LOW)
    return jnp.concatenate([table] * (sz.chunk // HALF), axis=1)


def own_rows(sz, ref, which):
    blocks = [ref[aligned(b * BLOCK + which * HALF, HALF), :] for b in range(sz.blocks)]
    return jnp.concatenate(blocks, axis=0)


def project_kernel(sz, layer, deps, sc, unit_r, stats_r, *refs):
    given, refs = refs[:2], refs[2 + deps :]
    keep, send, sc_o, weights, sems = refs
    c, h = sc[0], sc[1]
    copies = out_copies(sz, layer, c, h, given, weights, sems)
    run_copies(copies, True, False)
    for i in range(4):
        sc_o[i] = sc[i]
    sides = []
    for which, out in ((c, keep), (1 - c, send)):
        sides.append((out, own_rows(sz, unit_r, which)))
        lines = [
            stats_r[0:1, aligned(b * BLOCK + which * HALF, HALF)] for b in range(sz.blocks)
        ]
        table = scalar_lines(sz, lines)
        for d in range(sz.head_axis):
            out[d, sz.rows :, :] = table
    run_copies(copies, False, True)
    for out, rows in sides:
        for d in range(sz.head_axis):
            chunk = weights[:, aligned((h ^ d) * sz.chunk, sz.chunk)]
            out[d, : sz.rows, :] = dot(rows, chunk, NN).astype(LOW)


def turn_kernel(sz, sc, *refs):
    given, given_out, refs = refs[:6], refs[6:8], refs[8:]
    wide_o, out_o, wv, ov, sems = refs[:2], refs[2:4], refs[4], refs[5], refs[6]
    for layer in range(2):
        copies = weight_copies(sz, layer, sc[0], sc[1], given, wv, sems)
        run_copies(copies, True, True)
        copies = out_copies(sz, layer, sc[0], sc[1], given_out, ov, sems)
        run_copies(copies, True, True)
        wide_o[layer][...] = jnp.transpose(wv[...])
        out_o[layer][...] = jnp.transpose(ov[...])


def out_at(out, d):
    return out[d] if isinstance(out, tuple) else out.at[d]


def lift_kernel(sz, layer, deps, sc, cat_r, normed_r, zero_gains, one_gains, small_r, *refs):
    weights, refs = refs[0], refs[1 + deps :]
    keep, send, sc_o, common_o, wide = refs[0], refs[1:-3], *refs[-3:]
    c, h = sc[0], sc[1]
    for i in range(4):
        sc_o[i] = sc[i]
    wide[...] = jnp.zeros_like(wide)
    for which, out in ((c, keep), (1 - c, send)):
        rows = own_rows(sz, cat_r, which)
        along = jnp.zeros((sz.rows, 1), F32)
        for d in range(sz.head_axis):
            cols = aligned((h ^ d) * sz.chunk, sz.chunk)
            product = dot(rows, weights[:, cols], NN)
            out_at(out, d)[: sz.rows, :] = product.astype(LOW)
            blocks = [
                normed_r[aligned(b * BLOCK + which * HALF, HALF), cols] for b in range(sz.blocks)
            ]
            product = product * jnp.concatenate(blocks, axis=0).astype(F32)
            wide[0:1, cols] += jnp.sum(product, axis=0, keepdims=True)
            along = along + jnp.sum(product, axis=1, keepdims=True)
        lines = [
            jnp.transpose(jnp.broadcast_to(along[b * HALF : (b + 1) * HALF], (HALF, 128)))[0:1, :]
            for b in range(sz.blocks)
        ]
        table = scalar_lines(sz, lines)
        for d in range(sz.head_axis):
            out_at(out, d)[sz.rows :, :] = table
    gain_grad = wide[0:1, :] / pick(c == layer, zero_gains[0:1, :], one_gains[0:1, :])
    flat = [small_r[j : j + 1, sz.channels :] for j in range(sz.taps)]
    flat += [gain_grad[:, q * sz.chunk : (q + 1) * sz.chunk] for q in range(sz.head_axis)]
    high, low = split_low(jnp.concatenate(flat, axis=0))
    common_o[...] = jnp.concatenate([high, low], axis=0).astype(LOW)


def backward_kernel(sz, layer, deps, sc, *refs):
    n = sz.head_axis
    sources = 2 * n + 2 if layer == 0 else 1 + n
    src, refs = refs[:sources], refs[sources:]
    gl_r, lin_r, ssd_r, inc_r = refs[:4]
    table, gains, ov = refs[4], refs[5:7], refs[7]
    halo, halo_grad, begin = refs[8:11]
    refs = refs[11 + deps :]
    cat_o, scaled_o, small_o, sums_o, fin_o, rim_o, sc_o = refs[:7]
    refs = refs[7:]
    if layer == 0:
        mixed_o, refs = refs[0], refs[1:]
    ms, ext, back, state, heads_p, small = refs
    i_step = pl.program_id(0)
    b = sz.blocks - 1 - i_step
    c, h = sc[0], sc[1]
    ch, st = sz.channels, sz.states
    pv = pick(c == layer, gains[0][...], gains[1][...])
    rp = table[...]

    @pl.when(i_step == 0)
    def _():
        back[BLOCK : BLOCK + 8, :] = halo_grad[...]
        state[...] = begin[...]
        small[...] = jnp.zeros_like(small)
        for i in range(4):
            sc_o[i] = sc[i]
        if layer == 0:
            for i in range(2):
                extra = src[i * n][sz.rows :, :].astype(F32)
                for d in range(1, n):
                    extra = extra + src[i * n + d][sz.rows :, :].astype(F32)
                heads_p[8 * i : 8 * i + 8, :] = extra[0:8, :HALF] + extra[8:16, :HALF]

    if layer == 0:
        rows = aligned(b * HALF, HALF)
        put_pieces(
            sz, ms, c, h, [r[rows, :] for r in src[:n]], [r[rows, :] for r in src[n : 2 * n]]
        )
        halves = []
        for k in range(2):
            alpha = lax.rsqrt(line_of(src[2 * n + k][...], b) / sz.inner + EPS)
            beta = alpha * alpha * line_of(heads_p[...], 8 * k + b) / sz.inner
            halves.append((alpha, beta))
        alpha, beta = (
            pick(
                c == 0,
                jnp.concatenate([halves[0][q], halves[1][q]], axis=1),
                jnp.concatenate([halves[1][q], halves[0][q]], axis=1),
            )
            for q in range(2)
        )
    else:
        stats = src[1][...]
        for d in range(1, n):
            stats = stats + src[1 + d][...]
        alpha = lax.rsqrt(stats[0:1, :] / sz.inner + EPS)
        beta = alpha * alpha * alpha * stats[1:2, :] / sz.inner

    sub = lax.broadcasted_iota(jnp.int32, rp.shape, 0)
    cols = jnp.transpose(jnp.where(sub == 12, alpha, jnp.where(sub == 13, beta, rp)))
    alpha, beta = cols[:, 12:13], cols[:, 13:14]

    gl = gl_r[...]
    ssd = ssd_r[...]
    sig = sigmoid(gl)
    swish = gl * sig
    slope = sig * (1.0 + gl * (1.0 - sig))
    gated = ssd * swish
    if layer == 0:
        mixed_grad = ms[...]
        mixed_o[...] = mixed_grad
    else:
        mixed_grad = src[0][...]
    scaled_grad = dot(mixed_grad, ov[...], NN)
    gain = pv[5:6, :ch]
    normal = gated * alpha
    small[4:5, :ch] += jnp.sum(scaled_grad * normal, axis=0, keepdims=True)
    scaled_o[...] = (normal * gain).astype(LOW)
    gated_grad = alpha * (scaled_grad * gain) - beta * gated
    ssd_grad = (gated_grad * swish).astype(LOW)
    gate_grad = (gated_grad * ssd * slope).astype(LOW)
    sgf = ssd_grad.astype(F32)

    before = lin_r[pl.ds(pl.multiple_of(jnp.maximum(b * BLOCK - 16, 0), 16), 16), :]
    ext[0:8, :] = pick(b > 0, before.astype(F32)[8:16, :], halo[...])
    ext[8 : 8 + BLOCK, :] = lin_r[aligned(b * BLOCK, BLOCK), :].astype(F32)
    taps = pv[1:5, : sz.lin]
    pre = conv_forward(sz, ext, taps)
    psig = sigmoid(pre)
    pact = pre * psig
    pslope = psig * (1.0 + pre * (1.0 - psig))
    act = pact.astype(LOW)
    values, bm, cm = act[:, :ch], act[:, ch : ch + st], act[:, ch + st :]
    vf = values.astype(F32)
    small[5:6, :ch] += jnp.sum(sgf * vf, axis=0, keepdims=True)

    mask = lower_mask()
    gram = dot(cm, bm, NT)
    gram_grad = jnp.zeros((BLOCK, BLOCK), F32)
    mixes, parts = [], []
    for i in range(sz.heads):
        decay = decay_of(sz, cols, rp, i, mask)
        mixes.append((gram * decay).astype(LOW))
        parts.append(per_head(ssd_grad, i, sz.head_width))
        gram_grad = gram_grad + dot(parts[-1], values, NT) * decay
    intra_grad = dot(jnp.concatenate(mixes, axis=0), jnp.concatenate(parts, axis=0), TN)

    ecum = spread(cols, sz.heads, sz.heads, sz.head_width)
    to_end = spread(cols, 2 * sz.heads, sz.heads, sz.head_width)
    inter_grad = (sgf * ecum).astype(LOW)
    low_state = state[...].astype(LOW)
    carried = (vf * to_end).astype(LOW)
    carried_grad = dot(bm, low_state, NT)
    gram_low = gram_grad.astype(LOW)
    b_grad = dot(gram_low, cm, TN) + dot(carried, low_state, NN)
    c_grad = dot(gram_low, bm, NN) + dot(inter_grad, inc_r[0], NN)
    value_grad = intra_grad + pv[6:7, :ch] * sgf + carried_grad * to_end
    entry = dot(inter_grad, cm, TN)
    for i in range(sz.heads):
        rows = slice(i * sz.head_width, (i + 1) * sz.head_width)
        total = cols[BLOCK - 1 : BLOCK, sz.heads + i : sz.heads + i + 1]
        state[rows, :] = total * state[rows, :] + entry[rows]

    pre_grad = jnp.concatenate([value_grad, b_grad, c_grad], axis=1) * pslope
    back[0:BLOCK, :] = pre_grad
    lin_grad = taps[0:1] * back[sz.taps - 1 : sz.taps - 1 + BLOCK, :]
    for j in range(1, sz.taps):
        at = sz.taps - 1 - j
        lin_grad = lin_grad + taps[j : j + 1] * back[at : at + BLOCK, :]
    for j in range(sz.taps):
        small[j : j + 1, :] += jnp.sum(pre_grad * ext[5 + j : 5 + j + BLOCK, :], axis=0, keepdims=True)
    back[BLOCK : BLOCK + 8, :] = back[0:8, :]
    cat_o[...] = jnp.concatenate([gate_grad, lin_grad.astype(LOW)], axis=1)

    @pl.when(i_step == sz.blocks - 1)
    def _():
        fin_o[...] = state[...]
        rim_o[...] = back[0:8, :]
        sums = small[...]
        flat = [sums[j : j + 1, :ch] for j in range(sz.taps + 2)]
        flat = [jnp.concatenate(flat[j : j + 3], axis=1) for j in range(0, len(flat), 3)]
        flat = flat + [jnp.zeros_like(flat[0])] * (4 - len(flat))
        high, low = split_low(jnp.concatenate(flat, axis=0))
        rest = jnp.zeros((PAD - 8, high.shape[1]), F32)
        small_o[...] = jnp.concatenate([high, low, rest], axis=0).astype(LOW)
        sums_o[...] = sums


def weights_kernel(sz, seq, deps, with_common, sc, normed, cat, mixed, scaled, small, *refs):
    if with_common:
        common, refs = refs[0], refs[1:]
    refs = refs[deps:]
    sc_o, outs, heads, full, wide = refs[0], refs[1 : seq + 1], refs[seq + 1 : -2], refs[-2], refs[-1]
    for i in range(4):
        sc_o[i] = sc[i]
    ch, st = sz.channels, sz.states
    step = sz.chunk
    for q in range(sz.head_axis):
        at = slice(q * step, (q + 1) * step)
        grads = dot(normed[:, at], cat[...], TN)
        full[at, : 2 * ch] = grads[:, : 2 * ch].astype(LOW)
        wide[at, :] = grads[:, 2 * ch :]
        full[at, 2 * ch :] = dot(mixed[:, at], scaled[...], TN).astype(LOW)
    rows = sz.width // seq
    part = rows // sz.head_axis
    for r, out in enumerate(outs):
        out[:rows, :] = full[aligned(lax.rem(sc[2] + r, seq) * rows, rows), :]
        out[rows:, :] = small[...]
    for d, out in enumerate(heads):
        lines = [
            wide[aligned(lax.rem(sc[2] + r, seq) * rows + (sc[1] ^ d) * part, part), :]
            for r in range(seq)
        ]
        if with_common:
            lines = [common[...].astype(F32)] + lines
        out[...] = jnp.concatenate(lines, axis=0).astype(LOW)


def resplit(extra):
    half = extra.shape[0] // 2
    high, low = split_low(extra[:half, :] + extra[half:, :])
    return jnp.concatenate([high, low], axis=0)


def join_kernel(sz, parts, riders, deps, sc, keep, *refs):
    n = sz.head_axis
    recv, refs = refs[0] if parts == 1 else refs[:parts], refs[parts:]
    more = [(refs[i * (n + 1)], refs[i * (n + 1) + 1 : (i + 1) * (n + 1)]) for i in range(riders)]
    refs = refs[riders * (n + 1) + deps :]
    sc_o, outs = refs[0], refs[1:]
    rows = sz.rows
    for i in range(4):
        sc_o[i] = sc[i]
    extra = resplit(keep[0, rows:, :].astype(F32) + out_at(recv, 0)[rows:, :].astype(F32))
    for d, out in enumerate(outs):
        both = keep[d, :rows, :].astype(F32) + out_at(recv, d)[:rows, :].astype(F32)
        out[:rows, :] = both.astype(out.dtype)
        out[rows : rows + PAD, :] = extra.astype(out.dtype)
        at = rows + PAD
        for common, rider in more:
            size = rider[d].shape[0]
            out[at : at + PAD, :] = common[...].astype(out.dtype)
            out[at + PAD : at + PAD + size, :] = rider[d][...].astype(out.dtype)
            at += PAD + size


def total_of(parts, rows):
    total = parts[0][rows, :].astype(F32)
    for p in parts[1:]:
        total = total + p[rows, :].astype(F32)
    return total


def output_kernel(sz, layer, sc, *refs):
    n = sz.head_axis
    parts, refs = refs[:n], refs[n:]
    resid = refs[0]
    res_o, low_o, mixed_o, square_o, sc_o = refs[-5:]
    for i in range(4):
        sc_o[i] = sc[i]
    extra = total_of(parts, slice(sz.rows, sz.rows + PAD))
    square = extra[0:8, :HALF] + extra[8:16, :HALF]
    square_o[...] = square
    inv = lax.rsqrt(square / sz.inner + EPS)
    for b in range(sz.blocks):
        rows = slice(b * HALF, (b + 1) * HALF)
        col = column_of(inv[b : b + 1, :], HALF)[:, 0:1]
        mixed = total_of(parts, rows) * col
        res = resid[rows, :].astype(F32) + mixed
        res_o[rows, :] = res
        low_o[rows, :] = res.astype(LOW)
        mixed_o[rows, :] = mixed


def input_kernel(sz, layer, sc, *refs):
    n = sz.head_axis
    parts, refs = refs[:n], refs[n:]
    resid, outg, inv_r, gains = refs[0], refs[1], refs[2], refs[3:5]
    refs = refs[5:]
    if layer == 1:
        mixed = refs[0]
        grad_o, low_o, sc_o = refs[-3:]
    else:
        one_low, one_heads = refs[0], refs[1 : 1 + n]
        low_o, swap_o, shared_o, sc_o = refs[-4:]
    for i in range(4):
        sc_o[i] = sc[i]
    c, h = sc[0], sc[1]
    first = c == 0
    mine = aligned(h * sz.chunk, sz.chunk)
    gain = pick(c == layer, gains[0][0:1, mine], gains[1][0:1, mine])
    extra = total_of(parts, slice(sz.rows, sz.rows + PAD))
    along = extra[0:8, :HALF] + extra[8:16, :HALF]
    tops, lows = [], []
    for b in range(sz.blocks):
        rows = slice(b * HALF, (b + 1) * HALF)
        at = b * BLOCK
        inv_row = pick(c == 0, inv_r[:, at : at + HALF], inv_r[:, at + HALF : at + BLOCK])
        inv = column_of(inv_row, HALF)[:, 0:1]
        share = column_of(along[b : b + 1, :] / sz.width, HALF)[:, 0:1]
        total = total_of(parts, rows)
        base = resid[rows, :].astype(F32)
        grad = outg[rows, :].astype(F32) + inv * (total * gain - base * (inv * share))
        low = grad.astype(LOW)
        low_o[rows, :] = low
        if layer == 0:
            swap_o[rows, :] = pick(first, one_low[rows, :], low)
        else:
            grad_o[rows, :] = grad
            dots = jnp.sum(low.astype(F32) * mixed[rows, :], axis=1, keepdims=True)
            row = jnp.transpose(jnp.broadcast_to(dots, (HALF, 128)))[0:1, :]
            high, rest = split_low(row)
            tops.append(high)
            lows.append(rest)
    if layer == 1:
        fill = [jnp.zeros((8 - sz.blocks, HALF), F32)] if sz.blocks < 8 else []
        extra = jnp.concatenate(tops + fill + lows + fill, axis=0)
        extra = jnp.concatenate([extra] * (sz.chunk // HALF), axis=1)
        low_o[sz.rows :, :] = extra.astype(LOW)
    else:
        size = shared_o.shape[0]
        at = sz.rows + PAD
        zero = total_of(parts, slice(at, at + size))
        one = total_of(one_heads, slice(None))
        zero, one = (jnp.concatenate([resplit(v[:PAD]), v[PAD:]], axis=0) for v in (zero, one))
        shared_o[...] = pick(first, zero, one)
        swap_o[sz.rows :, :] = pick(first, one, zero).astype(LOW)


def sum_kernel(sz, last, sc, *refs):
    if last:
        parts, done, outs = refs[:-3], refs[-3], refs[-2:]
    else:
        parts, outs = refs[:-1], refs[-1:]
    rows = outs[0].shape[0] - PAD
    total = total_of(parts, slice(None))
    extra = total[rows:]
    high, low = split_low(extra[0:4, :] + extra[4:8, :])
    extra = jnp.concatenate([high, low, jnp.zeros((PAD - 8, extra.shape[1]), F32)], axis=0)
    sums = jnp.concatenate([total[:rows], extra], axis=0).astype(LOW)
    if last:
        outs[0][...] = pick(sc[0] == 0, sums, done[...])
        outs[1][...] = pick(sc[0] == 0, done[...], sums)
    else:
        outs[0][...] = sums


def final_kernel(sz, sc, own, got, *refs):
    gate_o, inner_o, out_o, conv_o, norm_o, skip_o = refs
    c = sc[0]
    ch = sz.channels
    rows = own.shape[0] - PAD
    lane = lax.broadcasted_iota(jnp.int32, skip_o.shape, 1)
    skip = jnp.zeros(skip_o.shape, F32)
    for i in range(2):
        which = pick(i == 0, c, 1 - c)
        to = aligned(which * ch, ch)
        sums = (own if i == 0 else got)[...].astype(F32)
        gate_o[:, to] = sums[:rows, :ch]
        inner_o[:, to] = sums[:rows, ch : 2 * ch]
        out_o[to, :] = jnp.transpose(sums[:rows, 2 * ch :])
        lines = sums[rows : rows + 4, :] + sums[rows + 4 : rows + 8, :]
        for j in range(sz.taps):
            conv_o[j : j + 1, to] = lines[j // 3 : j // 3 + 1, (j % 3) * ch : (j % 3 + 1) * ch]
        norm_o[:, to] = lines[1:2, ch : 2 * ch]
        skips = lines[1:2, 2 * ch :]
        for q in range(sz.heads):
            part = jnp.sum(per_head(skips, q, sz.head_width), axis=1, keepdims=True)
            skip = jnp.where(lane == which * sz.heads + q, part, skip)
    skip_o[...] = skip
def shared_kernel(sz, seq, sc, *refs):
    pieces, shared_o, taps_o, gain_o = refs[:-3], *refs[-3:]
    total = total_of(pieces, slice(BLOCK, None))
    shared_o[...] = total[PAD:]
    common = total[: PAD // 2] + total[PAD // 2 : PAD]
    place = sc[2] * sz.head_axis + sc[1]
    span = common.shape[1]
    size = span // (seq * sz.head_axis)
    turned = pltpu.roll(common, lax.rem(span - place * size, span), 1)
    taps_o[...] = turned[: sz.taps, :size]
    size = sz.width // (seq * sz.head_axis)
    at = place * size
    line = jnp.broadcast_to(line_of(common, sz.taps + at // span), common.shape)
    turned = pltpu.roll(line, lax.rem(span - lax.rem(at, span), span), 1)
    gain_o[...] = turned[:1, :size]


def slice_kernel(sz, slots, sc, order, tokens, rates, *refs):
    outs, sc_o, sems = refs[:slots], refs[slots], refs[slots + 1]
    copies = []
    for r in range(slots):
        rows = tokens.at[order[lax.rem(sc[3] + r, slots)], aligned(sc[0] * HALF, HALF), :]
        copies.append(pltpu.make_async_copy(rows, outs[r].at[:HALF], sems.at[r]))
    for copy in copies:
        copy.start()
    for i in range(4):
        sc_o[i] = sc[i]
    for r in range(slots):
        first, rest = split_low(rates[0, order[lax.rem(sc[3] + r, slots)]])
        second, rest = split_low(rest)
        lines = jnp.concatenate([first, second, rest, jnp.zeros_like(rest)], axis=1)
        lines = jnp.concatenate([lines, jnp.zeros_like(lines)], axis=0)
        outs[r][HALF:, :] = lines.astype(LOW)
    for copy in copies:
        copy.wait()


def rates_of(piece):
    lines = piece[HALF:, :].astype(F32)[:8, :]
    return (lines[:, :BLOCK] + lines[:, BLOCK : 2 * BLOCK]) + lines[:, 2 * BLOCK : 3 * BLOCK]


def pack_kernel(sz, sc, order, grads, gate, inner, out, in_gain, conv_i, conv_s, skip, norm, *refs):
    gate_o, inner_o, o_o, mine_o, send_o, sems = *refs[:5], refs[-1]
    c, h = sc[0], sc[1]
    ch = sz.channels
    outs = refs[5:-1]
    slices = []
    for r, to in enumerate(outs):
        rows = grads.at[order[lax.rem(sc[3] + r, len(outs))], aligned(c * HALF, HALF), :]
        slices.append(pltpu.make_async_copy(rows, to, sems.at[3 + r]))
    cols = aligned((1 - c) * ch, ch)
    rows = aligned((h * 2 + 1 - c) * ch, ch)
    copies = [
        pltpu.make_async_copy(gate.at[0, :, cols], gate_o, sems.at[0]),
        pltpu.make_async_copy(inner.at[0, :, cols], inner_o, sems.at[1]),
        pltpu.make_async_copy(out.at[0, rows, :], o_o, sems.at[2]),
        *slices,
    ]
    for copy in copies:
        copy.start()
    for which, ref in ((c, mine_o), (1 - c, send_o)):
        at = aligned(which * ch, ch)
        ref[...] = jnp.zeros_like(ref)
        ref[0:1, :] = in_gain[...]
        ref[1 : 1 + sz.taps, :ch] = conv_i[0, :, at]
        ref[1 : 1 + sz.taps, ch : sz.lin] = conv_s[0]
        ref[5:6, :ch] = norm[:, at]
        low = spread(skip[...], 0, sz.heads, sz.head_width)
        high = spread(skip[...], sz.heads, sz.heads, sz.head_width)
        ref[6:7, :ch] = pick(which == 0, low, high)
    for copy in copies:
        copy.wait()


def decay_table(rate, c, n):
    lane = lax.broadcasted_iota(jnp.int32, rate.shape, 1)
    cum = rate
    step = 1
    while step < BLOCK:
        cum = cum + jnp.where(lane >= step, pltpu.roll(cum, step, 1), 0.0)
        step *= 2
    end = cum[:, BLOCK - 1 :]
    lines = [cum, jnp.exp(cum), jnp.exp(end - cum) * -rate, jnp.log(-rate) - cum]
    low = jnp.concatenate([v[:n] for v in lines], axis=0)
    high = jnp.concatenate([v[n:] for v in lines], axis=0)
    return pick(c == 0, low, high)


def leave_kernel(sz, slots, riders, sc, zero_own, zero_other, one_own, one_other, *refs):
    c = sc[0]
    if riders:
        shared, refs = refs[0], refs[1:]
        total = shared[...] + one_other[sz.rows :, :].astype(F32)
        extra = resplit(total[:PAD])
        part = (total.shape[0] - PAD) // riders
    outs = refs[:slots]
    for i in range(4):
        refs[slots][i] = sc[i]
    for r in range(slots):
        rows = aligned(lax.rem(sc[3] + r, slots) * HALF, HALF)
        own = pick(c == 0, zero_own[rows, :], one_own[rows, :])
        other = pick(c == 0, zero_other[rows, :], one_other[rows, :])
        put_pair(outs[r], c, own, other)
        if riders:
            lines = [extra, total[PAD + r * part : PAD + (r + 1) * part]]
            outs[r][BLOCK:, :] = jnp.concatenate(lines, axis=0).astype(LOW)


def home_kernel(slots, sc, *refs):
    early, late, out, grad = refs[:slots], refs[slots : 2 * slots], refs[-3], refs[-2]
    for i in range(4):
        refs[-1][i] = sc[i]
    first = sc[0] == 0
    for r in range(slots):
        at = lax.rem(sc[3] - r + slots, slots)
        out[at] = pick(first, early[r][...], late[r][:BLOCK, :]).astype(F32)
        grad[at] = pick(first, late[r][:BLOCK, :], early[r][...]).astype(F32)


def whole(shape):
    return pl.BlockSpec(shape, lambda *_: (0,) * len(shape))


def per_device(
    tokens,
    slot_order,
    log_decay,
    grad_out,
    in_gain,
    w_gate,
    w_inner,
    w_shared,
    conv_inner,
    conv_shared,
    d_skip,
    norm_gain,
    w_out,
):
    slots = tokens.shape[0]
    span = tokens.shape[1]
    width = tokens.shape[2]
    seq = lax.axis_size("seq")
    head_axis = lax.axis_size("head")
    cores = lax.axis_size("section")
    spans = seq // slots
    c = lax.axis_index("section")
    z = lax.axis_index("seq")
    h = lax.axis_index("head")
    k = lax.rem(z, slots)
    inner_dev = w_gate.shape[2]
    channels = inner_dev // cores
    shared = w_shared.shape[2]
    heads_dev = d_skip.shape[1]
    taps = conv_inner.shape[1]
    sz = Sizes(
        slots * span // BLOCK,
        width,
        channels,
        heads_dev // cores,
        shared // 2,
        taps,
        head_axis,
        inner_dev * head_axis,
    )
    first = c == 0
    swap = [(0, 1), (1, 0)]
    nb, tok, rows, chunk = sz.blocks, sz.tokens, sz.rows, sz.chunk

    def cross(x):
        return lax.ppermute(x, "section", swap)

    def turn(x, r):
        pairs = [(i, i // slots * slots + (i % slots + r) % slots) for i in range(seq)]
        return lax.ppermute(x, "seq", pairs) if r else x

    def over_heads(x, d):
        return x if d == 0 else lax.ppermute(x, "head", [(i, i ^ d) for i in range(head_axis)])

    def next_span(x, way):
        pairs = [(i, i + way * slots) for i in range(seq) if 0 <= i + way * slots < seq]
        return lax.ppermute(x, "seq", pairs)

    def shape(dims, dtype):
        return jax.ShapeDtypeStruct(dims, dtype)

    prefetch = functools.partial(pltpu.PrefetchScalarGridSpec, num_scalar_prefetch=1)
    options = pltpu.CompilerParams(vmem_limit_bytes=VMEM_BYTES)
    from_hbm = pltpu.CompilerParams(vmem_limit_bytes=ALL_VMEM_BYTES)
    anywhere = pl.BlockSpec(memory_space=pl.ANY)
    smem = pl.BlockSpec(memory_space=pltpu.SMEM)
    vmem = pl.BlockSpec(memory_space=pltpu.VMEM)
    index_shape = shape((4,), jnp.int32)

    def cost(flops, moved):
        return pl.CostEstimate(flops=int(flops), bytes_accessed=int(moved), transcendentals=0)

    def to_members(pieces):
        return [turn(x, r) for r, x in enumerate(pieces)]

    sc = jnp.stack([c, h, z, k]).astype(jnp.int32)
    *tok_slices, sc = pl.pallas_call(
        functools.partial(slice_kernel, sz, slots),
        in_specs=[smem, smem, anywhere, vmem],
        out_specs=[vmem] * slots + [smem],
        out_shape=[shape((HALF + PAD, width), LOW)] * slots + [index_shape],
        scratch_shapes=[pltpu.SemaphoreType.DMA((slots,))],
        compiler_params=from_hbm,
    )(sc, slot_order, tokens, log_decay)
    tok_pieces = to_members(tok_slices)
    tok_others = [cross(x) for x in tok_pieces]

    wide = 2 * channels + shared
    gate_sent, inner_sent, o_sent, pv_mine, pv_sent, *out_slices = pl.pallas_call(
        functools.partial(pack_kernel, sz),
        in_specs=[smem, smem] + [anywhere] * 4 + [vmem] * 5,
        out_specs=[vmem] * (5 + slots),
        out_shape=[
            shape((width, channels), LOW),
            shape((width, channels), LOW),
            shape((channels, width), LOW),
            shape((16, width), F32),
            shape((16, width), F32),
        ]
        + [shape((HALF, width), LOW)] * slots,
        scratch_shapes=[pltpu.SemaphoreType.DMA((3 + slots,))],
        compiler_params=from_hbm,
    )(
        sc, slot_order, grad_out, w_gate, w_inner, w_out,
        in_gain, conv_inner, conv_shared, d_skip, norm_gain,
    )
    sent = [cross(x) for x in (gate_sent, inner_sent, w_shared[0], o_sent)]
    gains = [pv_mine, cross(pv_sent)]

    def span_total(table):
        ends = table[: sz.heads, BLOCK - 1 :: BLOCK]
        return jnp.repeat(jnp.exp(jnp.sum(ends, axis=1)), sz.head_width)[:, None]

    parts_shape = shape((head_axis, rows + PAD, chunk), LOW)
    in_weights = [w_gate, w_inner, w_shared, *sent[:3]]
    last_weights = [w_out, sent[3]]
    wide_weights = pltpu.VMEM((width, wide), LOW)
    out_weights = pltpu.VMEM((channels, width), LOW)
    copy_sems = pltpu.SemaphoreType.DMA((4,))
    dense = 2 * tok * width * (wide + channels)

    def forward(layer, sc, sources):
        def at(b, _):
            return (b, 0)

        piece = pl.BlockSpec((HALF, chunk), at)
        table = pl.BlockSpec((16, BLOCK), lambda b, _: (0, b))
        if layer == 0:
            src_specs = [whole((HALF + PAD, width))] * (2 * slots)
            more_specs = [table, table]
            more_shapes = [shape((16, tok), F32)] * 2
        else:
            src_specs = [piece] * (2 * head_axis) + [whole((HALF, width))] * (2 * slots) + [table]
            more_specs = [pl.BlockSpec((BLOCK, width), at)]
            more_shapes = [shape((tok, width), LOW)]

        last = [] if layer == 0 else [turned[3]]

        def call(halo, begin):
            return pl.pallas_call(
                functools.partial(forward_kernel, sz, layer, slots),
                grid_spec=prefetch(
                    grid=(nb,),
                    in_specs=src_specs
                    + [whole((16, width)), whole((16, width))]
                    + [anywhere] * len(in_weights)
                    + [whole((8, sz.lin)), whole((channels, sz.states))]
                    + [whole(x.shape) for x in last],
                    out_specs=[
                        pl.BlockSpec((BLOCK, width), at),
                        pl.BlockSpec((BLOCK, channels), at),
                        pl.BlockSpec((BLOCK, sz.lin), at),
                        pl.BlockSpec((BLOCK, channels), at),
                        pl.BlockSpec((1, channels, sz.states), lambda b, _: (b, 0, 0)),
                        pl.BlockSpec((1, BLOCK), lambda b, _: (0, b)),
                        pl.BlockSpec((2, BLOCK), lambda b, _: (0, b)),
                        pl.BlockSpec((BLOCK, channels), at),
                        whole((channels, sz.states)),
                        smem,
                        piece,
                    ]
                    + more_specs,
                    scratch_shapes=[
                        pltpu.VMEM((BLOCK, width), LOW),
                        pltpu.VMEM((BLOCK, width), LOW),
                        wide_weights,
                        pltpu.VMEM((BLOCK + 8, sz.lin), F32),
                        pltpu.VMEM((channels, sz.states), F32),
                        copy_sems,
                    ],
                ),
                out_shape=[
                    shape((tok, width), LOW),
                    shape((tok, channels), F32),
                    shape((tok, sz.lin), LOW),
                    shape((tok, channels), F32),
                    shape((nb, channels, sz.states), LOW),
                    shape((1, tok), F32),
                    shape((2, tok), F32),
                    shape((tok, channels), LOW),
                    shape((channels, sz.states), F32),
                    index_shape,
                    shape((rows, chunk), LOW),
                ]
                + more_shapes,
                compiler_params=options,
                cost_estimate=cost(6 * dense, 16e6),
            )(sc, *sources, *gains, *in_weights, halo, begin, *last)

        halo = jnp.zeros((8, sz.lin), F32)
        begin = jnp.zeros((channels, sz.states), F32)
        if spans == 1:
            return call(halo, begin), halo
        trial = call(halo, begin)
        halo = next_span(trial[2][tok - 8 :].astype(F32), 1)
        local = call(halo, begin)[8]
        total = span_total(trial[11] if layer == 0 else sources[-1])
        for _ in range(spans - 1):
            begin = next_span(total * begin + local, 1)
        return call(halo, begin), halo

    def backward(layer, sc, sources, saved, decays, halo, deps):
        def at(i, _):
            return (nb - 1 - i, 0)

        if layer == 0:
            src_specs = [whole(s.shape) for s in sources]
        else:
            stat = pl.BlockSpec((2, BLOCK), lambda i, _: (0, nb - 1 - i))
            src_specs = [pl.BlockSpec((BLOCK, width), at)] + [stat] * head_axis
        gl, lin, ssd, inc = saved
        mixed_spec = [pl.BlockSpec((BLOCK, width), at)] if layer == 0 else []
        mixed_shape = [shape((tok, width), LOW)] if layer == 0 else []

        def call(halo_grad, begin):
            return pl.pallas_call(
                functools.partial(backward_kernel, sz, layer, len(deps)),
                grid_spec=prefetch(
                    grid=(nb,),
                    in_specs=src_specs
                    + [
                        pl.BlockSpec((BLOCK, channels), at),
                        whole(lin.shape),
                        pl.BlockSpec((BLOCK, channels), at),
                        pl.BlockSpec((1, channels, sz.states), lambda i, _: (nb - 1 - i, 0, 0)),
                        pl.BlockSpec((16, BLOCK), lambda i, _: (0, nb - 1 - i)),
                        whole((16, width)),
                        whole((16, width)),
                        whole((width, channels)),
                        whole((8, sz.lin)),
                        whole((8, sz.lin)),
                        whole((channels, sz.states)),
                    ]
                    + [anywhere] * len(deps),
                    out_specs=[
                        pl.BlockSpec((BLOCK, wide), at),
                        pl.BlockSpec((BLOCK, channels), at),
                        whole((PAD, 3 * channels)),
                        whole((8, sz.lin)),
                        whole((channels, sz.states)),
                        whole((8, sz.lin)),
                        smem,
                    ]
                    + mixed_spec,
                    scratch_shapes=[
                        pltpu.VMEM((BLOCK, width), LOW),
                        pltpu.VMEM((BLOCK + 8, sz.lin), F32),
                        pltpu.VMEM((BLOCK + 8, sz.lin), F32),
                        pltpu.VMEM((channels, sz.states), F32),
                        pltpu.VMEM((PAD, HALF), F32),
                        pltpu.VMEM((8, sz.lin), F32),
                    ],
                ),
                out_shape=[
                    shape((tok, wide), LOW),
                    shape((tok, channels), LOW),
                    shape((PAD, 3 * channels), LOW),
                    shape((8, sz.lin), F32),
                    shape((channels, sz.states), F32),
                    shape((8, sz.lin), F32),
                    index_shape,
                ]
                + mixed_shape,
                compiler_params=options,
                cost_estimate=cost(8 * dense, 16e6),
            )(
                sc, *sources, gl, lin, ssd, inc, decays, *gains, turned[2 + layer],
                halo, halo_grad, begin, *deps,
            )

        halo_grad = jnp.zeros((8, sz.lin), F32)
        begin = jnp.zeros((channels, sz.states), F32)
        if spans == 1:
            return call(halo_grad, begin)
        local = call(halo_grad, begin)[4]
        for _ in range(spans - 1):
            begin = next_span(span_total(decays) * begin + local, -1)
        halo_grad = next_span(call(halo_grad, begin)[5], -1)
        return call(halo_grad, begin)

    def project(layer, sc, unit, stats, deps):
        return pl.pallas_call(
            functools.partial(project_kernel, sz, layer, len(deps)),
            in_specs=[smem, vmem, vmem] + [anywhere] * (2 + len(deps)),
            out_specs=[vmem, vmem, smem],
            out_shape=[parts_shape, parts_shape, index_shape],
            scratch_shapes=[out_weights, copy_sems],
            compiler_params=options,
            cost_estimate=cost(dense / 4, 4e6),
        )(sc, unit, stats, *last_weights, *deps)

    def lift(layer, sc, cat, normed, small, deps):
        outs = pl.pallas_call(
            functools.partial(lift_kernel, sz, layer, len(deps)),
            in_specs=[smem] + [vmem] * 6 + [anywhere] * len(deps),
            out_specs=[vmem] * (1 + head_axis) + [smem, vmem],
            out_shape=[parts_shape]
            + [shape(parts_shape.shape[1:], LOW)] * head_axis
            + [index_shape, shape((PAD, chunk), LOW)],
            scratch_shapes=[pltpu.VMEM((8, width), F32)],
            compiler_params=options,
            cost_estimate=cost(dense, 8e6),
        )(sc, cat, normed, *gains, small, turned[layer], *deps)
        return outs[0], list(outs[1:-2]), outs[-2], outs[-1]

    def scatter(sc, keep, send, riders=(), deps=()):
        size = rows + PAD + sum(PAD + rider[1].shape[0] for rider in riders)
        flat = [x for rider in riders for x in rider]
        got = [cross(x) for x in (send if isinstance(send, list) else [send])]
        joined = pl.pallas_call(
            functools.partial(join_kernel, sz, len(got), len(riders), len(deps)),
            in_specs=[smem] + [vmem] * (1 + len(got) + len(flat)) + [anywhere] * len(deps),
            out_specs=[smem] + [vmem] * head_axis,
            out_shape=[index_shape, shape((size, chunk), F32)]
            + [shape((size, chunk), LOW)] * (head_axis - 1),
            compiler_params=options,
        )(sc, keep, *got, *flat, *deps)
        return [over_heads(joined[1 + d], d) for d in far_first(head_axis)], joined[0]

    def gather(low):
        own = [over_heads(low, d) for d in far_first(head_axis)]
        return own + [cross(x) for x in own]

    turned = pl.pallas_call(
        functools.partial(turn_kernel, sz),
        in_specs=[smem] + [anywhere] * 8,
        out_specs=[vmem] * 4,
        out_shape=[shape((wide, width), LOW)] * 2 + [shape((width, channels), LOW)] * 2,
        scratch_shapes=[wide_weights, out_weights, copy_sems],
        compiler_params=options,
        cost_estimate=cost(1e9, 8e6),
    )

    def section_output(layer, sc, parts, resid, deps=()):
        return pl.pallas_call(
            functools.partial(output_kernel, sz, layer),
            in_specs=[smem] + [vmem] * (head_axis + 1) + [anywhere] * len(deps),
            out_specs=[vmem] * 4 + [smem],
            out_shape=[
                shape((rows, chunk), F32),
                shape((rows, chunk), LOW),
                shape((rows, chunk), F32),
                shape((8, HALF), F32),
                index_shape,
            ],
            compiler_params=options,
        )(sc, *parts, resid, *deps)

    part = width // seq
    columns = 3 * channels
    share = part // head_axis
    shared_size = seq * share + PAD

    def section_input(layer, sc, parts, *others, deps=()):
        if layer == 0:
            outs = [
                shape((rows + PAD, chunk), LOW),
                shape((rows + shared_size, chunk), LOW),
                shape((shared_size, chunk), F32),
            ]
        else:
            outs = [shape((rows, chunk), F32), shape((rows + PAD, chunk), LOW)]
        return pl.pallas_call(
            functools.partial(input_kernel, sz, layer),
            in_specs=[smem] + [vmem] * (head_axis + len(others)) + [anywhere] * len(deps),
            out_specs=[vmem] * len(outs) + [smem],
            out_shape=outs + [index_shape],
            compiler_params=options,
        )(sc, *parts, *others, *deps)

    def weight_grads(sc, normed, cat, mixed, scaled, small, deps=(), common=None):
        more = [] if common is None else [common]
        size = seq * share + PAD * len(more)
        outs = pl.pallas_call(
            functools.partial(weights_kernel, sz, seq, len(deps), bool(more)),
            in_specs=[smem] + [vmem] * (5 + len(more)) + [anywhere] * len(deps),
            out_specs=[smem] + [vmem] * (seq + head_axis),
            out_shape=[index_shape]
            + [shape((part + PAD, columns), LOW)] * seq
            + [shape((size, shared), LOW)] * head_axis,
            scratch_shapes=[pltpu.VMEM((width, columns), LOW), pltpu.VMEM((width, shared), F32)],
            compiler_params=options,
            cost_estimate=cost(4 * dense, 12e6),
        )(sc, normed, cat, mixed, scaled, small, *more, *deps)
        return over_seq(outs[1 : 1 + seq]), outs[1 + seq :], outs[0]

    def shifted(x, r):
        return lax.ppermute(x, "seq", [(i, (i + r) % seq) for i in range(seq)]) if r else x

    def over_seq(chunks):
        return [shifted(x, r) for r, x in enumerate(chunks)]

    def leave(sc, *arrays, riders=0):
        size = BLOCK + (share + PAD if riders else 0)
        pieces = pl.pallas_call(
            functools.partial(leave_kernel, sz, slots, riders),
            in_specs=[smem] + [vmem] * len(arrays),
            out_specs=[vmem] * slots + [smem],
            out_shape=[shape((size, chunk), LOW)] * slots + [index_shape],
            compiler_params=options,
        )(sc, *arrays)
        return to_members(pieces[:slots]), pieces[slots]

    out_pieces = to_members(out_slices)
    fw0, halo0 = forward(0, sc, tok_pieces + tok_others)
    base0, decays = fw0[10], fw0[11:13]
    pr0 = project(0, fw0[9], fw0[7], fw0[6], [out_pieces[1], out_pieces[-1]])
    out_others = [cross(x) for x in out_pieces]
    parts, sc_join = scatter(sc, pr0[0], pr0[1])
    turned = turned(sc_join, *in_weights, *last_weights)
    res1, low1, mixed0, square0, unused = section_output(0, sc, parts, base0, turned)
    pieces1 = gather(low1)
    square_other = cross(square0)

    fw1, halo1 = forward(1, sc, pieces1 + out_pieces + out_others + [decays[1]])
    stat = fw1[6] + cross(fw1[6])
    stats = [stat] + [over_heads(stat, d) for d in range(1, head_axis)]
    pr1 = project(1, fw1[9], fw1[7], fw1[6], [])
    parts_out, sc_out = scatter(sc, pr1[0], pr1[1])
    bw1 = backward(1, sc_out, [fw1[11]] + stats, fw1[1:5], decays[1], halo1, [])
    lf1 = lift(1, bw1[6], bw1[0], fw1[0], bw1[3], parts_out[1:])
    weights1, heads1, sc_weights = weight_grads(
        lf1[2], fw1[0], bw1[0], fw1[11], bw1[1], bw1[2], common=lf1[3]
    )
    parts, sc_join = scatter(sc_weights, lf1[0], lf1[1])
    igrad1, glow1, sc_in = section_input(
        1, sc_join, parts, res1, fw1[10], fw1[5], *gains, mixed0,
        deps=weights1[2:-1],
    )
    piecesg = gather(glow1)

    heads1 = [over_heads(heads1[d], d) for d in far_first(head_axis)]

    early, unused = leave(sc_in, low1, pieces1[head_axis], glow1, piecesg[head_axis])
    bw0 = backward(
        0, sc, piecesg + [square0, square_other], fw0[1:5], decays[0], halo0,
        weights1[1:2],
    )
    weights0, heads0, sc_weights = weight_grads(
        bw0[6], fw0[0], bw0[0], bw0[7], bw0[1], bw0[2], deps=early[1:] + weights1[-1:],
    )
    lf0 = lift(0, sc_weights, bw0[0], fw0[0], bw0[3], heads1[1:])
    parts, sc_join = scatter(lf0[2], lf0[0], lf0[1], [[lf0[3], *heads0]], weights0[1:2])

    unused, low2, unused_mixed, unused_square, sc_out = section_output(1, sc_in, parts_out, res1)
    glow0, to_other, shared_own, sc_end = section_input(
        0, sc_out, parts, base0, igrad1, fw0[5], *gains, low2, *heads1,
        deps=weights0[2:],
    )
    got = cross(to_other)
    if spans == 1:
        late, sc_end = leave(sc_end, glow0, got, low2, got, shared_own, riders=seq)
        shared_parts = late
    else:
        late, sc_end = leave(sc_end, glow0, got, low2, got)
        total = shared_own + got[rows:].astype(F32)
        extra = resplit(total[:PAD])
        fill = jnp.zeros((BLOCK, shared), F32)
        chunks = [
            jnp.concatenate([fill, extra, total[PAD + r * share : PAD + (r + 1) * share]])
            for r in range(seq)
        ]
        shared_parts = over_seq([x.astype(LOW) for x in chunks])
    def summed(sc, pieces, *done):
        return pl.pallas_call(
            functools.partial(sum_kernel, sz, bool(done)),
            in_specs=[smem] + [vmem] * (len(pieces) + len(done)),
            out_shape=[shape((part + PAD, columns), LOW)] * (1 + len(done)),
            compiler_params=options,
        )(sc, *pieces, *done)

    own_sums, other_sums = summed(sc_end, weights0, *summed(sc_in, weights1))
    final = pl.pallas_call(
        functools.partial(final_kernel, sz),
        in_specs=[smem] + [vmem] * 2,
        out_shape=[
            shape((part, inner_dev), F32),
            shape((part, inner_dev), F32),
            shape((inner_dev, part), F32),
            shape((taps, inner_dev), F32),
            shape((1, inner_dev), F32),
            shape((1, heads_dev), F32),
        ],
        compiler_params=options,
    )(sc, own_sums, cross(other_sums))
    section_out, input_grad, unused = pl.pallas_call(
        functools.partial(home_kernel, slots),
        in_specs=[smem] + [vmem] * (2 * slots) + [anywhere],
        out_specs=[vmem, vmem, smem],
        out_shape=[shape((slots, BLOCK, chunk), F32)] * 2 + [index_shape],
        compiler_params=options,
    )(sc, *early, *late, final[4])

    shared_sum, tap_grads, gain_grads = pl.pallas_call(
        functools.partial(shared_kernel, sz, seq),
        in_specs=[smem] + [vmem] * seq,
        out_shape=[
            shape((share, shared), F32),
            shape((taps, shared // (seq * head_axis)), F32),
            shape((1, width // (seq * head_axis)), F32),
        ],
        compiler_params=options,
    )(sc, *shared_parts)
    return (
        section_out[None],
        input_grad[None],
        gain_grads,
        final[0][None],
        final[1][None],
        shared_sum[None],
        final[3][None],
        tap_grads[None],
        final[5],
        final[4],
        final[2][None],
    )


def solution(mesh):
    placed = (
        P(None, "seq", None),
        P(),
        P("section", None, "head", "seq"),
        P(None, "seq", None),
        P("section", None),
        P("section", None, "head"),
        P("section", None, "head"),
        P("section", None, None),
        P("section", None, "head"),
        P("section", None, None),
        P("section", "head"),
        P("section", "head"),
        P("section", None, None),
    )
    return jax.shard_map(
        per_device,
        mesh=mesh,
        in_specs=placed,
        out_specs=(
            P("section", None, "seq", "head"),
            P("section", None, "seq", "head"),
            P("section", ("seq", "head")),
            P("section", "seq", "head"),
            P("section", "seq", "head"),
            P("section", ("seq", "head"), None),
            P("section", None, "head"),
            P("section", None, ("seq", "head")),
            P("section", "head"),
            P("section", "head"),
            P("section", "head", "seq"),
        ),
        check_vma=False,
    )
```

profile of v0, /device:TPU:9, one launch (start us, length us, event | category | flops | bytes accessed | tf_op | source)
XLA Modules:
  0.0 283.0 jit_solution(17353142218673127298)
XLA Ops:
  1.2 3.0 %shard_map.212 = (bf16[144,1024]{1,0:T(8,128)(2,1)}, bf16[144,1024]{1,0:T(8,128)(2,1)}, bf16[144,1024]{1,0:T(8,128)(2,1)}, bf16[144,1024]{1,0:T(8,128)(2,1)}, s32[4]{0:T(128)}) custom-call(s32[4]{0:T(128)} %pad_add_fusion.sc, s32[4]{0:T(128)} %order.3, bf16[4,256,1024]{2,1,0:T(8,128)(2,1)} %tokens.1, f32[1,4,8,256]{3,2,1,0:T(8,128)} %rates.1), custom_call_target="tpu_custom_call" | custom-call | tf_op jit(solution)/shard_map/pallas_call | solution.py:899
  4.3 1.3 collective-permute-start
  6.7 4.1 %shard_map.213 = (bf16[1024,256]{1,0:T(8,128)(2,1)}, bf16[1024,256]{1,0:T(8,128)(2,1)}, bf16[256,1024]{1,0:T(8,128)(2,1)}, f32[16,1024]{1,0:T(8,128)}, f32[16,10...) custom-call(s32[4]{0:T(128)} %get-tuple-element.153.sc, ...), custom_call_target="tpu_custom_call" | custom-call | tf_op jit(solution)/shard_map/pallas_call | solution.py:911
  11.9 1.7 collective-permute-start.2
  14.3 12.6 %collective-permute-start.9 = (bf16[1024,256]{1,0:T(8,128)(2,1)}, bf16[1024,256]{1,0:T(8,128)(2,1)S(1)}, u32[]{:S(2)}, u32[]{:S(2)}) collective-permute-start(bf16[1024,256]{1,0:T(8,128)(2,1)} %get-tuple-element.161), channel_id=1, source_target_pairs={{0,16},{16,0},{1,17},{17,1},{2,18},{18,2},{3,19},{19,3},{4,20},{20... | collective-permute-start | bytes 1572872 | tf_op jit(solution)/shard_map/ppermute | solution.py:868
  26.9 3.6 %collective-permute-done.1.refs_2_ = bf16[144,1024]{1,0:T(8,128)(2,1)} collective-permute-done((bf16[144,1024]{1,0:T(8,128)(2,1)}, bf16[144,1024]{1,0:T(8,128)(2,1)}, u32[]{:S(2)}, u32[]{:S(2)}) %collective-permute-start.1) | collective-permute-done | bytes 294944 | tf_op jit(solution)/shard_map/ppermute | solution.py:872
  30.6 1.5 collective-permute-start.10
  32.1 1.2 collective-permute-done.2.refs_3_
  37.2 14.3 %shard_map.214 = (bf16[1024,1024]{1,0:T(8,128)(2,1)}, f32[1024,256]{1,0:T(8,128)}, bf16[1024,512]{1,0:T(8,128)(2,1)}, f32[1024,256]{1,0:T(8,128)}, bf16[4,256,12...) custom-call(s32[4]{0:T(128)S(1)} %copy-done.20, ...), custom_call_target="tpu_custom_call" | custom-call | flops 12884901888 | bytes 16000000 | tf_op jit(solution)/shard_map/pallas_call | solution.py:962
  51.5 1.4 shard_map.215
  53.0 1.6 collective-permute-start.14
  54.6 2.3 collective-permute-done.14.refs_0_
  58.1 2.2 collective-permute-start.15
  60.8 2.3 collective-permute-start.25
  63.1 1.5 collective-permute-start.26
  64.6 5.2 %shard_map.217 = (bf16[768,1024]{1,0:T(8,128)(2,1)}, bf16[768,1024]{1,0:T(8,128)(2,1)}, bf16[1024,256]{1,0:T(8,128)(2,1)S(1)}, bf16[1024,256]{1,0:T(8,128)(2,1)S(1)}) custom-call(s32[4]{0:T(128)S(1)} %get-tuple-element.175.sc, bf16[1,1024,512]{2,1,0:T(8,128)(2,1)} %refs_19_.1, bf16[1,1024,512]{2,1,0:T(8,128)(2,1)} %refs_20_.1, ...), custom_call_target="tpu_custom_call" | custom-call | flops 1000000000 | bytes 8000000 | tf_op jit(solution)/shard_map/pallas_call | solution.py:1232
  70.1 3.2 %collective-permute-done.16.refs_2_ = bf16[528,256]{1,0:T(8,128)(2,1)S(1)} collective-permute-done((bf16[528,256]{1,0:T(8,128)(2,1)S(1)}, bf16[528,256]{1,0:T(8,128)(2,1)S(1)}, u32[]{:S(2)}, u32[]{:S(2)}) %collective-permute-start.16) | collective-permute-done | bytes 270368 | tf_op jit(solution)/shard_map/ppermute | solution.py:875
  74.9 1.5 collective-permute-start.18
  78.6 5.1 %collective-permute-done.18.refs_1_ = bf16[512,256]{1,0:T(8,128)(2,1)S(1)} collective-permute-done((bf16[512,256]{1,0:T(8,128)(2,1)S(1)}, bf16[512,256]{1,0:T(8,128)(2,1)S(1)}, u32[]{:S(2)}, u32[]{:S(2)}) %collective-permute-start.18) | collective-permute-done | bytes 262176 | tf_op jit(solution)/shard_map/ppermute | solution.py:875
  83.7 1.3 collective-permute-start.22
  85.1 4.6 %collective-permute-done.19.refs_2_ = bf16[512,256]{1,0:T(8,128)(2,1)S(1)} collective-permute-done((bf16[512,256]{1,0:T(8,128)(2,1)S(1)}, bf16[512,256]{1,0:T(8,128)(2,1)S(1)}, u32[]{:S(2)}, u32[]{:S(2)}) %collective-permute-start.19) | collective-permute-done | bytes 262176 | tf_op jit(solution)/shard_map/ppermute | solution.py:875
  91.7 13.0 %shard_map.219 = (bf16[1024,1024]{1,0:T(8,128)(2,1)}, f32[1024,256]{1,0:T(8,128)}, bf16[1024,512]{1,0:T(8,128)(2,1)}, f32[1024,256]{1,0:T(8,128)}, bf16[4,256,12...) custom-call(s32[4]{0:T(128)S(1)} %copy-done.20, ...), custom_call_target="tpu_custom_call" | custom-call | flops 12884901888 | bytes 16000000 | tf_op jit(solution)/shard_map/pallas_call | solution.py:962
  105.8 2.4 shard_map.220
  108.7 2.2 collective-permute-done.31
  111.0 1.2 collective-permute-start.32
  114.8 1.5 collective-permute-start.35
  117.5 12.0 %shard_map.222 = (bf16[1024,768]{1,0:T(8,128)(2,1)}, bf16[1024,256]{1,0:T(8,128)(2,1)S(1)}, bf16[16,768]{1,0:T(8,128)(2,1)S(1)}, f32[8,512]{1,0:T(8,128)S(1)}, f...) custom-call(s32[4]{0:T(128)S(1)} %get-tuple-element.189.sc, ...), custom_call_target="tpu_custom_call" | custom-call | flops 17179869184 | bytes 16000000 | tf_op jit(solution)/shard_map/pallas_call | solution.py:1038
  129.9 5.1 %shard_map.223 = (bf16[4,528,256]{2,1,0:T(8,128)(2,1)S(1)}, bf16[528,256]{1,0:T(8,128)(2,1)S(1)}, bf16[528,256]{1,0:T(8,128)(2,1)S(1)}, bf16[528,256]{1,0:T(8,12...) custom-call(s32[4]{0:T(128)S(1)} %get-tuple-element.195.sc, ...), custom_call_target="tpu_custom_call" | custom-call | flops 2147483648 | bytes 8000000 | tf_op jit(solution)/shard_map/pallas_call | solution.py:1115
  135.0 1.5 collective-permute-start.38
  137.1 5.6 %shard_map.224 = (s32[4]{0:T(128)S(1)}, bf16[272,768]{1,0:T(8,128)(2,1)S(1)}, bf16[272,768]{1,0:T(8,128)(2,1)S(1)}, bf16[272,768]{1,0:T(8,128)(2,1)S(1)}, bf16[2...) custom-call(s32[4]{0:T(128)S(1)} %get-tuple-element.202.sc, ...), custom_call_target="tpu_custom_call" | custom-call | flops 8589934592 | bytes 12000000 | tf_op jit(solution)/shard_map/pallas_call | solution.py:1196
  142.7 2.4 collective-permute-start.45
  145.1 1.3 shard_map.225
  146.3 1.5 collective-permute-start.42
  149.1 14.1 %collective-permute-done.45.refs_10_.refs_2_ = bf16[272,768]{1,0:T(8,128)(2,1)S(1)} collective-permute-done((bf16[272,768]{1,0:T(8,128)(2,1)S(1)}, bf16[272,768]{1,0:T(8,128)(2,1)S(1)}, u32[]{:S(2)}, u32[]{:S(2)}) %collective-permute-start.45) | collective-permute-done | bytes 417824 | tf_op jit(solution)/shard_map/ppermute | solution.py:1210
  163.2 2.2 shard_map.226
  165.4 1.5 collective-permute-start.50
  168.4 1.6 collective-permute-start.46
  170.0 3.8 %collective-permute-done.50.refs_1_ = bf16[528,256]{1,0:T(8,128)(2,1)S(1)} collective-permute-done((bf16[528,256]{1,0:T(8,128)(2,1)S(1)}, bf16[528,256]{1,0:T(8,128)(2,1)S(1)}, u32[]{:S(2)}, u32[]{:S(2)}) %collective-permute-start.50) | collective-permute-done | bytes 270368 | tf_op jit(solution)/shard_map/ppermute | solution.py:875
  173.8 2.7 collective-permute-start.53
  176.5 4.1 %collective-permute-done.51.refs_2_ = bf16[528,256]{1,0:T(8,128)(2,1)S(1)} collective-permute-done((bf16[528,256]{1,0:T(8,128)(2,1)S(1)}, bf16[528,256]{1,0:T(8,128)(2,1)S(1)}, u32[]{:S(2)}, u32[]{:S(2)}) %collective-permute-start.51) | collective-permute-done | bytes 270368 | tf_op jit(solution)/shard_map/ppermute | solution.py:875
  182.7 2.2 collective-permute-start.58
  184.9 1.5 collective-permute-start.59
  186.4 4.2 %collective-permute-start.48 = (bf16[256,256]{1,0:T(8,128)(2,1)S(1)}, bf16[256,256]{1,0:T(8,128)(2,1)S(1)}, u32[]{:S(2)}, u32[]{:S(2)}) collective-permute-start(bf16[256,256]{1,0:T(8,128)(2,1)S(1)} %get-tuple-element.226), channel_id=1, source_target_pairs={{0,8},{4,12},{8,0},{12,4},{1,9},{5,13},{9,1},{13,5},{2,10},{6,14},... | collective-permute-start | bytes 393224 | tf_op jit(solution)/shard_map/ppermute | solution.py:872
  190.6 12.8 %shard_map.229 = (bf16[1024,768]{1,0:T(8,128)(2,1)}, bf16[1024,256]{1,0:T(8,128)(2,1)S(1)}, bf16[16,768]{1,0:T(8,128)(2,1)S(1)}, f32[8,512]{1,0:T(8,128)S(1)}, f...) custom-call(s32[4]{0:T(128)S(1)} %copy-done.20, ...), custom_call_target="tpu_custom_call" | custom-call | flops 17179869184 | bytes 16000000 | tf_op jit(solution)/shard_map/pallas_call | solution.py:1038
  204.7 1.9 collective-permute-done.48.refs_1_.refs_2_
  206.7 5.6 %shard_map.230 = (s32[4]{0:T(128)S(1)}, bf16[272,768]{1,0:T(8,128)(2,1)S(1)}, bf16[272,768]{1,0:T(8,128)(2,1)S(1)}, bf16[272,768]{1,0:T(8,128)(2,1)S(1)}, bf16[2...) custom-call(s32[4]{0:T(128)S(1)} %get-tuple-element.237.sc, ...), custom_call_target="tpu_custom_call" | custom-call | flops 8589934592 | bytes 12000000 | tf_op jit(solution)/shard_map/pallas_call | solution.py:1196
  212.4 5.1 %shard_map.231 = (bf16[4,528,256]{2,1,0:T(8,128)(2,1)S(1)}, bf16[528,256]{1,0:T(8,128)(2,1)S(1)}, bf16[528,256]{1,0:T(8,128)(2,1)S(1)}, bf16[528,256]{1,0:T(8,12...) custom-call(s32[4]{0:T(128)S(1)} %get-tuple-element.244.sc, ...), custom_call_target="tpu_custom_call" | custom-call | flops 2147483648 | bytes 8000000 | tf_op jit(solution)/shard_map/pallas_call | solution.py:1115
  218.5 2.0 collective-permute-start.62
  221.6 1.9 collective-permute-start.70
  223.6 1.7 collective-permute-start.71
  225.3 1.8 shard_map.232
  228.9 1.2 collective-permute-start.68
  230.7 1.8 shard_map.228
  232.5 17.6 %collective-permute-done.70.refs_14_.refs_2_ = bf16[272,768]{1,0:T(8,128)(2,1)S(1)} collective-permute-done((bf16[272,768]{1,0:T(8,128)(2,1)S(1)}, bf16[272,768]{1,0:T(8,128)(2,1)S(1)}, u32[]{:S(2)}, u32[]{:S(2)}) %collective-permute-start.70) | collective-permute-done | bytes 417824 | tf_op jit(solution)/shard_map/ppermute | solution.py:1210
  250.1 2.3 collective-permute-done.71.refs_15_.refs_3_
  253.2 2.1 shard_map.233
  259.6 1.5 collective-permute-start.74
  261.2 1.5 collective-permute-start.75
  262.6 2.8 %collective-permute-done.73.refs_5_.refs_1_ = bf16[336,256]{1,0:T(8,128)(2,1)S(1)} collective-permute-done((bf16[336,256]{1,0:T(8,128)(2,1)S(1)}, bf16[336,256]{1,0:T(8,128)(2,1)S(1)}, u32[]{:S(2)}, u32[]{:S(2)}) %collective-permute-start.73) | collective-permute-done | bytes 172064 | tf_op jit(solution)/shard_map/ppermute | solution.py:872
  265.5 9.1 %collective-permute-done.74.refs_6_.refs_2_ = bf16[336,256]{1,0:T(8,128)(2,1)S(1)} collective-permute-done((bf16[336,256]{1,0:T(8,128)(2,1)S(1)}, bf16[336,256]{1,0:T(8,128)(2,1)S(1)}, u32[]{:S(2)}, u32[]{:S(2)}) %collective-permute-start.74) | collective-permute-done | bytes 172064 | tf_op jit(solution)/shard_map/ppermute | solution.py:872
  274.6 2.5 collective-permute-done.75.refs_7_.refs_3_
  277.1 1.2 shard_map.239
  278.3 1.8 shard_map.237
  280.8 2.0 shard_map.238
  (184 shorter events, 37.7 us)
Async XLA Ops:
  4.3 10.0 %collective-permute-start = (bf16[144,1024]{1,0:T(8,128)(2,1)}, bf16[144,1024]{1,0:T(8,128)(2,1)}, u32[]{:S(2)}, u32[]{:S(2)}) collective-permute-start(bf16[144,1024]{1,0:T(8,128)(2,1)} %get-tuple-element.155), channel_id=1, source_target_pairs={{0,4},{4,8},{8,12},{12,0},{1,5},{5,9},{9,13},{13,1},{2,6},{6,10},{... | collective-permute-start | bytes 884744 | tf_op jit(solution)/shard_map/ppermute | solution.py:872
  5.6 25.0 %collective-permute-start.1 = (bf16[144,1024]{1,0:T(8,128)(2,1)}, bf16[144,1024]{1,0:T(8,128)(2,1)}, u32[]{:S(2)}, u32[]{:S(2)}) collective-permute-start(bf16[144,1024]{1,0:T(8,128)(2,1)} %get-tuple-element.156), channel_id=1, source_target_pairs={{0,8},{4,12},{8,0},{12,4},{1,9},{5,13},{9,1},{13,5},{2,10},{6,14},... | collective-permute-start | bytes 884744 | tf_op jit(solution)/shard_map/ppermute | solution.py:872
  10.8 23.0 %collective-permute-start.8 = (bf16[1024,256]{1,0:T(8,128)(2,1)}, bf16[1024,256]{1,0:T(8,128)(2,1)S(1)}, u32[]{:S(2)}, u32[]{:S(2)}) collective-permute-start(bf16[1024,256]{1,0:T(8,128)(2,1)} %get-tuple-element.160), channel_id=1, source_target_pairs={{0,16},{16,0},{1,17},{17,1},{2,18},{18,2},{3,19},{19,3},{4,20},{20... | collective-permute-start | bytes 1572872 | tf_op jit(solution)/shard_map/ppermute | solution.py:868
  11.9 21.4 %collective-permute-start.2 = (bf16[144,1024]{1,0:T(8,128)(2,1)}, bf16[144,1024]{1,0:T(8,128)(2,1)S(1)}, u32[]{:S(2)}, u32[]{:S(2)}) collective-permute-start(bf16[144,1024]{1,0:T(8,128)(2,1)} %get-tuple-element.157), channel_id=1, source_target_pairs={{0,12},{4,0},{8,4},{12,8},{1,13},{5,1},{9,5},{13,9},{2,14},{6,2},{... | collective-permute-start | bytes 884744 | tf_op jit(solution)/shard_map/ppermute | solution.py:872
  13.7 20.1 %collective-permute-start.3 = (bf16[144,1024]{1,0:T(8,128)(2,1)S(1)}, bf16[144,1024]{1,0:T(8,128)(2,1)S(1)}, u32[]{:S(2)}, u32[]{:S(2)}) collective-permute-start(bf16[144,1024]{1,0:T(8,128)(2,1)S(1)} %copy-done.22), channel_id=1, source_target_pairs={{0,16},{16,0},{1,17},{17,1},{2,18},{18,2},{3,19},{19,3},{4,20},{20... | collective-permute-start | bytes 884744 | tf_op jit(solution)/shard_map/ppermute | solution.py:868
  14.3 20.0 %collective-permute-start.9 = (bf16[1024,256]{1,0:T(8,128)(2,1)}, bf16[1024,256]{1,0:T(8,128)(2,1)S(1)}, u32[]{:S(2)}, u32[]{:S(2)}) collective-permute-start(bf16[1024,256]{1,0:T(8,128)(2,1)} %get-tuple-element.161), channel_id=1, source_target_pairs={{0,16},{16,0},{1,17},{17,1},{2,18},{18,2},{3,19},{19,3},{4,20},{20... | collective-permute-start | bytes 1572872 | tf_op jit(solution)/shard_map/ppermute | solution.py:868
  34.3 17.2 %collective-permute-start.11 = (bf16[256,1024]{1,0:T(8,128)(2,1)}, bf16[256,1024]{1,0:T(8,128)(2,1)S(1)}, u32[]{:S(2)}, u32[]{:S(2)}) collective-permute-start(bf16[256,1024]{1,0:T(8,128)(2,1)} %get-tuple-element.165), channel_id=1, source_target_pairs={{0,16},{16,0},{1,17},{17,1},{2,18},{18,2},{3,19},{19,3},{4,20},{20... | collective-permute-start | bytes 1572872 | tf_op jit(solution)/shard_map/ppermute | solution.py:868
  34.4 17.1 %collective-permute-start.12 = (bf16[128,1024]{1,0:T(8,128)(2,1)}, bf16[128,1024]{1,0:T(8,128)(2,1)S(1)}, u32[]{:S(2)}, u32[]{:S(2)}) collective-permute-start(bf16[128,1024]{1,0:T(8,128)(2,1)} %get-tuple-element.166), channel_id=1, source_target_pairs={{0,4},{4,8},{8,12},{12,0},{1,5},{5,9},{9,13},{13,1},{2,6},{6,10},{... | collective-permute-start | bytes 786440 | tf_op jit(solution)/shard_map/ppermute | solution.py:872
  35.2 16.3 %collective-permute-start.13 = (bf16[128,1024]{1,0:T(8,128)(2,1)}, bf16[128,1024]{1,0:T(8,128)(2,1)S(1)}, u32[]{:S(2)}, u32[]{:S(2)}) collective-permute-start(bf16[128,1024]{1,0:T(8,128)(2,1)} %get-tuple-element.167), channel_id=1, source_target_pairs={{0,12},{4,0},{8,4},{12,8},{1,13},{5,1},{9,5},{13,9},{2,14},{6,2},{... | collective-permute-start | bytes 786440 | tf_op jit(solution)/shard_map/ppermute | solution.py:872
  58.1 11.7 %collective-permute-start.15 = (bf16[528,256]{1,0:T(8,128)(2,1)S(1)}, bf16[528,256]{1,0:T(8,128)(2,1)S(1)}, u32[]{:S(2)}, u32[]{:S(2)}) collective-permute-start(bf16[528,256]{1,0:T(8,128)(2,1)S(1)} %get-tuple-element.171), channel_id=1, source_target_pairs={{0,3},{1,2},{2,1},{3,0},{4,7},{5,6},{6,5},{7,4},{8,11},{9,10},{10,... | collective-permute-start | bytes 811016 | tf_op jit(solution)/shard_map/ppermute | solution.py:875
  60.3 12.9 %collective-permute-start.16 = (bf16[528,256]{1,0:T(8,128)(2,1)S(1)}, bf16[528,256]{1,0:T(8,128)(2,1)S(1)}, u32[]{:S(2)}, u32[]{:S(2)}) collective-permute-start(bf16[528,256]{1,0:T(8,128)(2,1)S(1)} %get-tuple-element.172), channel_id=1, source_target_pairs={{0,2},{1,3},{2,0},{3,1},{4,6},{5,7},{6,4},{7,5},{8,10},{9,11},{10,... | collective-permute-start | bytes 811016 | tf_op jit(solution)/shard_map/ppermute | solution.py:875
  60.6 13.2 %collective-permute-start.17 = (bf16[528,256]{1,0:T(8,128)(2,1)S(1)}, bf16[528,256]{1,0:T(8,128)(2,1)S(1)}, u32[]{:S(2)}, u32[]{:S(2)}) collective-permute-start(bf16[528,256]{1,0:T(8,128)(2,1)S(1)} %get-tuple-element.173), channel_id=1, source_target_pairs={{0,1},{1,0},{2,3},{3,2},{4,5},{5,4},{6,7},{7,6},{8,9},{9,8},{10,11... | collective-permute-start | bytes 811016 | tf_op jit(solution)/shard_map/ppermute | solution.py:875
  60.8 15.6 %collective-permute-start.25 = (bf16[128,1024]{1,0:T(8,128)(2,1)S(1)}, bf16[128,1024]{1,0:T(8,128)(2,1)S(1)}, u32[]{:S(2)}, u32[]{:S(2)}) collective-permute-start(bf16[128,1024]{1,0:T(8,128)(2,1)S(1)} %copy-done.26), channel_id=1, source_target_pairs={{0,8},{4,12},{8,0},{12,4},{1,9},{5,13},{9,1},{13,5},{2,10},{6,14},... | collective-permute-start | bytes 786440 | tf_op jit(solution)/shard_map/ppermute | solution.py:872
  63.1 14.2 %collective-permute-start.26 = (bf16[128,1024]{1,0:T(8,128)(2,1)S(1)}, bf16[128,1024]{1,0:T(8,128)(2,1)S(1)}, u32[]{:S(2)}, u32[]{:S(2)}) collective-permute-start(bf16[128,1024]{1,0:T(8,128)(2,1)S(1)} %copy-done.23), channel_id=1, source_target_pairs={{0,16},{16,0},{1,17},{17,1},{2,18},{18,2},{3,19},{19,3},{4,20},{20... | collective-permute-start | bytes 786440 | tf_op jit(solution)/shard_map/ppermute | solution.py:868
  69.8 7.8 %collective-permute-start.27 = (bf16[128,1024]{1,0:T(8,128)(2,1)S(1)}, bf16[128,1024]{1,0:T(8,128)(2,1)S(1)}, u32[]{:S(2)}, u32[]{:S(2)}) collective-permute-start(bf16[128,1024]{1,0:T(8,128)(2,1)S(1)} %collective-permute-done.12.refs_2_.refs_9_), channel_id=1, source_target_pairs={{0,16},{16,0},{1,17},{17,1},{2,18},{18,2},{3,19},{19,3},{4,20},{20... | collective-permute-start | bytes 786440 | tf_op jit(solution)/shard_map/ppermute | solution.py:868
  73.3 5.3 %collective-permute-start.29 = (bf16[128,1024]{1,0:T(8,128)(2,1)S(1)}, bf16[128,1024]{1,0:T(8,128)(2,1)S(1)}, u32[]{:S(2)}, u32[]{:S(2)}) collective-permute-start(bf16[128,1024]{1,0:T(8,128)(2,1)S(1)} %collective-permute-done.13.refs_3_.refs_11_), channel_id=1, source_target_pairs={{0,16},{16,0},{1,17},{17,1},{2,18},{18,2},{3,19},{19,3},{4,20},{20... | collective-permute-start | bytes 786440 | tf_op jit(solution)/shard_map/ppermute | solution.py:868
  74.9 8.9 %collective-permute-start.18 = (bf16[512,256]{1,0:T(8,128)(2,1)S(1)}, bf16[512,256]{1,0:T(8,128)(2,1)S(1)}, u32[]{:S(2)}, u32[]{:S(2)}) collective-permute-start(bf16[512,256]{1,0:T(8,128)(2,1)S(1)} %get-tuple-element.180.refs_0_.zero_own), channel_id=1, source_target_pairs={{0,3},{1,2},{2,1},{3,0},{4,7},{5,6},{6,5},{7,4},{8,11},{9,10},{10,... | collective-permute-start | bytes 786440 | tf_op jit(solution)/shard_map/ppermute | solution.py:875
  76.4 13.3 %collective-permute-start.19 = (bf16[512,256]{1,0:T(8,128)(2,1)S(1)}, bf16[512,256]{1,0:T(8,128)(2,1)S(1)}, u32[]{:S(2)}, u32[]{:S(2)}) collective-permute-start(bf16[512,256]{1,0:T(8,128)(2,1)S(1)} %get-tuple-element.180.refs_0_.zero_own), channel_id=1, source_target_pairs={{0,2},{1,3},{2,0},{3,1},{4,6},{5,7},{6,4},{7,5},{8,10},{9,11},{10,... | collective-permute-start | bytes 786440 | tf_op jit(solution)/shard_map/ppermute | solution.py:875
  77.3 12.8 %collective-permute-start.20 = (bf16[512,256]{1,0:T(8,128)(2,1)S(1)}, bf16[512,256]{1,0:T(8,128)(2,1)S(1)}, u32[]{:S(2)}, u32[]{:S(2)}) collective-permute-start(bf16[512,256]{1,0:T(8,128)(2,1)S(1)} %get-tuple-element.180.refs_0_.zero_own), channel_id=1, source_target_pairs={{0,1},{1,0},{2,3},{3,2},{4,5},{5,4},{6,7},{7,6},{8,9},{9,8},{10,11... | collective-permute-start | bytes 786440 | tf_op jit(solution)/shard_map/ppermute | solution.py:875
  77.6 12.7 %collective-permute-start.28 = (bf16[128,1024]{1,0:T(8,128)(2,1)S(1)}, bf16[128,1024]{1,0:T(8,128)(2,1)S(1)}, u32[]{:S(2)}, u32[]{:S(2)}) collective-permute-start(bf16[128,1024]{1,0:T(8,128)(2,1)S(1)} %collective-permute-done.25.refs_10_), channel_id=1, source_target_pairs={{0,16},{16,0},{1,17},{17,1},{2,18},{18,2},{3,19},{19,3},{4,20},{20... | collective-permute-start | bytes 786440 | tf_op jit(solution)/shard_map/ppermute | solution.py:868
  78.5 11.7 %collective-permute-start.21 = (bf16[512,256]{1,0:T(8,128)(2,1)S(1)}, bf16[512,256]{1,0:T(8,128)(2,1)S(1)}, u32[]{:S(2)}, u32[]{:S(2)}) collective-permute-start(bf16[512,256]{1,0:T(8,128)(2,1)S(1)} %get-tuple-element.180.refs_0_.zero_own), channel_id=1, source_target_pairs={{0,16},{16,0},{1,17},{17,1},{2,18},{18,2},{3,19},{19,3},{4,20},{20... | collective-permute-start | bytes 786440 | tf_op jit(solution)/shard_map/ppermute | solution.py:868
  83.7 6.5 %collective-permute-start.22 = (bf16[512,256]{1,0:T(8,128)(2,1)S(1)}, bf16[512,256]{1,0:T(8,128)(2,1)S(1)}, u32[]{:S(2)}, u32[]{:S(2)}) collective-permute-start(bf16[512,256]{1,0:T(8,128)(2,1)S(1)} %collective-permute-done.18.refs_1_), channel_id=1, source_target_pairs={{0,16},{16,0},{1,17},{17,1},{2,18},{18,2},{3,19},{19,3},{4,20},{20... | collective-permute-start | bytes 786440 | tf_op jit(solution)/shard_map/ppermute | solution.py:868
  108.2 5.4 %collective-permute-start.30 = (bf16[4,528,256]{2,1,0:T(8,128)(2,1)S(1)}, bf16[4,528,256]{2,1,0:T(8,128)(2,1)S(1)}, u32[]{:S(2)}, u32[]{:S(2)}) collective-permute-start(bf16[4,528,256]{2,1,0:T(8,128)(2,1)S(1)} %get-tuple-element.188), channel_id=1, source_target_pairs={{0,16},{16,0},{1,17},{17,1},{2,18},{18,2},{3,19},{19,3},{4,20},{20... | collective-permute-start | bytes 3244040 | tf_op jit(solution)/shard_map/ppermute | solution.py:868
  111.0 6.3 %collective-permute-start.32 = (f32[2,1024]{1,0:T(2,128)S(1)}, f32[2,1024]{1,0:T(2,128)S(1)}, u32[]{:S(2)}, u32[]{:S(2)}) collective-permute-start(f32[2,1024]{1,0:T(2,128)S(1)} %add.3.refs_1_), channel_id=1, source_target_pairs={{0,1},{1,0},{2,3},{3,2},{4,5},{5,4},{6,7},{7,6},{8,9},{9,8},{10,11... | collective-permute-start | bytes 24584 | tf_op jit(solution)/shard_map/ppermute | solution.py:875
  112.2 5.3 %collective-permute-start.33 = (f32[2,1024]{1,0:T(2,128)S(1)}, f32[2,1024]{1,0:T(2,128)S(1)}, u32[]{:S(2)}, u32[]{:S(2)}) collective-permute-start(f32[2,1024]{1,0:T(2,128)S(1)} %add.3.refs_1_), channel_id=1, source_target_pairs={{0,2},{1,3},{2,0},{3,1},{4,6},{5,7},{6,4},{7,5},{8,10},{9,11},{10,... | collective-permute-start | bytes 24584 | tf_op jit(solution)/shard_map/ppermute | solution.py:875
  112.7 4.8 %collective-permute-start.34 = (f32[2,1024]{1,0:T(2,128)S(1)}, f32[2,1024]{1,0:T(2,128)S(1)}, u32[]{:S(2)}, u32[]{:S(2)}) collective-permute-start(f32[2,1024]{1,0:T(2,128)S(1)} %add.3.refs_1_), channel_id=1, source_target_pairs={{0,3},{1,2},{2,1},{3,0},{4,7},{5,6},{6,5},{7,4},{8,11},{9,10},{10,... | collective-permute-start | bytes 24584 | tf_op jit(solution)/shard_map/ppermute | solution.py:875
  114.8 14.8 %collective-permute-start.35 = (bf16[528,256]{1,0:T(8,128)(2,1)S(1)}, bf16[528,256]{1,0:T(8,128)(2,1)S(1)}, u32[]{:S(2)}, u32[]{:S(2)}) collective-permute-start(bf16[528,256]{1,0:T(8,128)(2,1)S(1)} %get-tuple-element.199), channel_id=1, source_target_pairs={{0,3},{1,2},{2,1},{3,0},{4,7},{5,6},{6,5},{7,4},{8,11},{9,10},{10,... | collective-permute-start | bytes 811016 | tf_op jit(solution)/shard_map/ppermute | solution.py:875
  116.3 13.6 %collective-permute-start.36 = (bf16[528,256]{1,0:T(8,128)(2,1)S(1)}, bf16[528,256]{1,0:T(8,128)(2,1)S(1)}, u32[]{:S(2)}, u32[]{:S(2)}) collective-permute-start(bf16[528,256]{1,0:T(8,128)(2,1)S(1)} %get-tuple-element.200), channel_id=1, source_target_pairs={{0,2},{1,3},{2,0},{3,1},{4,6},{5,7},{6,4},{7,5},{8,10},{9,11},{10,... | collective-permute-start | bytes 811016 | tf_op jit(solution)/shard_map/ppermute | solution.py:875
  117.2 12.7 %collective-permute-start.37 = (bf16[528,256]{1,0:T(8,128)(2,1)S(1)}, bf16[528,256]{1,0:T(8,128)(2,1)S(1)}, u32[]{:S(2)}, u32[]{:S(2)}) collective-permute-start(bf16[528,256]{1,0:T(8,128)(2,1)S(1)} %get-tuple-element.201), channel_id=1, source_target_pairs={{0,1},{1,0},{2,3},{3,2},{4,5},{5,4},{6,7},{7,6},{8,9},{9,8},{10,11... | collective-permute-start | bytes 811016 | tf_op jit(solution)/shard_map/ppermute | solution.py:875
  135.0 10.0 %collective-permute-start.38 = (bf16[528,256]{1,0:T(8,128)(2,1)S(1)}, bf16[528,256]{1,0:T(8,128)(2,1)S(1)}, u32[]{:S(2)}, u32[]{:S(2)}) collective-permute-start(bf16[528,256]{1,0:T(8,128)(2,1)S(1)} %get-tuple-element.208), channel_id=1, source_target_pairs={{0,16},{16,0},{1,17},{17,1},{2,18},{18,2},{3,19},{19,3},{4,20},{20... | collective-permute-start | bytes 811016 | tf_op jit(solution)/shard_map/ppermute | solution.py:868
  136.6 8.5 %collective-permute-start.39 = (bf16[528,256]{1,0:T(8,128)(2,1)S(1)}, bf16[528,256]{1,0:T(8,128)(2,1)S(1)}, u32[]{:S(2)}, u32[]{:S(2)}) collective-permute-start(bf16[528,256]{1,0:T(8,128)(2,1)S(1)} %get-tuple-element.209), channel_id=1, source_target_pairs={{0,16},{16,0},{1,17},{17,1},{2,18},{18,2},{3,19},{19,3},{4,20},{20... | collective-permute-start | bytes 811016 | tf_op jit(solution)/shard_map/ppermute | solution.py:868
  136.6 8.4 %collective-permute-start.40 = (bf16[528,256]{1,0:T(8,128)(2,1)S(1)}, bf16[528,256]{1,0:T(8,128)(2,1)S(1)}, u32[]{:S(2)}, u32[]{:S(2)}) collective-permute-start(bf16[528,256]{1,0:T(8,128)(2,1)S(1)} %get-tuple-element.210), channel_id=1, source_target_pairs={{0,16},{16,0},{1,17},{17,1},{2,18},{18,2},{3,19},{19,3},{4,20},{20... | collective-permute-start | bytes 811016 | tf_op jit(solution)/shard_map/ppermute | solution.py:868
  137.1 8.0 %collective-permute-start.41 = (bf16[528,256]{1,0:T(8,128)(2,1)S(1)}, bf16[528,256]{1,0:T(8,128)(2,1)S(1)}, u32[]{:S(2)}, u32[]{:S(2)}) collective-permute-start(bf16[528,256]{1,0:T(8,128)(2,1)S(1)} %get-tuple-element.211), channel_id=1, source_target_pairs={{0,16},{16,0},{1,17},{17,1},{2,18},{18,2},{3,19},{19,3},{4,20},{20... | collective-permute-start | bytes 811016 | tf_op jit(solution)/shard_map/ppermute | solution.py:868
  142.7 20.5 %collective-permute-start.45 = (bf16[272,768]{1,0:T(8,128)(2,1)S(1)}, bf16[272,768]{1,0:T(8,128)(2,1)S(1)}, u32[]{:S(2)}, u32[]{:S(2)}) collective-permute-start(bf16[272,768]{1,0:T(8,128)(2,1)S(1)} %get-tuple-element.221), channel_id=1, source_target_pairs={{0,8},{4,12},{8,0},{12,4},{1,9},{5,13},{9,1},{13,5},{2,10},{6,14},... | collective-permute-start | bytes 1253384 | tf_op jit(solution)/shard_map/ppermute | solution.py:1210
  146.3 16.9 %collective-permute-start.42 = (bf16[528,256]{1,0:T(8,128)(2,1)S(1)}, bf16[528,256]{1,0:T(8,128)(2,1)S(1)}, u32[]{:S(2)}, u32[]{:S(2)}) collective-permute-start(bf16[528,256]{1,0:T(8,128)(2,1)S(1)} %get-tuple-element.214), channel_id=1, source_target_pairs={{0,3},{1,2},{2,1},{3,0},{4,7},{5,6},{6,5},{7,4},{8,11},{9,10},{10,... | collective-permute-start | bytes 811016 | tf_op jit(solution)/shard_map/ppermute | solution.py:875
  147.9 15.3 %collective-permute-start.43 = (bf16[528,256]{1,0:T(8,128)(2,1)S(1)}, bf16[528,256]{1,0:T(8,128)(2,1)S(1)}, u32[]{:S(2)}, u32[]{:S(2)}) collective-permute-start(bf16[528,256]{1,0:T(8,128)(2,1)S(1)} %get-tuple-element.215), channel_id=1, source_target_pairs={{0,2},{1,3},{2,0},{3,1},{4,6},{5,7},{6,4},{7,5},{8,10},{9,11},{10,... | collective-permute-start | bytes 811016 | tf_op jit(solution)/shard_map/ppermute | solution.py:875
  148.8 14.4 %collective-permute-start.44 = (bf16[528,256]{1,0:T(8,128)(2,1)S(1)}, bf16[528,256]{1,0:T(8,128)(2,1)S(1)}, u32[]{:S(2)}, u32[]{:S(2)}) collective-permute-start(bf16[528,256]{1,0:T(8,128)(2,1)S(1)} %get-tuple-element.216), channel_id=1, source_target_pairs={{0,1},{1,0},{2,3},{3,2},{4,5},{5,4},{6,7},{7,6},{8,9},{9,8},{10,11... | collective-permute-start | bytes 811016 | tf_op jit(solution)/shard_map/ppermute | solution.py:875
  165.4 8.4 %collective-permute-start.50 = (bf16[528,256]{1,0:T(8,128)(2,1)S(1)}, bf16[528,256]{1,0:T(8,128)(2,1)S(1)}, u32[]{:S(2)}, u32[]{:S(2)}) collective-permute-start(bf16[528,256]{1,0:T(8,128)(2,1)S(1)} %get-tuple-element.223.one_own.refs_0_), channel_id=1, source_target_pairs={{0,3},{1,2},{2,1},{3,0},{4,7},{5,6},{6,5},{7,4},{8,11},{9,10},{10,... | collective-permute-start | bytes 811016 | tf_op jit(solution)/shard_map/ppermute | solution.py:875
  166.9 13.6 %collective-permute-start.51 = (bf16[528,256]{1,0:T(8,128)(2,1)S(1)}, bf16[528,256]{1,0:T(8,128)(2,1)S(1)}, u32[]{:S(2)}, u32[]{:S(2)}) collective-permute-start(bf16[528,256]{1,0:T(8,128)(2,1)S(1)} %get-tuple-element.223.one_own.refs_0_), channel_id=1, source_target_pairs={{0,2},{1,3},{2,0},{3,1},{4,6},{5,7},{6,4},{7,5},{8,10},{9,11},{10,... | collective-permute-start | bytes 811016 | tf_op jit(solution)/shard_map/ppermute | solution.py:875
  167.9 13.2 %collective-permute-start.52 = (bf16[528,256]{1,0:T(8,128)(2,1)S(1)}, bf16[528,256]{1,0:T(8,128)(2,1)S(1)}, u32[]{:S(2)}, u32[]{:S(2)}) collective-permute-start(bf16[528,256]{1,0:T(8,128)(2,1)S(1)} %get-tuple-element.223.one_own.refs_0_), channel_id=1, source_target_pairs={{0,1},{1,0},{2,3},{3,2},{4,5},{5,4},{6,7},{7,6},{8,9},{9,8},{10,11... | collective-permute-start | bytes 811016 | tf_op jit(solution)/shard_map/ppermute | solution.py:875
  168.1 16.8 %collective-permute-start.57 = (bf16[272,768]{1,0:T(8,128)(2,1)S(1)}, bf16[272,768]{1,0:T(8,128)(2,1)S(1)}, u32[]{:S(2)}, u32[]{:S(2)}) collective-permute-start(bf16[272,768]{1,0:T(8,128)(2,1)S(1)} %get-tuple-element.236), channel_id=1, source_target_pairs={{0,4},{4,8},{8,12},{12,0},{1,5},{5,9},{9,13},{13,1},{2,6},{6,10},{... | collective-permute-start | bytes 1253384 | tf_op jit(solution)/shard_map/ppermute | solution.py:1210
  168.4 12.8 %collective-permute-start.46 = (bf16[528,256]{1,0:T(8,128)(2,1)S(1)}, bf16[528,256]{1,0:T(8,128)(2,1)S(1)}, u32[]{:S(2)}, u32[]{:S(2)}) collective-permute-start(bf16[528,256]{1,0:T(8,128)(2,1)S(1)} %get-tuple-element.223.one_own.refs_0_), channel_id=1, source_target_pairs={{0,16},{16,0},{1,17},{17,1},{2,18},{18,2},{3,19},{19,3},{4,20},{20... | collective-permute-start | bytes 811016 | tf_op jit(solution)/shard_map/ppermute | solution.py:868
  173.8 12.6 %collective-permute-start.53 = (bf16[528,256]{1,0:T(8,128)(2,1)S(1)}, bf16[528,256]{1,0:T(8,128)(2,1)S(1)}, u32[]{:S(2)}, u32[]{:S(2)}) collective-permute-start(bf16[528,256]{1,0:T(8,128)(2,1)S(1)} %collective-permute-done.50.refs_1_), channel_id=1, source_target_pairs={{0,16},{16,0},{1,17},{17,1},{2,18},{18,2},{3,19},{19,3},{4,20},{20... | collective-permute-start | bytes 811016 | tf_op jit(solution)/shard_map/ppermute | solution.py:868
  180.6 5.8 %collective-permute-start.54 = (bf16[528,256]{1,0:T(8,128)(2,1)S(1)}, bf16[528,256]{1,0:T(8,128)(2,1)S(1)}, u32[]{:S(2)}, u32[]{:S(2)}) collective-permute-start(bf16[528,256]{1,0:T(8,128)(2,1)S(1)} %collective-permute-done.51.refs_2_), channel_id=1, source_target_pairs={{0,16},{16,0},{1,17},{17,1},{2,18},{18,2},{3,19},{19,3},{4,20},{20... | collective-permute-start | bytes 811016 | tf_op jit(solution)/shard_map/ppermute | solution.py:868
  181.1 9.5 %collective-permute-start.55 = (bf16[528,256]{1,0:T(8,128)(2,1)S(1)}, bf16[528,256]{1,0:T(8,128)(2,1)S(1)}, u32[]{:S(2)}, u32[]{:S(2)}) collective-permute-start(bf16[528,256]{1,0:T(8,128)(2,1)S(1)} %collective-permute-done.52.refs_3_), channel_id=1, source_target_pairs={{0,16},{16,0},{1,17},{17,1},{2,18},{18,2},{3,19},{19,3},{4,20},{20... | collective-permute-start | bytes 811016 | tf_op jit(solution)/shard_map/ppermute | solution.py:868
  182.7 20.7 %collective-permute-start.58 = (bf16[272,768]{1,0:T(8,128)(2,1)S(1)}, bf16[272,768]{1,0:T(8,128)(2,1)S(1)}, u32[]{:S(2)}, u32[]{:S(2)}) collective-permute-start(bf16[272,768]{1,0:T(8,128)(2,1)S(1)} %get-tuple-element.243), channel_id=1, source_target_pairs={{0,12},{4,0},{8,4},{12,8},{1,13},{5,1},{9,5},{13,9},{2,14},{6,2},{... | collective-permute-start | bytes 1253384 | tf_op jit(solution)/shard_map/ppermute | solution.py:1210
  184.9 27.4 %collective-permute-start.59 = (bf16[272,256]{1,0:T(8,128)(2,1)S(1)}, bf16[272,256]{1,0:T(8,128)(2,1)S(1)}, u32[]{:S(2)}, u32[]{:S(2)}) collective-permute-start(bf16[272,256]{1,0:T(8,128)(2,1)S(1)} %get-tuple-element.246), channel_id=1, source_target_pairs={{0,3},{1,2},{2,1},{3,0},{4,7},{5,6},{6,5},{7,4},{8,11},{9,10},{10,... | collective-permute-start | bytes 417800 | tf_op jit(solution)/shard_map/ppermute | solution.py:875
  186.4 18.1 %collective-permute-start.47 = (bf16[256,256]{1,0:T(8,128)(2,1)S(1)}, bf16[256,256]{1,0:T(8,128)(2,1)S(1)}, u32[]{:S(2)}, u32[]{:S(2)}) collective-permute-start(bf16[256,256]{1,0:T(8,128)(2,1)S(1)} %get-tuple-element.225), channel_id=1, source_target_pairs={{0,4},{4,8},{8,12},{12,0},{1,5},{5,9},{9,13},{13,1},{2,6},{6,10},{... | collective-permute-start | bytes 393224 | tf_op jit(solution)/shard_map/ppermute | solution.py:872
  186.4 20.2 %collective-permute-start.48 = (bf16[256,256]{1,0:T(8,128)(2,1)S(1)}, bf16[256,256]{1,0:T(8,128)(2,1)S(1)}, u32[]{:S(2)}, u32[]{:S(2)}) collective-permute-start(bf16[256,256]{1,0:T(8,128)(2,1)S(1)} %get-tuple-element.226), channel_id=1, source_target_pairs={{0,8},{4,12},{8,0},{12,4},{1,9},{5,13},{9,1},{13,5},{2,10},{6,14},... | collective-permute-start | bytes 393224 | tf_op jit(solution)/shard_map/ppermute | solution.py:872
  190.6 16.1 %collective-permute-start.49 = (bf16[256,256]{1,0:T(8,128)(2,1)S(1)}, bf16[256,256]{1,0:T(8,128)(2,1)S(1)}, u32[]{:S(2)}, u32[]{:S(2)}) collective-permute-start(bf16[256,256]{1,0:T(8,128)(2,1)S(1)} %get-tuple-element.227), channel_id=1, source_target_pairs={{0,12},{4,0},{8,4},{12,8},{1,13},{5,1},{9,5},{13,9},{2,14},{6,2},{... | collective-permute-start | bytes 393224 | tf_op jit(solution)/shard_map/ppermute | solution.py:872
  203.4 8.9 %collective-permute-start.60 = (bf16[272,256]{1,0:T(8,128)(2,1)S(1)}, bf16[272,256]{1,0:T(8,128)(2,1)S(1)}, u32[]{:S(2)}, u32[]{:S(2)}) collective-permute-start(bf16[272,256]{1,0:T(8,128)(2,1)S(1)} %get-tuple-element.247), channel_id=1, source_target_pairs={{0,2},{1,3},{2,0},{3,1},{4,6},{5,7},{6,4},{7,5},{8,10},{9,11},{10,... | collective-permute-start | bytes 417800 | tf_op jit(solution)/shard_map/ppermute | solution.py:875
  204.5 7.9 %collective-permute-start.61 = (bf16[272,256]{1,0:T(8,128)(2,1)S(1)}, bf16[272,256]{1,0:T(8,128)(2,1)S(1)}, u32[]{:S(2)}, u32[]{:S(2)}) collective-permute-start(bf16[272,256]{1,0:T(8,128)(2,1)S(1)} %get-tuple-element.248), channel_id=1, source_target_pairs={{0,1},{1,0},{2,3},{3,2},{4,5},{5,4},{6,7},{7,6},{8,9},{9,8},{10,11... | collective-permute-start | bytes 417800 | tf_op jit(solution)/shard_map/ppermute | solution.py:875
  212.3 13.0 %collective-permute-start.66 = (bf16[272,768]{1,0:T(8,128)(2,1)S(1)}, bf16[272,768]{1,0:T(8,128)(2,1)S(1)}, u32[]{:S(2)}, u32[]{:S(2)}) collective-permute-start(bf16[272,768]{1,0:T(8,128)(2,1)S(1)} %get-tuple-element.260), channel_id=1, source_target_pairs={{0,4},{4,8},{8,12},{12,0},{1,5},{5,9},{9,13},{13,1},{2,6},{6,10},{... | collective-permute-start | bytes 1253384 | tf_op jit(solution)/shard_map/ppermute | solution.py:1210
  220.5 4.8 %collective-permute-start.64 = (bf16[528,256]{1,0:T(8,128)(2,1)S(1)}, bf16[528,256]{1,0:T(8,128)(2,1)S(1)}, u32[]{:S(2)}, u32[]{:S(2)}) collective-permute-start(bf16[528,256]{1,0:T(8,128)(2,1)S(1)} %get-tuple-element.253), channel_id=1, source_target_pairs={{0,16},{16,0},{1,17},{17,1},{2,18},{18,2},{3,19},{19,3},{4,20},{20... | collective-permute-start | bytes 811016 | tf_op jit(solution)/shard_map/ppermute | solution.py:868
  221.0 4.3 %collective-permute-start.65 = (bf16[528,256]{1,0:T(8,128)(2,1)S(1)}, bf16[528,256]{1,0:T(8,128)(2,1)S(1)}, u32[]{:S(2)}, u32[]{:S(2)}) collective-permute-start(bf16[528,256]{1,0:T(8,128)(2,1)S(1)} %get-tuple-element.254), channel_id=1, source_target_pairs={{0,16},{16,0},{1,17},{17,1},{2,18},{18,2},{3,19},{19,3},{4,20},{20... | collective-permute-start | bytes 811016 | tf_op jit(solution)/shard_map/ppermute | solution.py:868
  221.6 28.5 %collective-permute-start.70 = (bf16[272,768]{1,0:T(8,128)(2,1)S(1)}, bf16[272,768]{1,0:T(8,128)(2,1)S(1)}, u32[]{:S(2)}, u32[]{:S(2)}) collective-permute-start(bf16[272,768]{1,0:T(8,128)(2,1)S(1)} %get-tuple-element.269), channel_id=1, source_target_pairs={{0,8},{4,12},{8,0},{12,4},{1,9},{5,13},{9,1},{13,5},{2,10},{6,14},... | collective-permute-start | bytes 1253384 | tf_op jit(solution)/shard_map/ppermute | solution.py:1210
  223.6 28.9 %collective-permute-start.71 = (bf16[272,768]{1,0:T(8,128)(2,1)S(1)}, bf16[272,768]{1,0:T(8,128)(2,1)S(1)}, u32[]{:S(2)}, u32[]{:S(2)}) collective-permute-start(bf16[272,768]{1,0:T(8,128)(2,1)S(1)} %get-tuple-element.270), channel_id=1, source_target_pairs={{0,12},{4,0},{8,4},{12,8},{1,13},{5,1},{9,5},{13,9},{2,14},{6,2},{... | collective-permute-start | bytes 1253384 | tf_op jit(solution)/shard_map/ppermute | solution.py:1210
  228.0 24.4 %collective-permute-start.67 = (bf16[800,256]{1,0:T(8,128)(2,1)S(1)}, bf16[800,256]{1,0:T(8,128)(2,1)S(1)}, u32[]{:S(2)}, u32[]{:S(2)}) collective-permute-start(bf16[800,256]{1,0:T(8,128)(2,1)S(1)} %get-tuple-element.262), channel_id=1, source_target_pairs={{0,3},{1,2},{2,1},{3,0},{4,7},{5,6},{6,5},{7,4},{8,11},{9,10},{10,... | collective-permute-start | bytes 1228808 | tf_op jit(solution)/shard_map/ppermute | solution.py:875
  228.9 23.5 %collective-permute-start.68 = (bf16[800,256]{1,0:T(8,128)(2,1)S(1)}, bf16[800,256]{1,0:T(8,128)(2,1)S(1)}, u32[]{:S(2)}, u32[]{:S(2)}) collective-permute-start(bf16[800,256]{1,0:T(8,128)(2,1)S(1)} %get-tuple-element.263), channel_id=1, source_target_pairs={{0,2},{1,3},{2,0},{3,1},{4,6},{5,7},{6,4},{7,5},{8,10},{9,11},{10,... | collective-permute-start | bytes 1228808 | tf_op jit(solution)/shard_map/ppermute | solution.py:875
  230.2 22.3 %collective-permute-start.69 = (bf16[800,256]{1,0:T(8,128)(2,1)S(1)}, bf16[800,256]{1,0:T(8,128)(2,1)S(1)}, u32[]{:S(2)}, u32[]{:S(2)}) collective-permute-start(bf16[800,256]{1,0:T(8,128)(2,1)S(1)} %get-tuple-element.264), channel_id=1, source_target_pairs={{0,1},{1,0},{2,3},{3,2},{4,5},{5,4},{6,7},{7,6},{8,9},{9,8},{10,11... | collective-permute-start | bytes 1228808 | tf_op jit(solution)/shard_map/ppermute | solution.py:875
  259.2 19.1 %collective-permute-start.76 = (bf16[272,768]{1,0:T(8,128)(2,1)S(1)}, bf16[272,768]{1,0:T(8,128)(2,1)S(1)}, u32[]{:S(2)}, u32[]{:S(2)}) collective-permute-start(bf16[272,768]{1,0:T(8,128)(2,1)S(1)} %get-tuple-element.283), channel_id=1, source_target_pairs={{0,16},{16,0},{1,17},{17,1},{2,18},{18,2},{3,19},{19,3},{4,20},{20... | collective-permute-start | bytes 1253384 | tf_op jit(solution)/shard_map/ppermute | solution.py:868
  259.6 5.8 %collective-permute-start.73 = (bf16[336,256]{1,0:T(8,128)(2,1)S(1)}, bf16[336,256]{1,0:T(8,128)(2,1)S(1)}, u32[]{:S(2)}, u32[]{:S(2)}) collective-permute-start(bf16[336,256]{1,0:T(8,128)(2,1)S(1)} %get-tuple-element.276), channel_id=1, source_target_pairs={{0,4},{4,8},{8,12},{12,0},{1,5},{5,9},{9,13},{13,1},{2,6},{6,10},{... | collective-permute-start | bytes 516104 | tf_op jit(solution)/shard_map/ppermute | solution.py:872
  259.6 14.9 %collective-permute-start.74 = (bf16[336,256]{1,0:T(8,128)(2,1)S(1)}, bf16[336,256]{1,0:T(8,128)(2,1)S(1)}, u32[]{:S(2)}, u32[]{:S(2)}) collective-permute-start(bf16[336,256]{1,0:T(8,128)(2,1)S(1)} %get-tuple-element.277), channel_id=1, source_target_pairs={{0,8},{4,12},{8,0},{12,4},{1,9},{5,13},{9,1},{13,5},{2,10},{6,14},... | collective-permute-start | bytes 516104 | tf_op jit(solution)/shard_map/ppermute | solution.py:872
  261.2 15.9 %collective-permute-start.75 = (bf16[336,256]{1,0:T(8,128)(2,1)S(1)}, bf16[336,256]{1,0:T(8,128)(2,1)S(1)}, u32[]{:S(2)}, u32[]{:S(2)}) collective-permute-start(bf16[336,256]{1,0:T(8,128)(2,1)S(1)} %get-tuple-element.278), channel_id=1, source_target_pairs={{0,12},{4,0},{8,4},{12,8},{1,13},{5,1},{9,5},{13,9},{2,14},{6,2},{... | collective-permute-start | bytes 516104 | tf_op jit(solution)/shard_map/ppermute | solution.py:872
  (44 other events, 335.1 us)
where the time goes:
time: 284 us; the launch traced here: 283 us
  Pallas kernels  111 us (39%)
  waiting for transfers between devices  85.1 us (30%)
  starting transfers between devices  79.6 us (28%)
  local copies, waits for them, and re-layouts  5.29 us (2%)
    ppermute x35, starting transfers between devices, cross(): return lax.ppermute(x, 'section', swap)  35.2 us
    ppermute x6, waiting for transfers between devices, shifted(): lax.ppermute(x, 'seq', [(i, (i + r) % seq) for i in range(seq)])  34.1 us
    pallas_call x2, Pallas kernels, call(): pl.pallas_call(functools.partial(forward_kernel, sz, layer, slots), grid_...  27.3 us
    pallas_call x2, Pallas kernels, call(): pl.pallas_call(functools.partial(backward_kernel, sz, layer, len(deps)),...  24.9 us
    ppermute x24, starting transfers between devices, over_heads(): lax.ppermute(x, 'head', [(i, i ^ d) for i in range(head_axis)])  21.6 us
    ppermute x12, waiting for transfers between devices, turn(): return lax.ppermute(x, 'seq', pairs) if r else x  21.2 us
    ppermute x24, waiting for transfers between devices, over_heads(): lax.ppermute(x, 'head', [(i, i ^ d) for i in range(head_axis)])  21.2 us
    ppermute x12, starting transfers between devices, turn(): return lax.ppermute(x, 'seq', pairs) if r else x  14.2 us
  transfers between devices with their start and end apart: 77, of which 24 were waited for; matrix products, arithmetic and copies ran while one was open for 0% of the time, Pallas kernels for 26%

commit v1 on v0

--- a/solution.py
+++ b/solution.py
@@ -654,7 +654,8 @@
         swap_o[sz.rows :, :] = pick(first, one, zero).astype(LOW)
 
 
-def sum_kernel(sz, last, sc, *refs):
+def sum_kernel(sz, last, deps, sc, *refs):
+    refs = refs[deps:]
     if last:
         parts, done, outs = refs[:-3], refs[-3], refs[-2:]
     else:
@@ -672,8 +673,9 @@
         outs[0][...] = sums
 
 
-def final_kernel(sz, sc, own, got, *refs):
-    gate_o, inner_o, out_o, conv_o, norm_o, skip_o = refs
+def final_kernel(sz, seq, sc, own, got, *refs):
+    pieces, refs = refs[:-9], refs[-9:]
+    gate_o, inner_o, out_o, conv_o, norm_o, skip_o, shared_o, taps_o, gain_o = refs
     c = sc[0]
     ch = sz.channels
     rows = own.shape[0] - PAD
@@ -695,8 +697,6 @@
             part = jnp.sum(per_head(skips, q, sz.head_width), axis=1, keepdims=True)
             skip = jnp.where(lane == which * sz.heads + q, part, skip)
     skip_o[...] = skip
-def shared_kernel(sz, seq, sc, *refs):
-    pieces, shared_o, taps_o, gain_o = refs[:-3], *refs[-3:]
     total = total_of(pieces, slice(BLOCK, None))
     shared_o[...] = total[PAD:]
     common = total[: PAD // 2] + total[PAD // 2 : PAD]
@@ -1264,10 +1264,19 @@
     lf0 = lift(0, sc_weights, bw0[0], fw0[0], bw0[3], heads1[1:])
     parts, sc_join = scatter(lf0[2], lf0[0], lf0[1], [[lf0[3], *heads0]], weights0[1:2])
 
+    def summed(sc, pieces, *done, deps=()):
+        return pl.pallas_call(
+            functools.partial(sum_kernel, sz, bool(done), len(deps)),
+            in_specs=[smem] + [anywhere] * len(deps) + [vmem] * (len(pieces) + len(done)),
+            out_shape=[shape((part + PAD, columns), LOW)] * (1 + len(done)),
+            compiler_params=options,
+        )(sc, *deps, *pieces, *done)
+
+    sums1 = summed(sc_in, weights1)
     unused, low2, unused_mixed, unused_square, sc_out = section_output(1, sc_in, parts_out, res1)
     glow0, to_other, shared_own, sc_end = section_input(
         0, sc_out, parts, base0, igrad1, fw0[5], *gains, low2, *heads1,
-        deps=weights0[2:],
+        deps=[*weights0[2:], *sums1],
     )
     got = cross(to_other)
     if spans == 1:
@@ -1283,18 +1292,10 @@
             for r in range(seq)
         ]
         shared_parts = over_seq([x.astype(LOW) for x in chunks])
-    def summed(sc, pieces, *done):
-        return pl.pallas_call(
-            functools.partial(sum_kernel, sz, bool(done)),
-            in_specs=[smem] + [vmem] * (len(pieces) + len(done)),
-            out_shape=[shape((part + PAD, columns), LOW)] * (1 + len(done)),
-            compiler_params=options,
-        )(sc, *pieces, *done)
-
-    own_sums, other_sums = summed(sc_end, weights0, *summed(sc_in, weights1))
+    own_sums, other_sums = summed(sc_end, weights0, *sums1)
     final = pl.pallas_call(
-        functools.partial(final_kernel, sz),
-        in_specs=[smem] + [vmem] * 2,
+        functools.partial(final_kernel, sz, seq),
+        in_specs=[smem] + [vmem] * (2 + seq),
         out_shape=[
             shape((part, inner_dev), F32),
             shape((part, inner_dev), F32),
@@ -1302,36 +1303,29 @@
             shape((taps, inner_dev), F32),
             shape((1, inner_dev), F32),
             shape((1, heads_dev), F32),
-        ],
-        compiler_params=options,
-    )(sc, own_sums, cross(other_sums))
-    section_out, input_grad, unused = pl.pallas_call(
-        functools.partial(home_kernel, slots),
-        in_specs=[smem] + [vmem] * (2 * slots) + [anywhere],
-        out_specs=[vmem, vmem, smem],
-        out_shape=[shape((slots, BLOCK, chunk), F32)] * 2 + [index_shape],
-        compiler_params=options,
-    )(sc, *early, *late, final[4])
-
-    shared_sum, tap_grads, gain_grads = pl.pallas_call(
-        functools.partial(shared_kernel, sz, seq),
-        in_specs=[smem] + [vmem] * seq,
-        out_shape=[
             shape((share, shared), F32),
             shape((taps, shared // (seq * head_axis)), F32),
             shape((1, width // (seq * head_axis)), F32),
         ],
         compiler_params=options,
-    )(sc, *shared_parts)
+    )(sc, own_sums, cross(other_sums), *shared_parts)
+    section_out, input_grad, unused = pl.pallas_call(
+        functools.partial(home_kernel, slots),
+        in_specs=[smem] + [vmem] * (2 * slots),
+        out_specs=[vmem, vmem, smem],
+        out_shape=[shape((slots, BLOCK, chunk), F32)] * 2 + [index_shape],
+        compiler_params=options,
+    )(sc, *early, *late)
+
     return (
         section_out[None],
         input_grad[None],
-        gain_grads,
+        final[8],
         final[0][None],
         final[1][None],
-        shared_sum[None],
+        final[6][None],
         final[3][None],
-        tap_grads[None],
+        final[7][None],
         final[5],
         final[4],
         final[2][None],

time: 284 us -> 284 us (level)
    unnamed x62 -> x64, local copies, waits for them, and re-layouts: 5.28 us -> 7.35 us
  transfers between devices with their start and end apart: 77 -> 77, of which waited for: 24 -> 23; matrix products, arithmetic and copies ran while one was open for 0% -> 0% of each run, Pallas kernels for 26% -> 27%
where the time goes in v1:
time: 284 us; the launch traced here: 283 us
  Pallas kernels  110 us (39%)
  waiting for transfers between devices  84 us (30%)
  starting transfers between devices  79.9 us (28%)
  local copies, waits for them, and re-layouts  7.36 us (3%)
    ppermute x35, starting transfers between devices, cross(): return lax.ppermute(x, 'section', swap)  35.6 us
    ppermute x6, waiting for transfers between devices, shifted(): lax.ppermute(x, 'seq', [(i, (i + r) % seq) for i in range(seq)])  32.6 us
    pallas_call x2, Pallas kernels, call(): pl.pallas_call(functools.partial(forward_kernel, sz, layer, slots), grid_...  27.3 us
    pallas_call x2, Pallas kernels, call(): pl.pallas_call(functools.partial(backward_kernel, sz, layer, len(deps)),...  24.8 us
    ppermute x24, starting transfers between devices, over_heads(): lax.ppermute(x, 'head', [(i, i ^ d) for i in range(head_axis)])  21.5 us
    ppermute x12, waiting for transfers between devices, turn(): return lax.ppermute(x, 'seq', pairs) if r else x  21.2 us
    ppermute x24, waiting for transfers between devices, over_heads(): lax.ppermute(x, 'head', [(i, i ^ d) for i in range(head_axis)])  20.9 us
    ppermute x12, starting transfers between devices, turn(): return lax.ppermute(x, 'seq', pairs) if r else x  14.2 us
  transfers between devices with their start and end apart: 77, of which 23 were waited for; matrix products, arithmetic and copies ran while one was open for 0% of the time, Pallas kernels for 27%

profile of v1, /device:TPU:9, one launch (start us, length us, event | category | flops | bytes accessed | tf_op | source)
XLA Modules:
  0.0 282.9 jit_solution(16705761574122990804)
XLA Ops:
  1.2 3.0 %shard_map.212 = (bf16[144,1024]{1,0:T(8,128)(2,1)}, bf16[144,1024]{1,0:T(8,128)(2,1)}, bf16[144,1024]{1,0:T(8,128)(2,1)}, bf16[144,1024]{1,0:T(8,128)(2,1)}, s32[4]{0:T(128)}) custom-call(s32[4]{0:T(128)} %pad_add_fusion.sc, s32[4]{0:T(128)} %order.3, bf16[4,256,1024]{2,1,0:T(8,128)(2,1)} %tokens.1, f32[1,4,8,256]{3,2,1,0:T(8,128)} %rates.1), custom_call_target="tpu_custom_call" | custom-call | tf_op jit(solution)/shard_map/pallas_call | solution.py:899
  4.3 1.3 collective-permute-start
  6.7 4.1 %shard_map.213 = (bf16[1024,256]{1,0:T(8,128)(2,1)}, bf16[1024,256]{1,0:T(8,128)(2,1)}, bf16[256,1024]{1,0:T(8,128)(2,1)}, f32[16,1024]{1,0:T(8,128)}, f32[16,10...) custom-call(s32[4]{0:T(128)} %get-tuple-element.153.sc, ...), custom_call_target="tpu_custom_call" | custom-call | tf_op jit(solution)/shard_map/pallas_call | solution.py:911
  11.9 1.7 collective-permute-start.2
  14.3 12.6 %collective-permute-start.9 = (bf16[1024,256]{1,0:T(8,128)(2,1)}, bf16[1024,256]{1,0:T(8,128)(2,1)S(1)}, u32[]{:S(2)}, u32[]{:S(2)}) collective-permute-start(bf16[1024,256]{1,0:T(8,128)(2,1)} %get-tuple-element.161), channel_id=1, source_target_pairs={{0,16},{16,0},{1,17},{17,1},{2,18},{18,2},{3,19},{19,3},{4,20},{20... | collective-permute-start | bytes 1572872 | tf_op jit(solution)/shard_map/ppermute | solution.py:868
  26.9 3.6 %collective-permute-done.1.refs_2_ = bf16[144,1024]{1,0:T(8,128)(2,1)} collective-permute-done((bf16[144,1024]{1,0:T(8,128)(2,1)}, bf16[144,1024]{1,0:T(8,128)(2,1)}, u32[]{:S(2)}, u32[]{:S(2)}) %collective-permute-start.1) | collective-permute-done | bytes 294944 | tf_op jit(solution)/shard_map/ppermute | solution.py:872
  30.6 1.5 collective-permute-start.10
  37.2 14.3 %shard_map.214 = (bf16[1024,1024]{1,0:T(8,128)(2,1)}, f32[1024,256]{1,0:T(8,128)}, bf16[1024,512]{1,0:T(8,128)(2,1)}, f32[1024,256]{1,0:T(8,128)}, bf16[4,256,12...) custom-call(s32[4]{0:T(128)S(1)} %copy-done.22, ...), custom_call_target="tpu_custom_call" | custom-call | flops 12884901888 | bytes 16000000 | tf_op jit(solution)/shard_map/pallas_call | solution.py:962
  51.5 1.4 shard_map.215
  53.0 1.6 collective-permute-start.14
  54.6 2.3 collective-permute-done.14.refs_0_
  58.1 2.2 collective-permute-start.15
  60.8 2.3 collective-permute-start.25
  63.1 1.5 collective-permute-start.26
  64.6 5.2 %shard_map.217 = (bf16[768,1024]{1,0:T(8,128)(2,1)}, bf16[768,1024]{1,0:T(8,128)(2,1)}, bf16[1024,256]{1,0:T(8,128)(2,1)S(1)}, bf16[1024,256]{1,0:T(8,128)(2,1)S(1)}) custom-call(s32[4]{0:T(128)S(1)} %get-tuple-element.175.sc, bf16[1,1024,512]{2,1,0:T(8,128)(2,1)} %refs_19_.1, bf16[1,1024,512]{2,1,0:T(8,128)(2,1)} %refs_20_.1, ...), custom_call_target="tpu_custom_call" | custom-call | flops 1000000000 | bytes 8000000 | tf_op jit(solution)/shard_map/pallas_call | solution.py:1232
  70.1 3.2 %collective-permute-done.16.refs_2_ = bf16[528,256]{1,0:T(8,128)(2,1)S(1)} collective-permute-done((bf16[528,256]{1,0:T(8,128)(2,1)S(1)}, bf16[528,256]{1,0:T(8,128)(2,1)S(1)}, u32[]{:S(2)}, u32[]{:S(2)}) %collective-permute-start.16) | collective-permute-done | bytes 270368 | tf_op jit(solution)/shard_map/ppermute | solution.py:875
  74.8 1.5 collective-permute-start.18
  78.6 5.1 %collective-permute-done.18.refs_1_ = bf16[512,256]{1,0:T(8,128)(2,1)S(1)} collective-permute-done((bf16[512,256]{1,0:T(8,128)(2,1)S(1)}, bf16[512,256]{1,0:T(8,128)(2,1)S(1)}, u32[]{:S(2)}, u32[]{:S(2)}) %collective-permute-start.18) | collective-permute-done | bytes 262176 | tf_op jit(solution)/shard_map/ppermute | solution.py:875
  83.7 1.3 collective-permute-start.22
  85.1 4.6 %collective-permute-done.19.refs_2_ = bf16[512,256]{1,0:T(8,128)(2,1)S(1)} collective-permute-done((bf16[512,256]{1,0:T(8,128)(2,1)S(1)}, bf16[512,256]{1,0:T(8,128)(2,1)S(1)}, u32[]{:S(2)}, u32[]{:S(2)}) %collective-permute-start.19) | collective-permute-done | bytes 262176 | tf_op jit(solution)/shard_map/ppermute | solution.py:875
  91.7 13.0 %shard_map.219 = (bf16[1024,1024]{1,0:T(8,128)(2,1)}, f32[1024,256]{1,0:T(8,128)}, bf16[1024,512]{1,0:T(8,128)(2,1)}, f32[1024,256]{1,0:T(8,128)}, bf16[4,256,12...) custom-call(s32[4]{0:T(128)S(1)} %copy-done.22, ...), custom_call_target="tpu_custom_call" | custom-call | flops 12884901888 | bytes 16000000 | tf_op jit(solution)/shard_map/pallas_call | solution.py:962
  105.8 2.4 shard_map.220
  108.7 2.2 collective-permute-done.31
  111.0 1.2 collective-permute-start.32
  114.8 1.5 collective-permute-start.35
  117.5 1.2 copy-done.25
  118.7 12.0 %shard_map.222 = (bf16[1024,768]{1,0:T(8,128)(2,1)}, bf16[1024,256]{1,0:T(8,128)(2,1)S(1)}, bf16[16,768]{1,0:T(8,128)(2,1)S(1)}, f32[8,512]{1,0:T(8,128)S(1)}, f...) custom-call(s32[4]{0:T(128)S(1)} %get-tuple-element.189.sc, ...), custom_call_target="tpu_custom_call" | custom-call | flops 17179869184 | bytes 16000000 | tf_op jit(solution)/shard_map/pallas_call | solution.py:1038
  130.8 5.1 %shard_map.223 = (bf16[4,528,256]{2,1,0:T(8,128)(2,1)S(1)}, bf16[528,256]{1,0:T(8,128)(2,1)S(1)}, bf16[528,256]{1,0:T(8,128)(2,1)S(1)}, bf16[528,256]{1,0:T(8,12...) custom-call(s32[4]{0:T(128)S(1)} %get-tuple-element.195.sc, ...), custom_call_target="tpu_custom_call" | custom-call | flops 2147483648 | bytes 8000000 | tf_op jit(solution)/shard_map/pallas_call | solution.py:1115
  135.8 1.9 collective-permute-start.38
  138.3 5.6 %shard_map.224 = (s32[4]{0:T(128)S(1)}, bf16[272,768]{1,0:T(8,128)(2,1)S(1)}, bf16[272,768]{1,0:T(8,128)(2,1)S(1)}, bf16[272,768]{1,0:T(8,128)(2,1)S(1)}, bf16[2...) custom-call(s32[4]{0:T(128)S(1)} %get-tuple-element.202.sc, ...), custom_call_target="tpu_custom_call" | custom-call | flops 8589934592 | bytes 12000000 | tf_op jit(solution)/shard_map/pallas_call | solution.py:1196
  143.9 2.4 collective-permute-start.45
  146.3 1.3 shard_map.225
  147.6 1.5 collective-permute-start.42
  150.3 14.1 %collective-permute-done.45.refs_10_.refs_2_ = bf16[272,768]{1,0:T(8,128)(2,1)S(1)} collective-permute-done((bf16[272,768]{1,0:T(8,128)(2,1)S(1)}, bf16[272,768]{1,0:T(8,128)(2,1)S(1)}, u32[]{:S(2)}, u32[]{:S(2)}) %collective-permute-start.45) | collective-permute-done | bytes 417824 | tf_op jit(solution)/shard_map/ppermute | solution.py:1210
  164.4 2.2 shard_map.226
  167.4 1.4 collective-permute-start.50
  170.3 1.6 collective-permute-start.46
  171.9 3.8 %collective-permute-done.50.refs_1_ = bf16[528,256]{1,0:T(8,128)(2,1)S(1)} collective-permute-done((bf16[528,256]{1,0:T(8,128)(2,1)S(1)}, bf16[528,256]{1,0:T(8,128)(2,1)S(1)}, u32[]{:S(2)}, u32[]{:S(2)}) %collective-permute-start.50) | collective-permute-done | bytes 270368 | tf_op jit(solution)/shard_map/ppermute | solution.py:875
  175.7 2.7 collective-permute-start.53
  178.4 4.1 %collective-permute-done.51.refs_2_ = bf16[528,256]{1,0:T(8,128)(2,1)S(1)} collective-permute-done((bf16[528,256]{1,0:T(8,128)(2,1)S(1)}, bf16[528,256]{1,0:T(8,128)(2,1)S(1)}, u32[]{:S(2)}, u32[]{:S(2)}) %collective-permute-start.51) | collective-permute-done | bytes 270368 | tf_op jit(solution)/shard_map/ppermute | solution.py:875
  184.6 2.2 collective-permute-start.58
  186.9 1.4 collective-permute-start.59
  188.3 4.2 %collective-permute-start.48 = (bf16[256,256]{1,0:T(8,128)(2,1)S(1)}, bf16[256,256]{1,0:T(8,128)(2,1)S(1)}, u32[]{:S(2)}, u32[]{:S(2)}) collective-permute-start(bf16[256,256]{1,0:T(8,128)(2,1)S(1)} %get-tuple-element.226), channel_id=1, source_target_pairs={{0,8},{4,12},{8,0},{12,4},{1,9},{5,13},{9,1},{13,5},{2,10},{6,14},... | collective-permute-start | bytes 393224 | tf_op jit(solution)/shard_map/ppermute | solution.py:872
  192.5 12.8 %shard_map.229 = (bf16[1024,768]{1,0:T(8,128)(2,1)}, bf16[1024,256]{1,0:T(8,128)(2,1)S(1)}, bf16[16,768]{1,0:T(8,128)(2,1)S(1)}, f32[8,512]{1,0:T(8,128)S(1)}, f...) custom-call(s32[4]{0:T(128)S(1)} %copy-done.22, ...), custom_call_target="tpu_custom_call" | custom-call | flops 17179869184 | bytes 16000000 | tf_op jit(solution)/shard_map/pallas_call | solution.py:1038
  206.6 1.9 collective-permute-done.48.refs_1_.refs_2_
  208.6 5.6 %shard_map.230 = (s32[4]{0:T(128)S(1)}, bf16[272,768]{1,0:T(8,128)(2,1)S(1)}, bf16[272,768]{1,0:T(8,128)(2,1)S(1)}, bf16[272,768]{1,0:T(8,128)(2,1)S(1)}, bf16[2...) custom-call(s32[4]{0:T(128)S(1)} %get-tuple-element.237.sc, ...), custom_call_target="tpu_custom_call" | custom-call | flops 8589934592 | bytes 12000000 | tf_op jit(solution)/shard_map/pallas_call | solution.py:1196
  214.2 5.1 %shard_map.231 = (bf16[4,528,256]{2,1,0:T(8,128)(2,1)S(1)}, bf16[528,256]{1,0:T(8,128)(2,1)S(1)}, bf16[528,256]{1,0:T(8,128)(2,1)S(1)}, bf16[528,256]{1,0:T(8,12...) custom-call(s32[4]{0:T(128)S(1)} %get-tuple-element.244.sc, ...), custom_call_target="tpu_custom_call" | custom-call | flops 2147483648 | bytes 8000000 | tf_op jit(solution)/shard_map/pallas_call | solution.py:1115
  220.3 2.0 collective-permute-start.62
  223.5 1.9 collective-permute-start.70
  225.4 1.7 collective-permute-start.71
  227.2 1.8 shard_map.232
  230.8 1.2 collective-permute-start.68
  234.1 1.8 shard_map.228
  235.9 16.1 %collective-permute-done.70.refs_14_.refs_2_ = bf16[272,768]{1,0:T(8,128)(2,1)S(1)} collective-permute-done((bf16[272,768]{1,0:T(8,128)(2,1)S(1)}, bf16[272,768]{1,0:T(8,128)(2,1)S(1)}, u32[]{:S(2)}, u32[]{:S(2)}) %collective-permute-start.70) | collective-permute-done | bytes 417824 | tf_op jit(solution)/shard_map/ppermute | solution.py:1210
  252.0 2.3 collective-permute-done.71.refs_15_.refs_3_
  255.1 2.1 shard_map.234
  257.7 1.4 collective-permute-done.72.zero_other.one_other
  261.6 1.5 collective-permute-start.74
  263.1 1.5 collective-permute-start.75
  264.5 2.8 %collective-permute-done.73.refs_5_.refs_1_ = bf16[336,256]{1,0:T(8,128)(2,1)S(1)} collective-permute-done((bf16[336,256]{1,0:T(8,128)(2,1)S(1)}, bf16[336,256]{1,0:T(8,128)(2,1)S(1)}, u32[]{:S(2)}, u32[]{:S(2)}) %collective-permute-start.73) | collective-permute-done | bytes 172064 | tf_op jit(solution)/shard_map/ppermute | solution.py:872
  267.4 9.1 %collective-permute-done.74.refs_6_.refs_2_ = bf16[336,256]{1,0:T(8,128)(2,1)S(1)} collective-permute-done((bf16[336,256]{1,0:T(8,128)(2,1)S(1)}, bf16[336,256]{1,0:T(8,128)(2,1)S(1)}, u32[]{:S(2)}, u32[]{:S(2)}) %collective-permute-start.74) | collective-permute-done | bytes 172064 | tf_op jit(solution)/shard_map/ppermute | solution.py:872
  276.5 2.5 collective-permute-done.75.refs_7_.refs_3_
  279.0 2.0 shard_map.236
  281.0 1.9 shard_map.238
  (185 shorter events, 38.9 us)
Async XLA Ops:
  4.3 10.0 %collective-permute-start = (bf16[144,1024]{1,0:T(8,128)(2,1)}, bf16[144,1024]{1,0:T(8,128)(2,1)}, u32[]{:S(2)}, u32[]{:S(2)}) collective-permute-start(bf16[144,1024]{1,0:T(8,128)(2,1)} %get-tuple-element.155), channel_id=1, source_target_pairs={{0,4},{4,8},{8,12},{12,0},{1,5},{5,9},{9,13},{13,1},{2,6},{6,10},{... | collective-permute-start | bytes 884744 | tf_op jit(solution)/shard_map/ppermute | solution.py:872
  5.6 25.0 %collective-permute-start.1 = (bf16[144,1024]{1,0:T(8,128)(2,1)}, bf16[144,1024]{1,0:T(8,128)(2,1)}, u32[]{:S(2)}, u32[]{:S(2)}) collective-permute-start(bf16[144,1024]{1,0:T(8,128)(2,1)} %get-tuple-element.156), channel_id=1, source_target_pairs={{0,8},{4,12},{8,0},{12,4},{1,9},{5,13},{9,1},{13,5},{2,10},{6,14},... | collective-permute-start | bytes 884744 | tf_op jit(solution)/shard_map/ppermute | solution.py:872
  10.8 23.0 %collective-permute-start.8 = (bf16[1024,256]{1,0:T(8,128)(2,1)}, bf16[1024,256]{1,0:T(8,128)(2,1)S(1)}, u32[]{:S(2)}, u32[]{:S(2)}) collective-permute-start(bf16[1024,256]{1,0:T(8,128)(2,1)} %get-tuple-element.160), channel_id=1, source_target_pairs={{0,16},{16,0},{1,17},{17,1},{2,18},{18,2},{3,19},{19,3},{4,20},{20... | collective-permute-start | bytes 1572872 | tf_op jit(solution)/shard_map/ppermute | solution.py:868
  11.9 21.4 %collective-permute-start.2 = (bf16[144,1024]{1,0:T(8,128)(2,1)}, bf16[144,1024]{1,0:T(8,128)(2,1)S(1)}, u32[]{:S(2)}, u32[]{:S(2)}) collective-permute-start(bf16[144,1024]{1,0:T(8,128)(2,1)} %get-tuple-element.157), channel_id=1, source_target_pairs={{0,12},{4,0},{8,4},{12,8},{1,13},{5,1},{9,5},{13,9},{2,14},{6,2},{... | collective-permute-start | bytes 884744 | tf_op jit(solution)/shard_map/ppermute | solution.py:872
  13.7 20.1 %collective-permute-start.3 = (bf16[144,1024]{1,0:T(8,128)(2,1)S(1)}, bf16[144,1024]{1,0:T(8,128)(2,1)S(1)}, u32[]{:S(2)}, u32[]{:S(2)}) collective-permute-start(bf16[144,1024]{1,0:T(8,128)(2,1)S(1)} %copy-done.23), channel_id=1, source_target_pairs={{0,16},{16,0},{1,17},{17,1},{2,18},{18,2},{3,19},{19,3},{4,20},{20... | collective-permute-start | bytes 884744 | tf_op jit(solution)/shard_map/ppermute | solution.py:868
  14.3 20.0 %collective-permute-start.9 = (bf16[1024,256]{1,0:T(8,128)(2,1)}, bf16[1024,256]{1,0:T(8,128)(2,1)S(1)}, u32[]{:S(2)}, u32[]{:S(2)}) collective-permute-start(bf16[1024,256]{1,0:T(8,128)(2,1)} %get-tuple-element.161), channel_id=1, source_target_pairs={{0,16},{16,0},{1,17},{17,1},{2,18},{18,2},{3,19},{19,3},{4,20},{20... | collective-permute-start | bytes 1572872 | tf_op jit(solution)/shard_map/ppermute | solution.py:868
  34.3 17.2 %collective-permute-start.11 = (bf16[256,1024]{1,0:T(8,128)(2,1)}, bf16[256,1024]{1,0:T(8,128)(2,1)S(1)}, u32[]{:S(2)}, u32[]{:S(2)}) collective-permute-start(bf16[256,1024]{1,0:T(8,128)(2,1)} %get-tuple-element.165), channel_id=1, source_target_pairs={{0,16},{16,0},{1,17},{17,1},{2,18},{18,2},{3,19},{19,3},{4,20},{20... | collective-permute-start | bytes 1572872 | tf_op jit(solution)/shard_map/ppermute | solution.py:868
  34.4 17.0 %collective-permute-start.12 = (bf16[128,1024]{1,0:T(8,128)(2,1)}, bf16[128,1024]{1,0:T(8,128)(2,1)S(1)}, u32[]{:S(2)}, u32[]{:S(2)}) collective-permute-start(bf16[128,1024]{1,0:T(8,128)(2,1)} %get-tuple-element.166), channel_id=1, source_target_pairs={{0,4},{4,8},{8,12},{12,0},{1,5},{5,9},{9,13},{13,1},{2,6},{6,10},{... | collective-permute-start | bytes 786440 | tf_op jit(solution)/shard_map/ppermute | solution.py:872
  35.2 16.3 %collective-permute-start.13 = (bf16[128,1024]{1,0:T(8,128)(2,1)}, bf16[128,1024]{1,0:T(8,128)(2,1)S(1)}, u32[]{:S(2)}, u32[]{:S(2)}) collective-permute-start(bf16[128,1024]{1,0:T(8,128)(2,1)} %get-tuple-element.167), channel_id=1, source_target_pairs={{0,12},{4,0},{8,4},{12,8},{1,13},{5,1},{9,5},{13,9},{2,14},{6,2},{... | collective-permute-start | bytes 786440 | tf_op jit(solution)/shard_map/ppermute | solution.py:872
  58.1 11.7 %collective-permute-start.15 = (bf16[528,256]{1,0:T(8,128)(2,1)S(1)}, bf16[528,256]{1,0:T(8,128)(2,1)S(1)}, u32[]{:S(2)}, u32[]{:S(2)}) collective-permute-start(bf16[528,256]{1,0:T(8,128)(2,1)S(1)} %get-tuple-element.171), channel_id=1, source_target_pairs={{0,3},{1,2},{2,1},{3,0},{4,7},{5,6},{6,5},{7,4},{8,11},{9,10},{10,... | collective-permute-start | bytes 811016 | tf_op jit(solution)/shard_map/ppermute | solution.py:875
  60.3 12.9 %collective-permute-start.16 = (bf16[528,256]{1,0:T(8,128)(2,1)S(1)}, bf16[528,256]{1,0:T(8,128)(2,1)S(1)}, u32[]{:S(2)}, u32[]{:S(2)}) collective-permute-start(bf16[528,256]{1,0:T(8,128)(2,1)S(1)} %get-tuple-element.172), channel_id=1, source_target_pairs={{0,2},{1,3},{2,0},{3,1},{4,6},{5,7},{6,4},{7,5},{8,10},{9,11},{10,... | collective-permute-start | bytes 811016 | tf_op jit(solution)/shard_map/ppermute | solution.py:875
  60.6 13.2 %collective-permute-start.17 = (bf16[528,256]{1,0:T(8,128)(2,1)S(1)}, bf16[528,256]{1,0:T(8,128)(2,1)S(1)}, u32[]{:S(2)}, u32[]{:S(2)}) collective-permute-start(bf16[528,256]{1,0:T(8,128)(2,1)S(1)} %get-tuple-element.173), channel_id=1, source_target_pairs={{0,1},{1,0},{2,3},{3,2},{4,5},{5,4},{6,7},{7,6},{8,9},{9,8},{10,11... | collective-permute-start | bytes 811016 | tf_op jit(solution)/shard_map/ppermute | solution.py:875
  60.8 15.6 %collective-permute-start.25 = (bf16[128,1024]{1,0:T(8,128)(2,1)S(1)}, bf16[128,1024]{1,0:T(8,128)(2,1)S(1)}, u32[]{:S(2)}, u32[]{:S(2)}) collective-permute-start(bf16[128,1024]{1,0:T(8,128)(2,1)S(1)} %copy-done.27), channel_id=1, source_target_pairs={{0,8},{4,12},{8,0},{12,4},{1,9},{5,13},{9,1},{13,5},{2,10},{6,14},... | collective-permute-start | bytes 786440 | tf_op jit(solution)/shard_map/ppermute | solution.py:872
  63.1 14.2 %collective-permute-start.26 = (bf16[128,1024]{1,0:T(8,128)(2,1)S(1)}, bf16[128,1024]{1,0:T(8,128)(2,1)S(1)}, u32[]{:S(2)}, u32[]{:S(2)}) collective-permute-start(bf16[128,1024]{1,0:T(8,128)(2,1)S(1)} %copy-done.24), channel_id=1, source_target_pairs={{0,16},{16,0},{1,17},{17,1},{2,18},{18,2},{3,19},{19,3},{4,20},{20... | collective-permute-start | bytes 786440 | tf_op jit(solution)/shard_map/ppermute | solution.py:868
  69.8 7.8 %collective-permute-start.27 = (bf16[128,1024]{1,0:T(8,128)(2,1)S(1)}, bf16[128,1024]{1,0:T(8,128)(2,1)S(1)}, u32[]{:S(2)}, u32[]{:S(2)}) collective-permute-start(bf16[128,1024]{1,0:T(8,128)(2,1)S(1)} %collective-permute-done.12.refs_2_.refs_9_), channel_id=1, source_target_pairs={{0,16},{16,0},{1,17},{17,1},{2,18},{18,2},{3,19},{19,3},{4,20},{20... | collective-permute-start | bytes 786440 | tf_op jit(solution)/shard_map/ppermute | solution.py:868
  73.3 5.3 %collective-permute-start.29 = (bf16[128,1024]{1,0:T(8,128)(2,1)S(1)}, bf16[128,1024]{1,0:T(8,128)(2,1)S(1)}, u32[]{:S(2)}, u32[]{:S(2)}) collective-permute-start(bf16[128,1024]{1,0:T(8,128)(2,1)S(1)} %collective-permute-done.13.refs_3_.refs_11_), channel_id=1, source_target_pairs={{0,16},{16,0},{1,17},{17,1},{2,18},{18,2},{3,19},{19,3},{4,20},{20... | collective-permute-start | bytes 786440 | tf_op jit(solution)/shard_map/ppermute | solution.py:868
  74.8 8.9 %collective-permute-start.18 = (bf16[512,256]{1,0:T(8,128)(2,1)S(1)}, bf16[512,256]{1,0:T(8,128)(2,1)S(1)}, u32[]{:S(2)}, u32[]{:S(2)}) collective-permute-start(bf16[512,256]{1,0:T(8,128)(2,1)S(1)} %get-tuple-element.180.refs_0_.zero_own), channel_id=1, source_target_pairs={{0,3},{1,2},{2,1},{3,0},{4,7},{5,6},{6,5},{7,4},{8,11},{9,10},{10,... | collective-permute-start | bytes 786440 | tf_op jit(solution)/shard_map/ppermute | solution.py:875
  76.4 13.3 %collective-permute-start.19 = (bf16[512,256]{1,0:T(8,128)(2,1)S(1)}, bf16[512,256]{1,0:T(8,128)(2,1)S(1)}, u32[]{:S(2)}, u32[]{:S(2)}) collective-permute-start(bf16[512,256]{1,0:T(8,128)(2,1)S(1)} %get-tuple-element.180.refs_0_.zero_own), channel_id=1, source_target_pairs={{0,2},{1,3},{2,0},{3,1},{4,6},{5,7},{6,4},{7,5},{8,10},{9,11},{10,... | collective-permute-start | bytes 786440 | tf_op jit(solution)/shard_map/ppermute | solution.py:875
  77.3 12.8 %collective-permute-start.20 = (bf16[512,256]{1,0:T(8,128)(2,1)S(1)}, bf16[512,256]{1,0:T(8,128)(2,1)S(1)}, u32[]{:S(2)}, u32[]{:S(2)}) collective-permute-start(bf16[512,256]{1,0:T(8,128)(2,1)S(1)} %get-tuple-element.180.refs_0_.zero_own), channel_id=1, source_target_pairs={{0,1},{1,0},{2,3},{3,2},{4,5},{5,4},{6,7},{7,6},{8,9},{9,8},{10,11... | collective-permute-start | bytes 786440 | tf_op jit(solution)/shard_map/ppermute | solution.py:875
  77.6 12.7 %collective-permute-start.28 = (bf16[128,1024]{1,0:T(8,128)(2,1)S(1)}, bf16[128,1024]{1,0:T(8,128)(2,1)S(1)}, u32[]{:S(2)}, u32[]{:S(2)}) collective-permute-start(bf16[128,1024]{1,0:T(8,128)(2,1)S(1)} %collective-permute-done.25.refs_10_), channel_id=1, source_target_pairs={{0,16},{16,0},{1,17},{17,1},{2,18},{18,2},{3,19},{19,3},{4,20},{20... | collective-permute-start | bytes 786440 | tf_op jit(solution)/shard_map/ppermute | solution.py:868
  78.5 11.7 %collective-permute-start.21 = (bf16[512,256]{1,0:T(8,128)(2,1)S(1)}, bf16[512,256]{1,0:T(8,128)(2,1)S(1)}, u32[]{:S(2)}, u32[]{:S(2)}) collective-permute-start(bf16[512,256]{1,0:T(8,128)(2,1)S(1)} %get-tuple-element.180.refs_0_.zero_own), channel_id=1, source_target_pairs={{0,16},{16,0},{1,17},{17,1},{2,18},{18,2},{3,19},{19,3},{4,20},{20... | collective-permute-start | bytes 786440 | tf_op jit(solution)/shard_map/ppermute | solution.py:868
  83.7 6.5 %collective-permute-start.22 = (bf16[512,256]{1,0:T(8,128)(2,1)S(1)}, bf16[512,256]{1,0:T(8,128)(2,1)S(1)}, u32[]{:S(2)}, u32[]{:S(2)}) collective-permute-start(bf16[512,256]{1,0:T(8,128)(2,1)S(1)} %collective-permute-done.18.refs_1_), channel_id=1, source_target_pairs={{0,16},{16,0},{1,17},{17,1},{2,18},{18,2},{3,19},{19,3},{4,20},{20... | collective-permute-start | bytes 786440 | tf_op jit(solution)/shard_map/ppermute | solution.py:868
  108.2 5.4 %collective-permute-start.30 = (bf16[4,528,256]{2,1,0:T(8,128)(2,1)S(1)}, bf16[4,528,256]{2,1,0:T(8,128)(2,1)S(1)}, u32[]{:S(2)}, u32[]{:S(2)}) collective-permute-start(bf16[4,528,256]{2,1,0:T(8,128)(2,1)S(1)} %get-tuple-element.188), channel_id=1, source_target_pairs={{0,16},{16,0},{1,17},{17,1},{2,18},{18,2},{3,19},{19,3},{4,20},{20... | collective-permute-start | bytes 3244040 | tf_op jit(solution)/shard_map/ppermute | solution.py:868
  111.0 6.3 %collective-permute-start.32 = (f32[2,1024]{1,0:T(2,128)S(1)}, f32[2,1024]{1,0:T(2,128)S(1)}, u32[]{:S(2)}, u32[]{:S(2)}) collective-permute-start(f32[2,1024]{1,0:T(2,128)S(1)} %add.3.refs_1_), channel_id=1, source_target_pairs={{0,1},{1,0},{2,3},{3,2},{4,5},{5,4},{6,7},{7,6},{8,9},{9,8},{10,11... | collective-permute-start | bytes 24584 | tf_op jit(solution)/shard_map/ppermute | solution.py:875
  112.2 5.3 %collective-permute-start.33 = (f32[2,1024]{1,0:T(2,128)S(1)}, f32[2,1024]{1,0:T(2,128)S(1)}, u32[]{:S(2)}, u32[]{:S(2)}) collective-permute-start(f32[2,1024]{1,0:T(2,128)S(1)} %add.3.refs_1_), channel_id=1, source_target_pairs={{0,2},{1,3},{2,0},{3,1},{4,6},{5,7},{6,4},{7,5},{8,10},{9,11},{10,... | collective-permute-start | bytes 24584 | tf_op jit(solution)/shard_map/ppermute | solution.py:875
  112.7 4.8 %collective-permute-start.34 = (f32[2,1024]{1,0:T(2,128)S(1)}, f32[2,1024]{1,0:T(2,128)S(1)}, u32[]{:S(2)}, u32[]{:S(2)}) collective-permute-start(f32[2,1024]{1,0:T(2,128)S(1)} %add.3.refs_1_), channel_id=1, source_target_pairs={{0,3},{1,2},{2,1},{3,0},{4,7},{5,6},{6,5},{7,4},{8,11},{9,10},{10,... | collective-permute-start | bytes 24584 | tf_op jit(solution)/shard_map/ppermute | solution.py:875
  114.8 16.0 %collective-permute-start.35 = (bf16[528,256]{1,0:T(8,128)(2,1)S(1)}, bf16[528,256]{1,0:T(8,128)(2,1)S(1)}, u32[]{:S(2)}, u32[]{:S(2)}) collective-permute-start(bf16[528,256]{1,0:T(8,128)(2,1)S(1)} %get-tuple-element.199), channel_id=1, source_target_pairs={{0,3},{1,2},{2,1},{3,0},{4,7},{5,6},{6,5},{7,4},{8,11},{9,10},{10,... | collective-permute-start | bytes 811016 | tf_op jit(solution)/shard_map/ppermute | solution.py:875
  116.3 14.5 %collective-permute-start.36 = (bf16[528,256]{1,0:T(8,128)(2,1)S(1)}, bf16[528,256]{1,0:T(8,128)(2,1)S(1)}, u32[]{:S(2)}, u32[]{:S(2)}) collective-permute-start(bf16[528,256]{1,0:T(8,128)(2,1)S(1)} %get-tuple-element.200), channel_id=1, source_target_pairs={{0,2},{1,3},{2,0},{3,1},{4,6},{5,7},{6,4},{7,5},{8,10},{9,11},{10,... | collective-permute-start | bytes 811016 | tf_op jit(solution)/shard_map/ppermute | solution.py:875
  117.2 13.5 %collective-permute-start.37 = (bf16[528,256]{1,0:T(8,128)(2,1)S(1)}, bf16[528,256]{1,0:T(8,128)(2,1)S(1)}, u32[]{:S(2)}, u32[]{:S(2)}) collective-permute-start(bf16[528,256]{1,0:T(8,128)(2,1)S(1)} %get-tuple-element.201), channel_id=1, source_target_pairs={{0,1},{1,0},{2,3},{3,2},{4,5},{5,4},{6,7},{7,6},{8,9},{9,8},{10,11... | collective-permute-start | bytes 811016 | tf_op jit(solution)/shard_map/ppermute | solution.py:875
  135.8 10.4 %collective-permute-start.38 = (bf16[528,256]{1,0:T(8,128)(2,1)S(1)}, bf16[528,256]{1,0:T(8,128)(2,1)S(1)}, u32[]{:S(2)}, u32[]{:S(2)}) collective-permute-start(bf16[528,256]{1,0:T(8,128)(2,1)S(1)} %get-tuple-element.208), channel_id=1, source_target_pairs={{0,16},{16,0},{1,17},{17,1},{2,18},{18,2},{3,19},{19,3},{4,20},{20... | collective-permute-start | bytes 811016 | tf_op jit(solution)/shard_map/ppermute | solution.py:868
  137.7 8.5 %collective-permute-start.39 = (bf16[528,256]{1,0:T(8,128)(2,1)S(1)}, bf16[528,256]{1,0:T(8,128)(2,1)S(1)}, u32[]{:S(2)}, u32[]{:S(2)}) collective-permute-start(bf16[528,256]{1,0:T(8,128)(2,1)S(1)} %get-tuple-element.209), channel_id=1, source_target_pairs={{0,16},{16,0},{1,17},{17,1},{2,18},{18,2},{3,19},{19,3},{4,20},{20... | collective-permute-start | bytes 811016 | tf_op jit(solution)/shard_map/ppermute | solution.py:868
  137.8 8.5 %collective-permute-start.40 = (bf16[528,256]{1,0:T(8,128)(2,1)S(1)}, bf16[528,256]{1,0:T(8,128)(2,1)S(1)}, u32[]{:S(2)}, u32[]{:S(2)}) collective-permute-start(bf16[528,256]{1,0:T(8,128)(2,1)S(1)} %get-tuple-element.210), channel_id=1, source_target_pairs={{0,16},{16,0},{1,17},{17,1},{2,18},{18,2},{3,19},{19,3},{4,20},{20... | collective-permute-start | bytes 811016 | tf_op jit(solution)/shard_map/ppermute | solution.py:868
  138.3 8.0 %collective-permute-start.41 = (bf16[528,256]{1,0:T(8,128)(2,1)S(1)}, bf16[528,256]{1,0:T(8,128)(2,1)S(1)}, u32[]{:S(2)}, u32[]{:S(2)}) collective-permute-start(bf16[528,256]{1,0:T(8,128)(2,1)S(1)} %get-tuple-element.211), channel_id=1, source_target_pairs={{0,16},{16,0},{1,17},{17,1},{2,18},{18,2},{3,19},{19,3},{4,20},{20... | collective-permute-start | bytes 811016 | tf_op jit(solution)/shard_map/ppermute | solution.py:868
  143.9 20.5 %collective-permute-start.45 = (bf16[272,768]{1,0:T(8,128)(2,1)S(1)}, bf16[272,768]{1,0:T(8,128)(2,1)S(1)}, u32[]{:S(2)}, u32[]{:S(2)}) collective-permute-start(bf16[272,768]{1,0:T(8,128)(2,1)S(1)} %get-tuple-element.221), channel_id=1, source_target_pairs={{0,8},{4,12},{8,0},{12,4},{1,9},{5,13},{9,1},{13,5},{2,10},{6,14},... | collective-permute-start | bytes 1253384 | tf_op jit(solution)/shard_map/ppermute | solution.py:1210
  147.6 16.8 %collective-permute-start.42 = (bf16[528,256]{1,0:T(8,128)(2,1)S(1)}, bf16[528,256]{1,0:T(8,128)(2,1)S(1)}, u32[]{:S(2)}, u32[]{:S(2)}) collective-permute-start(bf16[528,256]{1,0:T(8,128)(2,1)S(1)} %get-tuple-element.214), channel_id=1, source_target_pairs={{0,3},{1,2},{2,1},{3,0},{4,7},{5,6},{6,5},{7,4},{8,11},{9,10},{10,... | collective-permute-start | bytes 811016 | tf_op jit(solution)/shard_map/ppermute | solution.py:875
  149.1 15.3 %collective-permute-start.43 = (bf16[528,256]{1,0:T(8,128)(2,1)S(1)}, bf16[528,256]{1,0:T(8,128)(2,1)S(1)}, u32[]{:S(2)}, u32[]{:S(2)}) collective-permute-start(bf16[528,256]{1,0:T(8,128)(2,1)S(1)} %get-tuple-element.215), channel_id=1, source_target_pairs={{0,2},{1,3},{2,0},{3,1},{4,6},{5,7},{6,4},{7,5},{8,10},{9,11},{10,... | collective-permute-start | bytes 811016 | tf_op jit(solution)/shard_map/ppermute | solution.py:875
  150.0 14.4 %collective-permute-start.44 = (bf16[528,256]{1,0:T(8,128)(2,1)S(1)}, bf16[528,256]{1,0:T(8,128)(2,1)S(1)}, u32[]{:S(2)}, u32[]{:S(2)}) collective-permute-start(bf16[528,256]{1,0:T(8,128)(2,1)S(1)} %get-tuple-element.216), channel_id=1, source_target_pairs={{0,1},{1,0},{2,3},{3,2},{4,5},{5,4},{6,7},{7,6},{8,9},{9,8},{10,11... | collective-permute-start | bytes 811016 | tf_op jit(solution)/shard_map/ppermute | solution.py:875
  167.4 8.3 %collective-permute-start.50 = (bf16[528,256]{1,0:T(8,128)(2,1)S(1)}, bf16[528,256]{1,0:T(8,128)(2,1)S(1)}, u32[]{:S(2)}, u32[]{:S(2)}) collective-permute-start(bf16[528,256]{1,0:T(8,128)(2,1)S(1)} %get-tuple-element.223.one_own.refs_0_), channel_id=1, source_target_pairs={{0,3},{1,2},{2,1},{3,0},{4,7},{5,6},{6,5},{7,4},{8,11},{9,10},{10,... | collective-permute-start | bytes 811016 | tf_op jit(solution)/shard_map/ppermute | solution.py:875
  168.9 13.7 %collective-permute-start.51 = (bf16[528,256]{1,0:T(8,128)(2,1)S(1)}, bf16[528,256]{1,0:T(8,128)(2,1)S(1)}, u32[]{:S(2)}, u32[]{:S(2)}) collective-permute-start(bf16[528,256]{1,0:T(8,128)(2,1)S(1)} %get-tuple-element.223.one_own.refs_0_), channel_id=1, source_target_pairs={{0,2},{1,3},{2,0},{3,1},{4,6},{5,7},{6,4},{7,5},{8,10},{9,11},{10,... | collective-permute-start | bytes 811016 | tf_op jit(solution)/shard_map/ppermute | solution.py:875
  169.8 13.2 %collective-permute-start.52 = (bf16[528,256]{1,0:T(8,128)(2,1)S(1)}, bf16[528,256]{1,0:T(8,128)(2,1)S(1)}, u32[]{:S(2)}, u32[]{:S(2)}) collective-permute-start(bf16[528,256]{1,0:T(8,128)(2,1)S(1)} %get-tuple-element.223.one_own.refs_0_), channel_id=1, source_target_pairs={{0,1},{1,0},{2,3},{3,2},{4,5},{5,4},{6,7},{7,6},{8,9},{9,8},{10,11... | collective-permute-start | bytes 811016 | tf_op jit(solution)/shard_map/ppermute | solution.py:875
  170.1 16.8 %collective-permute-start.57 = (bf16[272,768]{1,0:T(8,128)(2,1)S(1)}, bf16[272,768]{1,0:T(8,128)(2,1)S(1)}, u32[]{:S(2)}, u32[]{:S(2)}) collective-permute-start(bf16[272,768]{1,0:T(8,128)(2,1)S(1)} %get-tuple-element.236), channel_id=1, source_target_pairs={{0,4},{4,8},{8,12},{12,0},{1,5},{5,9},{9,13},{13,1},{2,6},{6,10},{... | collective-permute-start | bytes 1253384 | tf_op jit(solution)/shard_map/ppermute | solution.py:1210
  170.3 12.8 %collective-permute-start.46 = (bf16[528,256]{1,0:T(8,128)(2,1)S(1)}, bf16[528,256]{1,0:T(8,128)(2,1)S(1)}, u32[]{:S(2)}, u32[]{:S(2)}) collective-permute-start(bf16[528,256]{1,0:T(8,128)(2,1)S(1)} %get-tuple-element.223.one_own.refs_0_), channel_id=1, source_target_pairs={{0,16},{16,0},{1,17},{17,1},{2,18},{18,2},{3,19},{19,3},{4,20},{20... | collective-permute-start | bytes 811016 | tf_op jit(solution)/shard_map/ppermute | solution.py:868
  175.7 12.6 %collective-permute-start.53 = (bf16[528,256]{1,0:T(8,128)(2,1)S(1)}, bf16[528,256]{1,0:T(8,128)(2,1)S(1)}, u32[]{:S(2)}, u32[]{:S(2)}) collective-permute-start(bf16[528,256]{1,0:T(8,128)(2,1)S(1)} %collective-permute-done.50.refs_1_), channel_id=1, source_target_pairs={{0,16},{16,0},{1,17},{17,1},{2,18},{18,2},{3,19},{19,3},{4,20},{20... | collective-permute-start | bytes 811016 | tf_op jit(solution)/shard_map/ppermute | solution.py:868
  182.5 5.8 %collective-permute-start.54 = (bf16[528,256]{1,0:T(8,128)(2,1)S(1)}, bf16[528,256]{1,0:T(8,128)(2,1)S(1)}, u32[]{:S(2)}, u32[]{:S(2)}) collective-permute-start(bf16[528,256]{1,0:T(8,128)(2,1)S(1)} %collective-permute-done.51.refs_2_), channel_id=1, source_target_pairs={{0,16},{16,0},{1,17},{17,1},{2,18},{18,2},{3,19},{19,3},{4,20},{20... | collective-permute-start | bytes 811016 | tf_op jit(solution)/shard_map/ppermute | solution.py:868
  183.0 9.5 %collective-permute-start.55 = (bf16[528,256]{1,0:T(8,128)(2,1)S(1)}, bf16[528,256]{1,0:T(8,128)(2,1)S(1)}, u32[]{:S(2)}, u32[]{:S(2)}) collective-permute-start(bf16[528,256]{1,0:T(8,128)(2,1)S(1)} %collective-permute-done.52.refs_3_), channel_id=1, source_target_pairs={{0,16},{16,0},{1,17},{17,1},{2,18},{18,2},{3,19},{19,3},{4,20},{20... | collective-permute-start | bytes 811016 | tf_op jit(solution)/shard_map/ppermute | solution.py:868
  184.6 20.7 %collective-permute-start.58 = (bf16[272,768]{1,0:T(8,128)(2,1)S(1)}, bf16[272,768]{1,0:T(8,128)(2,1)S(1)}, u32[]{:S(2)}, u32[]{:S(2)}) collective-permute-start(bf16[272,768]{1,0:T(8,128)(2,1)S(1)} %get-tuple-element.243), channel_id=1, source_target_pairs={{0,12},{4,0},{8,4},{12,8},{1,13},{5,1},{9,5},{13,9},{2,14},{6,2},{... | collective-permute-start | bytes 1253384 | tf_op jit(solution)/shard_map/ppermute | solution.py:1210
  186.9 27.3 %collective-permute-start.59 = (bf16[272,256]{1,0:T(8,128)(2,1)S(1)}, bf16[272,256]{1,0:T(8,128)(2,1)S(1)}, u32[]{:S(2)}, u32[]{:S(2)}) collective-permute-start(bf16[272,256]{1,0:T(8,128)(2,1)S(1)} %get-tuple-element.246), channel_id=1, source_target_pairs={{0,3},{1,2},{2,1},{3,0},{4,7},{5,6},{6,5},{7,4},{8,11},{9,10},{10,... | collective-permute-start | bytes 417800 | tf_op jit(solution)/shard_map/ppermute | solution.py:875
  188.3 18.0 %collective-permute-start.47 = (bf16[256,256]{1,0:T(8,128)(2,1)S(1)}, bf16[256,256]{1,0:T(8,128)(2,1)S(1)}, u32[]{:S(2)}, u32[]{:S(2)}) collective-permute-start(bf16[256,256]{1,0:T(8,128)(2,1)S(1)} %get-tuple-element.225), channel_id=1, source_target_pairs={{0,4},{4,8},{8,12},{12,0},{1,5},{5,9},{9,13},{13,1},{2,6},{6,10},{... | collective-permute-start | bytes 393224 | tf_op jit(solution)/shard_map/ppermute | solution.py:872
  188.3 20.2 %collective-permute-start.48 = (bf16[256,256]{1,0:T(8,128)(2,1)S(1)}, bf16[256,256]{1,0:T(8,128)(2,1)S(1)}, u32[]{:S(2)}, u32[]{:S(2)}) collective-permute-start(bf16[256,256]{1,0:T(8,128)(2,1)S(1)} %get-tuple-element.226), channel_id=1, source_target_pairs={{0,8},{4,12},{8,0},{12,4},{1,9},{5,13},{9,1},{13,5},{2,10},{6,14},... | collective-permute-start | bytes 393224 | tf_op jit(solution)/shard_map/ppermute | solution.py:872
  192.5 16.1 %collective-permute-start.49 = (bf16[256,256]{1,0:T(8,128)(2,1)S(1)}, bf16[256,256]{1,0:T(8,128)(2,1)S(1)}, u32[]{:S(2)}, u32[]{:S(2)}) collective-permute-start(bf16[256,256]{1,0:T(8,128)(2,1)S(1)} %get-tuple-element.227), channel_id=1, source_target_pairs={{0,12},{4,0},{8,4},{12,8},{1,13},{5,1},{9,5},{13,9},{2,14},{6,2},{... | collective-permute-start | bytes 393224 | tf_op jit(solution)/shard_map/ppermute | solution.py:872
  205.3 8.9 %collective-permute-start.60 = (bf16[272,256]{1,0:T(8,128)(2,1)S(1)}, bf16[272,256]{1,0:T(8,128)(2,1)S(1)}, u32[]{:S(2)}, u32[]{:S(2)}) collective-permute-start(bf16[272,256]{1,0:T(8,128)(2,1)S(1)} %get-tuple-element.247), channel_id=1, source_target_pairs={{0,2},{1,3},{2,0},{3,1},{4,6},{5,7},{6,4},{7,5},{8,10},{9,11},{10,... | collective-permute-start | bytes 417800 | tf_op jit(solution)/shard_map/ppermute | solution.py:875
  206.3 7.9 %collective-permute-start.61 = (bf16[272,256]{1,0:T(8,128)(2,1)S(1)}, bf16[272,256]{1,0:T(8,128)(2,1)S(1)}, u32[]{:S(2)}, u32[]{:S(2)}) collective-permute-start(bf16[272,256]{1,0:T(8,128)(2,1)S(1)} %get-tuple-element.248), channel_id=1, source_target_pairs={{0,1},{1,0},{2,3},{3,2},{4,5},{5,4},{6,7},{7,6},{8,9},{9,8},{10,11... | collective-permute-start | bytes 417800 | tf_op jit(solution)/shard_map/ppermute | solution.py:875
  214.1 13.0 %collective-permute-start.66 = (bf16[272,768]{1,0:T(8,128)(2,1)S(1)}, bf16[272,768]{1,0:T(8,128)(2,1)S(1)}, u32[]{:S(2)}, u32[]{:S(2)}) collective-permute-start(bf16[272,768]{1,0:T(8,128)(2,1)S(1)} %get-tuple-element.260), channel_id=1, source_target_pairs={{0,4},{4,8},{8,12},{12,0},{1,5},{5,9},{9,13},{13,1},{2,6},{6,10},{... | collective-permute-start | bytes 1253384 | tf_op jit(solution)/shard_map/ppermute | solution.py:1210
  222.3 4.8 %collective-permute-start.64 = (bf16[528,256]{1,0:T(8,128)(2,1)S(1)}, bf16[528,256]{1,0:T(8,128)(2,1)S(1)}, u32[]{:S(2)}, u32[]{:S(2)}) collective-permute-start(bf16[528,256]{1,0:T(8,128)(2,1)S(1)} %get-tuple-element.253), channel_id=1, source_target_pairs={{0,16},{16,0},{1,17},{17,1},{2,18},{18,2},{3,19},{19,3},{4,20},{20... | collective-permute-start | bytes 811016 | tf_op jit(solution)/shard_map/ppermute | solution.py:868
  222.8 4.3 %collective-permute-start.65 = (bf16[528,256]{1,0:T(8,128)(2,1)S(1)}, bf16[528,256]{1,0:T(8,128)(2,1)S(1)}, u32[]{:S(2)}, u32[]{:S(2)}) collective-permute-start(bf16[528,256]{1,0:T(8,128)(2,1)S(1)} %get-tuple-element.254), channel_id=1, source_target_pairs={{0,16},{16,0},{1,17},{17,1},{2,18},{18,2},{3,19},{19,3},{4,20},{20... | collective-permute-start | bytes 811016 | tf_op jit(solution)/shard_map/ppermute | solution.py:868
  223.5 28.5 %collective-permute-start.70 = (bf16[272,768]{1,0:T(8,128)(2,1)S(1)}, bf16[272,768]{1,0:T(8,128)(2,1)S(1)}, u32[]{:S(2)}, u32[]{:S(2)}) collective-permute-start(bf16[272,768]{1,0:T(8,128)(2,1)S(1)} %get-tuple-element.269), channel_id=1, source_target_pairs={{0,8},{4,12},{8,0},{12,4},{1,9},{5,13},{9,1},{13,5},{2,10},{6,14},... | collective-permute-start | bytes 1253384 | tf_op jit(solution)/shard_map/ppermute | solution.py:1210
  225.4 28.9 %collective-permute-start.71 = (bf16[272,768]{1,0:T(8,128)(2,1)S(1)}, bf16[272,768]{1,0:T(8,128)(2,1)S(1)}, u32[]{:S(2)}, u32[]{:S(2)}) collective-permute-start(bf16[272,768]{1,0:T(8,128)(2,1)S(1)} %get-tuple-element.270), channel_id=1, source_target_pairs={{0,12},{4,0},{8,4},{12,8},{1,13},{5,1},{9,5},{13,9},{2,14},{6,2},{... | collective-permute-start | bytes 1253384 | tf_op jit(solution)/shard_map/ppermute | solution.py:1210
  229.9 24.4 %collective-permute-start.67 = (bf16[800,256]{1,0:T(8,128)(2,1)S(1)}, bf16[800,256]{1,0:T(8,128)(2,1)S(1)}, u32[]{:S(2)}, u32[]{:S(2)}) collective-permute-start(bf16[800,256]{1,0:T(8,128)(2,1)S(1)} %get-tuple-element.262), channel_id=1, source_target_pairs={{0,3},{1,2},{2,1},{3,0},{4,7},{5,6},{6,5},{7,4},{8,11},{9,10},{10,... | collective-permute-start | bytes 1228808 | tf_op jit(solution)/shard_map/ppermute | solution.py:875
  230.8 23.5 %collective-permute-start.68 = (bf16[800,256]{1,0:T(8,128)(2,1)S(1)}, bf16[800,256]{1,0:T(8,128)(2,1)S(1)}, u32[]{:S(2)}, u32[]{:S(2)}) collective-permute-start(bf16[800,256]{1,0:T(8,128)(2,1)S(1)} %get-tuple-element.263), channel_id=1, source_target_pairs={{0,2},{1,3},{2,0},{3,1},{4,6},{5,7},{6,4},{7,5},{8,10},{9,11},{10,... | collective-permute-start | bytes 1228808 | tf_op jit(solution)/shard_map/ppermute | solution.py:875
  232.1 22.3 %collective-permute-start.69 = (bf16[800,256]{1,0:T(8,128)(2,1)S(1)}, bf16[800,256]{1,0:T(8,128)(2,1)S(1)}, u32[]{:S(2)}, u32[]{:S(2)}) collective-permute-start(bf16[800,256]{1,0:T(8,128)(2,1)S(1)} %get-tuple-element.264), channel_id=1, source_target_pairs={{0,1},{1,0},{2,3},{3,2},{4,5},{5,4},{6,7},{7,6},{8,9},{9,8},{10,11... | collective-permute-start | bytes 1228808 | tf_op jit(solution)/shard_map/ppermute | solution.py:875
  261.1 19.9 %collective-permute-start.76 = (bf16[272,768]{1,0:T(8,128)(2,1)S(1)}, bf16[272,768]{1,0:T(8,128)(2,1)S(1)}, u32[]{:S(2)}, u32[]{:S(2)}) collective-permute-start(bf16[272,768]{1,0:T(8,128)(2,1)S(1)} %get-tuple-element.285), channel_id=1, source_target_pairs={{0,16},{16,0},{1,17},{17,1},{2,18},{18,2},{3,19},{19,3},{4,20},{20... | collective-permute-start | bytes 1253384 | tf_op jit(solution)/shard_map/ppermute | solution.py:868
  261.5 5.8 %collective-permute-start.73 = (bf16[336,256]{1,0:T(8,128)(2,1)S(1)}, bf16[336,256]{1,0:T(8,128)(2,1)S(1)}, u32[]{:S(2)}, u32[]{:S(2)}) collective-permute-start(bf16[336,256]{1,0:T(8,128)(2,1)S(1)} %get-tuple-element.277), channel_id=1, source_target_pairs={{0,4},{4,8},{8,12},{12,0},{1,5},{5,9},{9,13},{13,1},{2,6},{6,10},{... | collective-permute-start | bytes 516104 | tf_op jit(solution)/shard_map/ppermute | solution.py:872
  261.6 14.9 %collective-permute-start.74 = (bf16[336,256]{1,0:T(8,128)(2,1)S(1)}, bf16[336,256]{1,0:T(8,128)(2,1)S(1)}, u32[]{:S(2)}, u32[]{:S(2)}) collective-permute-start(bf16[336,256]{1,0:T(8,128)(2,1)S(1)} %get-tuple-element.278), channel_id=1, source_target_pairs={{0,8},{4,12},{8,0},{12,4},{1,9},{5,13},{9,1},{13,5},{2,10},{6,14},... | collective-permute-start | bytes 516104 | tf_op jit(solution)/shard_map/ppermute | solution.py:872
  263.1 15.9 %collective-permute-start.75 = (bf16[336,256]{1,0:T(8,128)(2,1)S(1)}, bf16[336,256]{1,0:T(8,128)(2,1)S(1)}, u32[]{:S(2)}, u32[]{:S(2)}) collective-permute-start(bf16[336,256]{1,0:T(8,128)(2,1)S(1)} %get-tuple-element.279), channel_id=1, source_target_pairs={{0,12},{4,0},{8,4},{12,8},{1,13},{5,1},{9,5},{13,9},{2,14},{6,2},{... | collective-permute-start | bytes 516104 | tf_op jit(solution)/shard_map/ppermute | solution.py:872
  (45 other events, 291.0 us)

commit v2 on v1

--- a/solution.py
+++ b/solution.py
@@ -17,7 +17,7 @@
 NN = ((1,), (0,))
 NT = ((1,), (1,))
 TN = ((0,), (0,))
-VMEM_BYTES = 50 * 1024 * 1024
+VMEM_BYTES = 28 * 1024 * 1024
 ALL_VMEM_BYTES = 63 * 1024 * 1024
 
 

time: 284 us -> 268 us (0.944)
  Pallas kernels: 110 us -> 89.6 us
  waiting for transfers between devices: 84 us -> 92.7 us
    ppermute x6, waiting for transfers between devices: 32.6 us -> 37.6 us  [shifted(): lax.ppermute(x, 'seq', [(i, (i + r) % seq) for i in range(seq)])]
    pallas_call x2, Pallas kernels: 11.1 us -> 6.89 us  [weight_grads(): pl.pallas_call(functools.partial(weights_kernel, sz, seq, len(deps), bool...]
    pallas_call x2, Pallas kernels: 10.2 us -> 6.21 us  [lift(): pl.pallas_call(functools.partial(lift_kernel, sz, layer, len(deps)), in_s...]
    pallas_call x2, Pallas kernels: 27.3 us -> 23.6 us  [call(): pl.pallas_call(functools.partial(forward_kernel, sz, layer, slots), grid_...]
    pallas_call x1, Pallas kernels: 5.15 us -> 2.16 us  [per_device(): turned = turned(sc_join, *in_weights, *last_weights)]
    pallas_call x2, Pallas kernels: 24.8 us -> 21.9 us  [call(): pl.pallas_call(functools.partial(backward_kernel, sz, layer, len(deps)),...]
    ppermute x24, waiting for transfers between devices: 20.9 us -> 23.7 us  [over_heads(): lax.ppermute(x, 'head', [(i, i ^ d) for i in range(head_axis)])]
    unnamed x64 -> x40, local copies, waits for them, and re-layouts: 7.35 us -> 4.83 us
  transfers between devices with their start and end apart: 77 -> 77, of which waited for: 23 -> 25; matrix products, arithmetic and copies ran while one was open for 0% -> 0% of each run, Pallas kernels for 27% -> 23%
where the time goes in v2:
time: 268 us; the launch traced here: 267 us
  waiting for transfers between devices  92.7 us (35%)
  Pallas kernels  89.6 us (33%)
  starting transfers between devices  78.2 us (29%)
  local copies, waits for them, and re-layouts  4.84 us (2%)
    ppermute x6, waiting for transfers between devices, shifted(): lax.ppermute(x, 'seq', [(i, (i + r) % seq) for i in range(seq)])  37.6 us
    ppermute x35, starting transfers between devices, cross(): return lax.ppermute(x, 'section', swap)  34.1 us
    ppermute x24, waiting for transfers between devices, over_heads(): lax.ppermute(x, 'head', [(i, i ^ d) for i in range(head_axis)])  23.7 us
    pallas_call x2, Pallas kernels, call(): pl.pallas_call(functools.partial(forward_kernel, sz, layer, slots), grid_...  23.6 us
    ppermute x12, waiting for transfers between devices, turn(): return lax.ppermute(x, 'seq', pairs) if r else x  22 us
    pallas_call x2, Pallas kernels, call(): pl.pallas_call(functools.partial(backward_kernel, sz, layer, len(deps)),...  21.9 us
    ppermute x24, starting transfers between devices, over_heads(): lax.ppermute(x, 'head', [(i, i ^ d) for i in range(head_axis)])  21.7 us
    ppermute x12, starting transfers between devices, turn(): return lax.ppermute(x, 'seq', pairs) if r else x  12.7 us
  transfers between devices with their start and end apart: 77, of which 25 were waited for; matrix products, arithmetic and copies ran while one was open for 0% of the time, Pallas kernels for 23%

profile of v2, /device:TPU:9, one launch (start us, length us, event | category | flops | bytes accessed | tf_op | source)
XLA Modules:
  0.0 267.1 jit_solution(4792708088521644540)
XLA Ops:
  1.2 3.0 %shard_map.212 = (bf16[144,1024]{1,0:T(8,128)(2,1)}, bf16[144,1024]{1,0:T(8,128)(2,1)}, bf16[144,1024]{1,0:T(8,128)(2,1)}, bf16[144,1024]{1,0:T(8,128)(2,1)}, s32[4]{0:T(128)}) custom-call(s32[4]{0:T(128)} %pad_add_fusion.sc, s32[4]{0:T(128)} %order.3, bf16[4,256,1024]{2,1,0:T(8,128)(2,1)} %tokens.1, f32[1,4,8,256]{3,2,1,0:T(8,128)} %rates.1), custom_call_target="tpu_custom_call" | custom-call | tf_op jit(solution)/shard_map/pallas_call | solution.py:899
  4.3 1.3 collective-permute-start
  6.7 4.1 %shard_map.213 = (bf16[1024,256]{1,0:T(8,128)(2,1)}, bf16[1024,256]{1,0:T(8,128)(2,1)}, bf16[256,1024]{1,0:T(8,128)(2,1)}, f32[16,1024]{1,0:T(8,128)}, f32[16,10...) custom-call(s32[4]{0:T(128)} %get-tuple-element.153.sc, ...), custom_call_target="tpu_custom_call" | custom-call | tf_op jit(solution)/shard_map/pallas_call | solution.py:911
  11.9 1.7 collective-permute-start.2
  14.3 12.6 %collective-permute-start.9 = (bf16[1024,256]{1,0:T(8,128)(2,1)}, bf16[1024,256]{1,0:T(8,128)(2,1)S(1)}, u32[]{:S(2)}, u32[]{:S(2)}) collective-permute-start(bf16[1024,256]{1,0:T(8,128)(2,1)} %get-tuple-element.161), channel_id=1, source_target_pairs={{0,16},{16,0},{1,17},{17,1},{2,18},{18,2},{3,19},{19,3},{4,20},{20... | collective-permute-start | bytes 1572872 | tf_op jit(solution)/shard_map/ppermute | solution.py:868
  26.9 3.6 %collective-permute-done.1.refs_2_ = bf16[144,1024]{1,0:T(8,128)(2,1)} collective-permute-done((bf16[144,1024]{1,0:T(8,128)(2,1)}, bf16[144,1024]{1,0:T(8,128)(2,1)}, u32[]{:S(2)}, u32[]{:S(2)}) %collective-permute-start.1) | collective-permute-done | bytes 294944 | tf_op jit(solution)/shard_map/ppermute | solution.py:872
  30.6 1.5 collective-permute-start.10
  32.1 1.2 collective-permute-done.2.refs_3_
  36.3 1.2 copy-done.1
  37.5 1.2 copy-done.3
  39.6 13.7 %shard_map.214 = (bf16[1024,1024]{1,0:T(8,128)(2,1)S(1)}, f32[1024,256]{1,0:T(8,128)S(1)}, bf16[1024,512]{1,0:T(8,128)(2,1)S(1)}, f32[1024,256]{1,0:T(8,128)S(1)...) custom-call(s32[4]{0:T(128)S(1)} %copy-done.8, ...), custom_call_target="tpu_custom_call" | custom-call | flops 12884901888 | bytes 16000000 | tf_op jit(solution)/shard_map/pallas_call | solution.py:962
  54.3 1.4 shard_map.215
  56.9 2.3 collective-permute-done.14.refs_0_
  60.4 2.2 collective-permute-start.15
  63.1 2.3 collective-permute-start.25
  65.4 1.5 collective-permute-start.26
  66.9 2.2 shard_map.217
  69.1 2.0 collective-permute-start.27
  71.1 4.5 %collective-permute-done.16.refs_2_ = bf16[528,256]{1,0:T(8,128)(2,1)S(1)} collective-permute-done((bf16[528,256]{1,0:T(8,128)(2,1)S(1)}, bf16[528,256]{1,0:T(8,128)(2,1)S(1)}, u32[]{:S(2)}, u32[]{:S(2)}) %collective-permute-start.16) | collective-permute-done | bytes 270368 | tf_op jit(solution)/shard_map/ppermute | solution.py:875
  77.1 1.5 collective-permute-start.18
  80.8 5.1 %collective-permute-done.18.refs_1_ = bf16[512,256]{1,0:T(8,128)(2,1)S(1)} collective-permute-done((bf16[512,256]{1,0:T(8,128)(2,1)S(1)}, bf16[512,256]{1,0:T(8,128)(2,1)S(1)}, u32[]{:S(2)}, u32[]{:S(2)}) %collective-permute-start.18) | collective-permute-done | bytes 262176 | tf_op jit(solution)/shard_map/ppermute | solution.py:875
  86.0 1.3 collective-permute-start.22
  87.3 4.6 %collective-permute-done.19.refs_2_ = bf16[512,256]{1,0:T(8,128)(2,1)S(1)} collective-permute-done((bf16[512,256]{1,0:T(8,128)(2,1)S(1)}, bf16[512,256]{1,0:T(8,128)(2,1)S(1)}, u32[]{:S(2)}, u32[]{:S(2)}) %collective-permute-start.19) | collective-permute-done | bytes 262176 | tf_op jit(solution)/shard_map/ppermute | solution.py:875
  93.9 9.9 %shard_map.219 = (bf16[1024,1024]{1,0:T(8,128)(2,1)S(1)}, f32[1024,256]{1,0:T(8,128)S(1)}, bf16[1024,512]{1,0:T(8,128)(2,1)S(1)}, f32[1024,256]{1,0:T(8,128)S(1)...) custom-call(s32[4]{0:T(128)S(1)} %copy-done.8, ...), custom_call_target="tpu_custom_call" | custom-call | flops 12884901888 | bytes 16000000 | tf_op jit(solution)/shard_map/pallas_call | solution.py:962
  103.9 1.6 shard_map.220
  106.1 2.2 collective-permute-done.31
  108.3 1.2 collective-permute-start.32
  110.9 1.1 shard_map.221
  112.1 1.5 collective-permute-start.35
  114.8 10.8 %shard_map.222 = (bf16[1024,768]{1,0:T(8,128)(2,1)S(1)}, bf16[1024,256]{1,0:T(8,128)(2,1)S(1)}, bf16[16,768]{1,0:T(8,128)(2,1)S(1)}, f32[8,512]{1,0:T(8,128)S(1)...) custom-call(s32[4]{0:T(128)S(1)} %get-tuple-element.189.sc, ...), custom_call_target="tpu_custom_call" | custom-call | flops 17179869184 | bytes 16000000 | tf_op jit(solution)/shard_map/pallas_call | solution.py:1038
  125.6 1.6 collective-permute-done.36.refs_2_
  127.2 3.1 %shard_map.223 = (bf16[4,528,256]{2,1,0:T(8,128)(2,1)S(1)}, bf16[528,256]{1,0:T(8,128)(2,1)S(1)}, bf16[528,256]{1,0:T(8,128)(2,1)S(1)}, bf16[528,256]{1,0:T(8,12...) custom-call(s32[4]{0:T(128)S(1)} %get-tuple-element.195.sc, ...), custom_call_target="tpu_custom_call" | custom-call | flops 2147483648 | bytes 8000000 | tf_op jit(solution)/shard_map/pallas_call | solution.py:1115
  131.6 3.4 %shard_map.224 = (s32[4]{0:T(128)S(1)}, bf16[272,768]{1,0:T(8,128)(2,1)S(1)}, bf16[272,768]{1,0:T(8,128)(2,1)S(1)}, bf16[272,768]{1,0:T(8,128)(2,1)S(1)}, bf16[2...) custom-call(s32[4]{0:T(128)S(1)} %get-tuple-element.202.sc, ...), custom_call_target="tpu_custom_call" | custom-call | flops 8589934592 | bytes 12000000 | tf_op jit(solution)/shard_map/pallas_call | solution.py:1196
  135.0 2.4 collective-permute-start.45
  137.4 1.3 shard_map.225
  138.7 1.4 collective-permute-start.42
  141.4 14.1 %collective-permute-done.45.refs_10_.refs_2_ = bf16[272,768]{1,0:T(8,128)(2,1)S(1)} collective-permute-done((bf16[272,768]{1,0:T(8,128)(2,1)S(1)}, bf16[272,768]{1,0:T(8,128)(2,1)S(1)}, u32[]{:S(2)}, u32[]{:S(2)}) %collective-permute-start.45) | collective-permute-done | bytes 417824 | tf_op jit(solution)/shard_map/ppermute | solution.py:1210
  155.6 2.2 shard_map.226
  157.8 1.4 collective-permute-start.50
  160.8 1.6 collective-permute-start.46
  162.4 3.7 %collective-permute-done.50.refs_1_ = bf16[528,256]{1,0:T(8,128)(2,1)S(1)} collective-permute-done((bf16[528,256]{1,0:T(8,128)(2,1)S(1)}, bf16[528,256]{1,0:T(8,128)(2,1)S(1)}, u32[]{:S(2)}, u32[]{:S(2)}) %collective-permute-start.50) | collective-permute-done | bytes 270368 | tf_op jit(solution)/shard_map/ppermute | solution.py:875
  166.1 2.7 %collective-permute-start.53 = (bf16[528,256]{1,0:T(8,128)(2,1)S(1)}, bf16[528,256]{1,0:T(8,128)(2,1)S(1)}, u32[]{:S(2)}, u32[]{:S(2)}) collective-permute-start(bf16[528,256]{1,0:T(8,128)(2,1)S(1)} %collective-permute-done.50.refs_1_), channel_id=1, source_target_pairs={{0,16},{16,0},{1,17},{17,1},{2,18},{18,2},{3,19},{19,3},{4,20},{20... | collective-permute-start | bytes 811016 | tf_op jit(solution)/shard_map/ppermute | solution.py:868
  168.8 4.1 %collective-permute-done.51.refs_2_ = bf16[528,256]{1,0:T(8,128)(2,1)S(1)} collective-permute-done((bf16[528,256]{1,0:T(8,128)(2,1)S(1)}, bf16[528,256]{1,0:T(8,128)(2,1)S(1)}, u32[]{:S(2)}, u32[]{:S(2)}) %collective-permute-start.51) | collective-permute-done | bytes 270368 | tf_op jit(solution)/shard_map/ppermute | solution.py:875
  175.0 2.3 collective-permute-start.58
  177.3 1.4 collective-permute-start.59
  178.7 4.2 %collective-permute-start.48 = (bf16[256,256]{1,0:T(8,128)(2,1)S(1)}, bf16[256,256]{1,0:T(8,128)(2,1)S(1)}, u32[]{:S(2)}, u32[]{:S(2)}) collective-permute-start(bf16[256,256]{1,0:T(8,128)(2,1)S(1)} %get-tuple-element.226), channel_id=1, source_target_pairs={{0,8},{4,12},{8,0},{12,4},{1,9},{5,13},{9,1},{13,5},{2,10},{6,14},... | collective-permute-start | bytes 393224 | tf_op jit(solution)/shard_map/ppermute | solution.py:872
  182.9 11.1 %shard_map.229 = (bf16[1024,768]{1,0:T(8,128)(2,1)S(1)}, bf16[1024,256]{1,0:T(8,128)(2,1)S(1)}, bf16[16,768]{1,0:T(8,128)(2,1)S(1)}, f32[8,512]{1,0:T(8,128)S(1)...) custom-call(s32[4]{0:T(128)S(1)} %copy-done.8, ...), custom_call_target="tpu_custom_call" | custom-call | flops 17179869184 | bytes 16000000 | tf_op jit(solution)/shard_map/pallas_call | solution.py:1038
  195.3 3.5 %collective-permute-done.48.refs_1_.refs_2_ = bf16[256,256]{1,0:T(8,128)(2,1)S(1)} collective-permute-done((bf16[256,256]{1,0:T(8,128)(2,1)S(1)}, bf16[256,256]{1,0:T(8,128)(2,1)S(1)}, u32[]{:S(2)}, u32[]{:S(2)}) %collective-permute-start.48) | collective-permute-done | bytes 131104 | tf_op jit(solution)/shard_map/ppermute | solution.py:872
  198.8 3.5 %shard_map.230 = (s32[4]{0:T(128)S(1)}, bf16[272,768]{1,0:T(8,128)(2,1)S(1)}, bf16[272,768]{1,0:T(8,128)(2,1)S(1)}, bf16[272,768]{1,0:T(8,128)(2,1)S(1)}, bf16[2...) custom-call(s32[4]{0:T(128)S(1)} %get-tuple-element.237.sc, ...), custom_call_target="tpu_custom_call" | custom-call | flops 8589934592 | bytes 12000000 | tf_op jit(solution)/shard_map/pallas_call | solution.py:1196
  202.4 3.1 %shard_map.231 = (bf16[4,528,256]{2,1,0:T(8,128)(2,1)S(1)}, bf16[528,256]{1,0:T(8,128)(2,1)S(1)}, bf16[528,256]{1,0:T(8,128)(2,1)S(1)}, bf16[528,256]{1,0:T(8,12...) custom-call(s32[4]{0:T(128)S(1)} %get-tuple-element.244.sc, ...), custom_call_target="tpu_custom_call" | custom-call | flops 2147483648 | bytes 8000000 | tf_op jit(solution)/shard_map/pallas_call | solution.py:1115
  207.7 3.1 %collective-permute-start.70 = (bf16[272,768]{1,0:T(8,128)(2,1)S(1)}, bf16[272,768]{1,0:T(8,128)(2,1)S(1)}, u32[]{:S(2)}, u32[]{:S(2)}) collective-permute-start(bf16[272,768]{1,0:T(8,128)(2,1)S(1)} %get-tuple-element.269), channel_id=1, source_target_pairs={{0,8},{4,12},{8,0},{12,4},{1,9},{5,13},{9,1},{13,5},{2,10},{6,14},... | collective-permute-start | bytes 1253384 | tf_op jit(solution)/shard_map/ppermute | solution.py:1210
  210.8 1.7 collective-permute-start.71
  214.7 1.1 collective-permute-start.68
  217.2 1.8 shard_map.228
  219.0 19.2 %collective-permute-done.70.refs_14_.refs_2_ = bf16[272,768]{1,0:T(8,128)(2,1)S(1)} collective-permute-done((bf16[272,768]{1,0:T(8,128)(2,1)S(1)}, bf16[272,768]{1,0:T(8,128)(2,1)S(1)}, u32[]{:S(2)}, u32[]{:S(2)}) %collective-permute-start.70) | collective-permute-done | bytes 417824 | tf_op jit(solution)/shard_map/ppermute | solution.py:1210
  238.2 4.3 %collective-permute-done.71.refs_15_.refs_3_ = bf16[272,768]{1,0:T(8,128)(2,1)S(1)} collective-permute-done((bf16[272,768]{1,0:T(8,128)(2,1)S(1)}, bf16[272,768]{1,0:T(8,128)(2,1)S(1)}, u32[]{:S(2)}, u32[]{:S(2)}) %collective-permute-start.71) | collective-permute-done | bytes 417824 | tf_op jit(solution)/shard_map/ppermute | solution.py:1210
  242.5 1.2 shard_map.234
  244.2 1.4 collective-permute-done.72.zero_other.one_other
  245.6 1.2 shard_map.235
  248.0 1.5 collective-permute-start.75
  249.5 4.4 %collective-permute-done.73.refs_5_.refs_1_ = bf16[336,256]{1,0:T(8,128)(2,1)S(1)} collective-permute-done((bf16[336,256]{1,0:T(8,128)(2,1)S(1)}, bf16[336,256]{1,0:T(8,128)(2,1)S(1)}, u32[]{:S(2)}, u32[]{:S(2)}) %collective-permute-start.73) | collective-permute-done | bytes 172064 | tf_op jit(solution)/shard_map/ppermute | solution.py:872
  253.8 9.1 %collective-permute-done.74.refs_6_.refs_2_ = bf16[336,256]{1,0:T(8,128)(2,1)S(1)} collective-permute-done((bf16[336,256]{1,0:T(8,128)(2,1)S(1)}, bf16[336,256]{1,0:T(8,128)(2,1)S(1)}, u32[]{:S(2)}, u32[]{:S(2)}) %collective-permute-start.74) | collective-permute-done | bytes 172064 | tf_op jit(solution)/shard_map/ppermute | solution.py:872
  263.2 2.0 shard_map.236
  265.2 1.9 shard_map.238
  (161 shorter events, 35.5 us)
Async XLA Ops:
  4.3 10.0 %collective-permute-start = (bf16[144,1024]{1,0:T(8,128)(2,1)}, bf16[144,1024]{1,0:T(8,128)(2,1)}, u32[]{:S(2)}, u32[]{:S(2)}) collective-permute-start(bf16[144,1024]{1,0:T(8,128)(2,1)} %get-tuple-element.155), channel_id=1, source_target_pairs={{0,4},{4,8},{8,12},{12,0},{1,5},{5,9},{9,13},{13,1},{2,6},{6,10},{... | collective-permute-start | bytes 884744 | tf_op jit(solution)/shard_map/ppermute | solution.py:872
  5.6 25.0 %collective-permute-start.1 = (bf16[144,1024]{1,0:T(8,128)(2,1)}, bf16[144,1024]{1,0:T(8,128)(2,1)}, u32[]{:S(2)}, u32[]{:S(2)}) collective-permute-start(bf16[144,1024]{1,0:T(8,128)(2,1)} %get-tuple-element.156), channel_id=1, source_target_pairs={{0,8},{4,12},{8,0},{12,4},{1,9},{5,13},{9,1},{13,5},{2,10},{6,14},... | collective-permute-start | bytes 884744 | tf_op jit(solution)/shard_map/ppermute | solution.py:872
  10.8 23.0 %collective-permute-start.8 = (bf16[1024,256]{1,0:T(8,128)(2,1)}, bf16[1024,256]{1,0:T(8,128)(2,1)S(1)}, u32[]{:S(2)}, u32[]{:S(2)}) collective-permute-start(bf16[1024,256]{1,0:T(8,128)(2,1)} %get-tuple-element.160), channel_id=1, source_target_pairs={{0,16},{16,0},{1,17},{17,1},{2,18},{18,2},{3,19},{19,3},{4,20},{20... | collective-permute-start | bytes 1572872 | tf_op jit(solution)/shard_map/ppermute | solution.py:868
  11.9 21.4 %collective-permute-start.2 = (bf16[144,1024]{1,0:T(8,128)(2,1)}, bf16[144,1024]{1,0:T(8,128)(2,1)S(1)}, u32[]{:S(2)}, u32[]{:S(2)}) collective-permute-start(bf16[144,1024]{1,0:T(8,128)(2,1)} %get-tuple-element.157), channel_id=1, source_target_pairs={{0,12},{4,0},{8,4},{12,8},{1,13},{5,1},{9,5},{13,9},{2,14},{6,2},{... | collective-permute-start | bytes 884744 | tf_op jit(solution)/shard_map/ppermute | solution.py:872
  13.7 20.1 %collective-permute-start.3 = (bf16[144,1024]{1,0:T(8,128)(2,1)S(1)}, bf16[144,1024]{1,0:T(8,128)(2,1)S(1)}, u32[]{:S(2)}, u32[]{:S(2)}) collective-permute-start(bf16[144,1024]{1,0:T(8,128)(2,1)S(1)} %copy-done.9), channel_id=1, source_target_pairs={{0,16},{16,0},{1,17},{17,1},{2,18},{18,2},{3,19},{19,3},{4,20},{20... | collective-permute-start | bytes 884744 | tf_op jit(solution)/shard_map/ppermute | solution.py:868
  14.3 20.0 %collective-permute-start.9 = (bf16[1024,256]{1,0:T(8,128)(2,1)}, bf16[1024,256]{1,0:T(8,128)(2,1)S(1)}, u32[]{:S(2)}, u32[]{:S(2)}) collective-permute-start(bf16[1024,256]{1,0:T(8,128)(2,1)} %get-tuple-element.161), channel_id=1, source_target_pairs={{0,16},{16,0},{1,17},{17,1},{2,18},{18,2},{3,19},{19,3},{4,20},{20... | collective-permute-start | bytes 1572872 | tf_op jit(solution)/shard_map/ppermute | solution.py:868
  34.3 20.0 %collective-permute-start.11 = (bf16[256,1024]{1,0:T(8,128)(2,1)}, bf16[256,1024]{1,0:T(8,128)(2,1)S(1)}, u32[]{:S(2)}, u32[]{:S(2)}) collective-permute-start(bf16[256,1024]{1,0:T(8,128)(2,1)} %get-tuple-element.165), channel_id=1, source_target_pairs={{0,16},{16,0},{1,17},{17,1},{2,18},{18,2},{3,19},{19,3},{4,20},{20... | collective-permute-start | bytes 1572872 | tf_op jit(solution)/shard_map/ppermute | solution.py:868
  34.4 19.9 %collective-permute-start.12 = (bf16[128,1024]{1,0:T(8,128)(2,1)}, bf16[128,1024]{1,0:T(8,128)(2,1)S(1)}, u32[]{:S(2)}, u32[]{:S(2)}) collective-permute-start(bf16[128,1024]{1,0:T(8,128)(2,1)} %get-tuple-element.166), channel_id=1, source_target_pairs={{0,4},{4,8},{8,12},{12,0},{1,5},{5,9},{9,13},{13,1},{2,6},{6,10},{... | collective-permute-start | bytes 786440 | tf_op jit(solution)/shard_map/ppermute | solution.py:872
  35.2 19.0 %collective-permute-start.13 = (bf16[128,1024]{1,0:T(8,128)(2,1)}, bf16[128,1024]{1,0:T(8,128)(2,1)S(1)}, u32[]{:S(2)}, u32[]{:S(2)}) collective-permute-start(bf16[128,1024]{1,0:T(8,128)(2,1)} %get-tuple-element.167), channel_id=1, source_target_pairs={{0,12},{4,0},{8,4},{12,8},{1,13},{5,1},{9,5},{13,9},{2,14},{6,2},{... | collective-permute-start | bytes 786440 | tf_op jit(solution)/shard_map/ppermute | solution.py:872
  60.4 8.7 %collective-permute-start.15 = (bf16[528,256]{1,0:T(8,128)(2,1)S(1)}, bf16[528,256]{1,0:T(8,128)(2,1)S(1)}, u32[]{:S(2)}, u32[]{:S(2)}) collective-permute-start(bf16[528,256]{1,0:T(8,128)(2,1)S(1)} %get-tuple-element.171), channel_id=1, source_target_pairs={{0,3},{1,2},{2,1},{3,0},{4,7},{5,6},{6,5},{7,4},{8,11},{9,10},{10,... | collective-permute-start | bytes 811016 | tf_op jit(solution)/shard_map/ppermute | solution.py:875
  62.6 12.9 %collective-permute-start.16 = (bf16[528,256]{1,0:T(8,128)(2,1)S(1)}, bf16[528,256]{1,0:T(8,128)(2,1)S(1)}, u32[]{:S(2)}, u32[]{:S(2)}) collective-permute-start(bf16[528,256]{1,0:T(8,128)(2,1)S(1)} %get-tuple-element.172), channel_id=1, source_target_pairs={{0,2},{1,3},{2,0},{3,1},{4,6},{5,7},{6,4},{7,5},{8,10},{9,11},{10,... | collective-permute-start | bytes 811016 | tf_op jit(solution)/shard_map/ppermute | solution.py:875
  62.8 13.2 %collective-permute-start.17 = (bf16[528,256]{1,0:T(8,128)(2,1)S(1)}, bf16[528,256]{1,0:T(8,128)(2,1)S(1)}, u32[]{:S(2)}, u32[]{:S(2)}) collective-permute-start(bf16[528,256]{1,0:T(8,128)(2,1)S(1)} %get-tuple-element.173), channel_id=1, source_target_pairs={{0,1},{1,0},{2,3},{3,2},{4,5},{5,4},{6,7},{7,6},{8,9},{9,8},{10,11... | collective-permute-start | bytes 811016 | tf_op jit(solution)/shard_map/ppermute | solution.py:875
  63.1 15.5 %collective-permute-start.25 = (bf16[128,1024]{1,0:T(8,128)(2,1)S(1)}, bf16[128,1024]{1,0:T(8,128)(2,1)S(1)}, u32[]{:S(2)}, u32[]{:S(2)}) collective-permute-start(bf16[128,1024]{1,0:T(8,128)(2,1)S(1)} %copy-done.19), channel_id=1, source_target_pairs={{0,8},{4,12},{8,0},{12,4},{1,9},{5,13},{9,1},{13,5},{2,10},{6,14},... | collective-permute-start | bytes 786440 | tf_op jit(solution)/shard_map/ppermute | solution.py:872
  65.4 14.2 %collective-permute-start.26 = (bf16[128,1024]{1,0:T(8,128)(2,1)S(1)}, bf16[128,1024]{1,0:T(8,128)(2,1)S(1)}, u32[]{:S(2)}, u32[]{:S(2)}) collective-permute-start(bf16[128,1024]{1,0:T(8,128)(2,1)S(1)} %copy-done.10), channel_id=1, source_target_pairs={{0,16},{16,0},{1,17},{17,1},{2,18},{18,2},{3,19},{19,3},{4,20},{20... | collective-permute-start | bytes 786440 | tf_op jit(solution)/shard_map/ppermute | solution.py:868
  69.1 10.8 %collective-permute-start.27 = (bf16[128,1024]{1,0:T(8,128)(2,1)S(1)}, bf16[128,1024]{1,0:T(8,128)(2,1)S(1)}, u32[]{:S(2)}, u32[]{:S(2)}) collective-permute-start(bf16[128,1024]{1,0:T(8,128)(2,1)S(1)} %collective-permute-done.12.refs_2_.refs_9_), channel_id=1, source_target_pairs={{0,16},{16,0},{1,17},{17,1},{2,18},{18,2},{3,19},{19,3},{4,20},{20... | collective-permute-start | bytes 786440 | tf_op jit(solution)/shard_map/ppermute | solution.py:868
  75.5 5.2 %collective-permute-start.29 = (bf16[128,1024]{1,0:T(8,128)(2,1)S(1)}, bf16[128,1024]{1,0:T(8,128)(2,1)S(1)}, u32[]{:S(2)}, u32[]{:S(2)}) collective-permute-start(bf16[128,1024]{1,0:T(8,128)(2,1)S(1)} %collective-permute-done.13.refs_3_.refs_11_), channel_id=1, source_target_pairs={{0,16},{16,0},{1,17},{17,1},{2,18},{18,2},{3,19},{19,3},{4,20},{20... | collective-permute-start | bytes 786440 | tf_op jit(solution)/shard_map/ppermute | solution.py:868
  77.1 8.9 %collective-permute-start.18 = (bf16[512,256]{1,0:T(8,128)(2,1)S(1)}, bf16[512,256]{1,0:T(8,128)(2,1)S(1)}, u32[]{:S(2)}, u32[]{:S(2)}) collective-permute-start(bf16[512,256]{1,0:T(8,128)(2,1)S(1)} %get-tuple-element.180.refs_0_.zero_own), channel_id=1, source_target_pairs={{0,3},{1,2},{2,1},{3,0},{4,7},{5,6},{6,5},{7,4},{8,11},{9,10},{10,... | collective-permute-start | bytes 786440 | tf_op jit(solution)/shard_map/ppermute | solution.py:875
  78.6 13.3 %collective-permute-start.19 = (bf16[512,256]{1,0:T(8,128)(2,1)S(1)}, bf16[512,256]{1,0:T(8,128)(2,1)S(1)}, u32[]{:S(2)}, u32[]{:S(2)}) collective-permute-start(bf16[512,256]{1,0:T(8,128)(2,1)S(1)} %get-tuple-element.180.refs_0_.zero_own), channel_id=1, source_target_pairs={{0,2},{1,3},{2,0},{3,1},{4,6},{5,7},{6,4},{7,5},{8,10},{9,11},{10,... | collective-permute-start | bytes 786440 | tf_op jit(solution)/shard_map/ppermute | solution.py:875
  79.6 12.8 %collective-permute-start.20 = (bf16[512,256]{1,0:T(8,128)(2,1)S(1)}, bf16[512,256]{1,0:T(8,128)(2,1)S(1)}, u32[]{:S(2)}, u32[]{:S(2)}) collective-permute-start(bf16[512,256]{1,0:T(8,128)(2,1)S(1)} %get-tuple-element.180.refs_0_.zero_own), channel_id=1, source_target_pairs={{0,1},{1,0},{2,3},{3,2},{4,5},{5,4},{6,7},{7,6},{8,9},{9,8},{10,11... | collective-permute-start | bytes 786440 | tf_op jit(solution)/shard_map/ppermute | solution.py:875
  79.8 12.7 %collective-permute-start.28 = (bf16[128,1024]{1,0:T(8,128)(2,1)S(1)}, bf16[128,1024]{1,0:T(8,128)(2,1)S(1)}, u32[]{:S(2)}, u32[]{:S(2)}) collective-permute-start(bf16[128,1024]{1,0:T(8,128)(2,1)S(1)} %collective-permute-done.25.refs_10_), channel_id=1, source_target_pairs={{0,16},{16,0},{1,17},{17,1},{2,18},{18,2},{3,19},{19,3},{4,20},{20... | collective-permute-start | bytes 786440 | tf_op jit(solution)/shard_map/ppermute | solution.py:868
  80.7 11.7 %collective-permute-start.21 = (bf16[512,256]{1,0:T(8,128)(2,1)S(1)}, bf16[512,256]{1,0:T(8,128)(2,1)S(1)}, u32[]{:S(2)}, u32[]{:S(2)}) collective-permute-start(bf16[512,256]{1,0:T(8,128)(2,1)S(1)} %get-tuple-element.180.refs_0_.zero_own), channel_id=1, source_target_pairs={{0,16},{16,0},{1,17},{17,1},{2,18},{18,2},{3,19},{19,3},{4,20},{20... | collective-permute-start | bytes 786440 | tf_op jit(solution)/shard_map/ppermute | solution.py:868
  86.0 6.5 %collective-permute-start.22 = (bf16[512,256]{1,0:T(8,128)(2,1)S(1)}, bf16[512,256]{1,0:T(8,128)(2,1)S(1)}, u32[]{:S(2)}, u32[]{:S(2)}) collective-permute-start(bf16[512,256]{1,0:T(8,128)(2,1)S(1)} %collective-permute-done.18.refs_1_), channel_id=1, source_target_pairs={{0,16},{16,0},{1,17},{17,1},{2,18},{18,2},{3,19},{19,3},{4,20},{20... | collective-permute-start | bytes 786440 | tf_op jit(solution)/shard_map/ppermute | solution.py:868
  105.5 5.4 %collective-permute-start.30 = (bf16[4,528,256]{2,1,0:T(8,128)(2,1)S(1)}, bf16[4,528,256]{2,1,0:T(8,128)(2,1)S(1)}, u32[]{:S(2)}, u32[]{:S(2)}) collective-permute-start(bf16[4,528,256]{2,1,0:T(8,128)(2,1)S(1)} %get-tuple-element.188), channel_id=1, source_target_pairs={{0,16},{16,0},{1,17},{17,1},{2,18},{18,2},{3,19},{19,3},{4,20},{20... | collective-permute-start | bytes 3244040 | tf_op jit(solution)/shard_map/ppermute | solution.py:868
  108.3 6.3 %collective-permute-start.32 = (f32[2,1024]{1,0:T(2,128)S(1)}, f32[2,1024]{1,0:T(2,128)S(1)}, u32[]{:S(2)}, u32[]{:S(2)}) collective-permute-start(f32[2,1024]{1,0:T(2,128)S(1)} %add.3.refs_1_), channel_id=1, source_target_pairs={{0,1},{1,0},{2,3},{3,2},{4,5},{5,4},{6,7},{7,6},{8,9},{9,8},{10,11... | collective-permute-start | bytes 24584 | tf_op jit(solution)/shard_map/ppermute | solution.py:875
  109.5 5.3 %collective-permute-start.33 = (f32[2,1024]{1,0:T(2,128)S(1)}, f32[2,1024]{1,0:T(2,128)S(1)}, u32[]{:S(2)}, u32[]{:S(2)}) collective-permute-start(f32[2,1024]{1,0:T(2,128)S(1)} %add.3.refs_1_), channel_id=1, source_target_pairs={{0,2},{1,3},{2,0},{3,1},{4,6},{5,7},{6,4},{7,5},{8,10},{9,11},{10,... | collective-permute-start | bytes 24584 | tf_op jit(solution)/shard_map/ppermute | solution.py:875
  110.0 4.8 %collective-permute-start.34 = (f32[2,1024]{1,0:T(2,128)S(1)}, f32[2,1024]{1,0:T(2,128)S(1)}, u32[]{:S(2)}, u32[]{:S(2)}) collective-permute-start(f32[2,1024]{1,0:T(2,128)S(1)} %add.3.refs_1_), channel_id=1, source_target_pairs={{0,3},{1,2},{2,1},{3,0},{4,7},{5,6},{6,5},{7,4},{8,11},{9,10},{10,... | collective-permute-start | bytes 24584 | tf_op jit(solution)/shard_map/ppermute | solution.py:875
  112.1 13.5 %collective-permute-start.35 = (bf16[528,256]{1,0:T(8,128)(2,1)S(1)}, bf16[528,256]{1,0:T(8,128)(2,1)S(1)}, u32[]{:S(2)}, u32[]{:S(2)}) collective-permute-start(bf16[528,256]{1,0:T(8,128)(2,1)S(1)} %get-tuple-element.199), channel_id=1, source_target_pairs={{0,3},{1,2},{2,1},{3,0},{4,7},{5,6},{6,5},{7,4},{8,11},{9,10},{10,... | collective-permute-start | bytes 811016 | tf_op jit(solution)/shard_map/ppermute | solution.py:875
  113.6 13.6 %collective-permute-start.36 = (bf16[528,256]{1,0:T(8,128)(2,1)S(1)}, bf16[528,256]{1,0:T(8,128)(2,1)S(1)}, u32[]{:S(2)}, u32[]{:S(2)}) collective-permute-start(bf16[528,256]{1,0:T(8,128)(2,1)S(1)} %get-tuple-element.200), channel_id=1, source_target_pairs={{0,2},{1,3},{2,0},{3,1},{4,6},{5,7},{6,4},{7,5},{8,10},{9,11},{10,... | collective-permute-start | bytes 811016 | tf_op jit(solution)/shard_map/ppermute | solution.py:875
  114.6 12.7 %collective-permute-start.37 = (bf16[528,256]{1,0:T(8,128)(2,1)S(1)}, bf16[528,256]{1,0:T(8,128)(2,1)S(1)}, u32[]{:S(2)}, u32[]{:S(2)}) collective-permute-start(bf16[528,256]{1,0:T(8,128)(2,1)S(1)} %get-tuple-element.201), channel_id=1, source_target_pairs={{0,1},{1,0},{2,3},{3,2},{4,5},{5,4},{6,7},{7,6},{8,9},{9,8},{10,11... | collective-permute-start | bytes 811016 | tf_op jit(solution)/shard_map/ppermute | solution.py:875
  130.4 7.0 %collective-permute-start.38 = (bf16[528,256]{1,0:T(8,128)(2,1)S(1)}, bf16[528,256]{1,0:T(8,128)(2,1)S(1)}, u32[]{:S(2)}, u32[]{:S(2)}) collective-permute-start(bf16[528,256]{1,0:T(8,128)(2,1)S(1)} %get-tuple-element.208), channel_id=1, source_target_pairs={{0,16},{16,0},{1,17},{17,1},{2,18},{18,2},{3,19},{19,3},{4,20},{20... | collective-permute-start | bytes 811016 | tf_op jit(solution)/shard_map/ppermute | solution.py:868
  131.0 6.4 %collective-permute-start.39 = (bf16[528,256]{1,0:T(8,128)(2,1)S(1)}, bf16[528,256]{1,0:T(8,128)(2,1)S(1)}, u32[]{:S(2)}, u32[]{:S(2)}) collective-permute-start(bf16[528,256]{1,0:T(8,128)(2,1)S(1)} %get-tuple-element.209), channel_id=1, source_target_pairs={{0,16},{16,0},{1,17},{17,1},{2,18},{18,2},{3,19},{19,3},{4,20},{20... | collective-permute-start | bytes 811016 | tf_op jit(solution)/shard_map/ppermute | solution.py:868
  131.1 6.3 %collective-permute-start.40 = (bf16[528,256]{1,0:T(8,128)(2,1)S(1)}, bf16[528,256]{1,0:T(8,128)(2,1)S(1)}, u32[]{:S(2)}, u32[]{:S(2)}) collective-permute-start(bf16[528,256]{1,0:T(8,128)(2,1)S(1)} %get-tuple-element.210), channel_id=1, source_target_pairs={{0,16},{16,0},{1,17},{17,1},{2,18},{18,2},{3,19},{19,3},{4,20},{20... | collective-permute-start | bytes 811016 | tf_op jit(solution)/shard_map/ppermute | solution.py:868
  131.5 5.9 %collective-permute-start.41 = (bf16[528,256]{1,0:T(8,128)(2,1)S(1)}, bf16[528,256]{1,0:T(8,128)(2,1)S(1)}, u32[]{:S(2)}, u32[]{:S(2)}) collective-permute-start(bf16[528,256]{1,0:T(8,128)(2,1)S(1)} %get-tuple-element.211), channel_id=1, source_target_pairs={{0,16},{16,0},{1,17},{17,1},{2,18},{18,2},{3,19},{19,3},{4,20},{20... | collective-permute-start | bytes 811016 | tf_op jit(solution)/shard_map/ppermute | solution.py:868
  135.0 20.5 %collective-permute-start.45 = (bf16[272,768]{1,0:T(8,128)(2,1)S(1)}, bf16[272,768]{1,0:T(8,128)(2,1)S(1)}, u32[]{:S(2)}, u32[]{:S(2)}) collective-permute-start(bf16[272,768]{1,0:T(8,128)(2,1)S(1)} %get-tuple-element.221), channel_id=1, source_target_pairs={{0,8},{4,12},{8,0},{12,4},{1,9},{5,13},{9,1},{13,5},{2,10},{6,14},... | collective-permute-start | bytes 1253384 | tf_op jit(solution)/shard_map/ppermute | solution.py:1210
  138.7 16.8 %collective-permute-start.42 = (bf16[528,256]{1,0:T(8,128)(2,1)S(1)}, bf16[528,256]{1,0:T(8,128)(2,1)S(1)}, u32[]{:S(2)}, u32[]{:S(2)}) collective-permute-start(bf16[528,256]{1,0:T(8,128)(2,1)S(1)} %get-tuple-element.214), channel_id=1, source_target_pairs={{0,3},{1,2},{2,1},{3,0},{4,7},{5,6},{6,5},{7,4},{8,11},{9,10},{10,... | collective-permute-start | bytes 811016 | tf_op jit(solution)/shard_map/ppermute | solution.py:875
  140.1 15.4 %collective-permute-start.43 = (bf16[528,256]{1,0:T(8,128)(2,1)S(1)}, bf16[528,256]{1,0:T(8,128)(2,1)S(1)}, u32[]{:S(2)}, u32[]{:S(2)}) collective-permute-start(bf16[528,256]{1,0:T(8,128)(2,1)S(1)} %get-tuple-element.215), channel_id=1, source_target_pairs={{0,2},{1,3},{2,0},{3,1},{4,6},{5,7},{6,4},{7,5},{8,10},{9,11},{10,... | collective-permute-start | bytes 811016 | tf_op jit(solution)/shard_map/ppermute | solution.py:875
  141.1 14.4 %collective-permute-start.44 = (bf16[528,256]{1,0:T(8,128)(2,1)S(1)}, bf16[528,256]{1,0:T(8,128)(2,1)S(1)}, u32[]{:S(2)}, u32[]{:S(2)}) collective-permute-start(bf16[528,256]{1,0:T(8,128)(2,1)S(1)} %get-tuple-element.216), channel_id=1, source_target_pairs={{0,1},{1,0},{2,3},{3,2},{4,5},{5,4},{6,7},{7,6},{8,9},{9,8},{10,11... | collective-permute-start | bytes 811016 | tf_op jit(solution)/shard_map/ppermute | solution.py:875
  157.8 8.3 %collective-permute-start.50 = (bf16[528,256]{1,0:T(8,128)(2,1)S(1)}, bf16[528,256]{1,0:T(8,128)(2,1)S(1)}, u32[]{:S(2)}, u32[]{:S(2)}) collective-permute-start(bf16[528,256]{1,0:T(8,128)(2,1)S(1)} %get-tuple-element.223.one_own.refs_0_), channel_id=1, source_target_pairs={{0,3},{1,2},{2,1},{3,0},{4,7},{5,6},{6,5},{7,4},{8,11},{9,10},{10,... | collective-permute-start | bytes 811016 | tf_op jit(solution)/shard_map/ppermute | solution.py:875
  159.2 13.7 %collective-permute-start.51 = (bf16[528,256]{1,0:T(8,128)(2,1)S(1)}, bf16[528,256]{1,0:T(8,128)(2,1)S(1)}, u32[]{:S(2)}, u32[]{:S(2)}) collective-permute-start(bf16[528,256]{1,0:T(8,128)(2,1)S(1)} %get-tuple-element.223.one_own.refs_0_), channel_id=1, source_target_pairs={{0,2},{1,3},{2,0},{3,1},{4,6},{5,7},{6,4},{7,5},{8,10},{9,11},{10,... | collective-permute-start | bytes 811016 | tf_op jit(solution)/shard_map/ppermute | solution.py:875
  160.2 13.2 %collective-permute-start.52 = (bf16[528,256]{1,0:T(8,128)(2,1)S(1)}, bf16[528,256]{1,0:T(8,128)(2,1)S(1)}, u32[]{:S(2)}, u32[]{:S(2)}) collective-permute-start(bf16[528,256]{1,0:T(8,128)(2,1)S(1)} %get-tuple-element.223.one_own.refs_0_), channel_id=1, source_target_pairs={{0,1},{1,0},{2,3},{3,2},{4,5},{5,4},{6,7},{7,6},{8,9},{9,8},{10,11... | collective-permute-start | bytes 811016 | tf_op jit(solution)/shard_map/ppermute | solution.py:875
  160.5 16.8 %collective-permute-start.57 = (bf16[272,768]{1,0:T(8,128)(2,1)S(1)}, bf16[272,768]{1,0:T(8,128)(2,1)S(1)}, u32[]{:S(2)}, u32[]{:S(2)}) collective-permute-start(bf16[272,768]{1,0:T(8,128)(2,1)S(1)} %get-tuple-element.236), channel_id=1, source_target_pairs={{0,4},{4,8},{8,12},{12,0},{1,5},{5,9},{9,13},{13,1},{2,6},{6,10},{... | collective-permute-start | bytes 1253384 | tf_op jit(solution)/shard_map/ppermute | solution.py:1210
  160.8 12.7 %collective-permute-start.46 = (bf16[528,256]{1,0:T(8,128)(2,1)S(1)}, bf16[528,256]{1,0:T(8,128)(2,1)S(1)}, u32[]{:S(2)}, u32[]{:S(2)}) collective-permute-start(bf16[528,256]{1,0:T(8,128)(2,1)S(1)} %get-tuple-element.223.one_own.refs_0_), channel_id=1, source_target_pairs={{0,16},{16,0},{1,17},{17,1},{2,18},{18,2},{3,19},{19,3},{4,20},{20... | collective-permute-start | bytes 811016 | tf_op jit(solution)/shard_map/ppermute | solution.py:868
  166.1 12.5 %collective-permute-start.53 = (bf16[528,256]{1,0:T(8,128)(2,1)S(1)}, bf16[528,256]{1,0:T(8,128)(2,1)S(1)}, u32[]{:S(2)}, u32[]{:S(2)}) collective-permute-start(bf16[528,256]{1,0:T(8,128)(2,1)S(1)} %collective-permute-done.50.refs_1_), channel_id=1, source_target_pairs={{0,16},{16,0},{1,17},{17,1},{2,18},{18,2},{3,19},{19,3},{4,20},{20... | collective-permute-start | bytes 811016 | tf_op jit(solution)/shard_map/ppermute | solution.py:868
  172.9 5.7 %collective-permute-start.54 = (bf16[528,256]{1,0:T(8,128)(2,1)S(1)}, bf16[528,256]{1,0:T(8,128)(2,1)S(1)}, u32[]{:S(2)}, u32[]{:S(2)}) collective-permute-start(bf16[528,256]{1,0:T(8,128)(2,1)S(1)} %collective-permute-done.51.refs_2_), channel_id=1, source_target_pairs={{0,16},{16,0},{1,17},{17,1},{2,18},{18,2},{3,19},{19,3},{4,20},{20... | collective-permute-start | bytes 811016 | tf_op jit(solution)/shard_map/ppermute | solution.py:868
  173.4 9.4 %collective-permute-start.55 = (bf16[528,256]{1,0:T(8,128)(2,1)S(1)}, bf16[528,256]{1,0:T(8,128)(2,1)S(1)}, u32[]{:S(2)}, u32[]{:S(2)}) collective-permute-start(bf16[528,256]{1,0:T(8,128)(2,1)S(1)} %collective-permute-done.52.refs_3_), channel_id=1, source_target_pairs={{0,16},{16,0},{1,17},{17,1},{2,18},{18,2},{3,19},{19,3},{4,20},{20... | collective-permute-start | bytes 811016 | tf_op jit(solution)/shard_map/ppermute | solution.py:868
  175.0 18.9 %collective-permute-start.58 = (bf16[272,768]{1,0:T(8,128)(2,1)S(1)}, bf16[272,768]{1,0:T(8,128)(2,1)S(1)}, u32[]{:S(2)}, u32[]{:S(2)}) collective-permute-start(bf16[272,768]{1,0:T(8,128)(2,1)S(1)} %get-tuple-element.243), channel_id=1, source_target_pairs={{0,12},{4,0},{8,4},{12,8},{1,13},{5,1},{9,5},{13,9},{2,14},{6,2},{... | collective-permute-start | bytes 1253384 | tf_op jit(solution)/shard_map/ppermute | solution.py:1210
  177.3 25.1 %collective-permute-start.59 = (bf16[272,256]{1,0:T(8,128)(2,1)S(1)}, bf16[272,256]{1,0:T(8,128)(2,1)S(1)}, u32[]{:S(2)}, u32[]{:S(2)}) collective-permute-start(bf16[272,256]{1,0:T(8,128)(2,1)S(1)} %get-tuple-element.246), channel_id=1, source_target_pairs={{0,3},{1,2},{2,1},{3,0},{4,7},{5,6},{6,5},{7,4},{8,11},{9,10},{10,... | collective-permute-start | bytes 417800 | tf_op jit(solution)/shard_map/ppermute | solution.py:875
  178.6 16.4 %collective-permute-start.47 = (bf16[256,256]{1,0:T(8,128)(2,1)S(1)}, bf16[256,256]{1,0:T(8,128)(2,1)S(1)}, u32[]{:S(2)}, u32[]{:S(2)}) collective-permute-start(bf16[256,256]{1,0:T(8,128)(2,1)S(1)} %get-tuple-element.225), channel_id=1, source_target_pairs={{0,4},{4,8},{8,12},{12,0},{1,5},{5,9},{9,13},{13,1},{2,6},{6,10},{... | collective-permute-start | bytes 393224 | tf_op jit(solution)/shard_map/ppermute | solution.py:872
  178.7 20.2 %collective-permute-start.48 = (bf16[256,256]{1,0:T(8,128)(2,1)S(1)}, bf16[256,256]{1,0:T(8,128)(2,1)S(1)}, u32[]{:S(2)}, u32[]{:S(2)}) collective-permute-start(bf16[256,256]{1,0:T(8,128)(2,1)S(1)} %get-tuple-element.226), channel_id=1, source_target_pairs={{0,8},{4,12},{8,0},{12,4},{1,9},{5,13},{9,1},{13,5},{2,10},{6,14},... | collective-permute-start | bytes 393224 | tf_op jit(solution)/shard_map/ppermute | solution.py:872
  182.8 16.0 %collective-permute-start.49 = (bf16[256,256]{1,0:T(8,128)(2,1)S(1)}, bf16[256,256]{1,0:T(8,128)(2,1)S(1)}, u32[]{:S(2)}, u32[]{:S(2)}) collective-permute-start(bf16[256,256]{1,0:T(8,128)(2,1)S(1)} %get-tuple-element.227), channel_id=1, source_target_pairs={{0,12},{4,0},{8,4},{12,8},{1,13},{5,1},{9,5},{13,9},{2,14},{6,2},{... | collective-permute-start | bytes 393224 | tf_op jit(solution)/shard_map/ppermute | solution.py:872
  194.0 8.4 %collective-permute-start.60 = (bf16[272,256]{1,0:T(8,128)(2,1)S(1)}, bf16[272,256]{1,0:T(8,128)(2,1)S(1)}, u32[]{:S(2)}, u32[]{:S(2)}) collective-permute-start(bf16[272,256]{1,0:T(8,128)(2,1)S(1)} %get-tuple-element.247), channel_id=1, source_target_pairs={{0,2},{1,3},{2,0},{3,1},{4,6},{5,7},{6,4},{7,5},{8,10},{9,11},{10,... | collective-permute-start | bytes 417800 | tf_op jit(solution)/shard_map/ppermute | solution.py:875
  195.0 7.3 %collective-permute-start.61 = (bf16[272,256]{1,0:T(8,128)(2,1)S(1)}, bf16[272,256]{1,0:T(8,128)(2,1)S(1)}, u32[]{:S(2)}, u32[]{:S(2)}) collective-permute-start(bf16[272,256]{1,0:T(8,128)(2,1)S(1)} %get-tuple-element.248), channel_id=1, source_target_pairs={{0,1},{1,0},{2,3},{3,2},{4,5},{5,4},{6,7},{7,6},{8,9},{9,8},{10,11... | collective-permute-start | bytes 417800 | tf_op jit(solution)/shard_map/ppermute | solution.py:875
  202.3 10.3 %collective-permute-start.66 = (bf16[272,768]{1,0:T(8,128)(2,1)S(1)}, bf16[272,768]{1,0:T(8,128)(2,1)S(1)}, u32[]{:S(2)}, u32[]{:S(2)}) collective-permute-start(bf16[272,768]{1,0:T(8,128)(2,1)S(1)} %get-tuple-element.260), channel_id=1, source_target_pairs={{0,4},{4,8},{8,12},{12,0},{1,5},{5,9},{9,13},{13,1},{2,6},{6,10},{... | collective-permute-start | bytes 1253384 | tf_op jit(solution)/shard_map/ppermute | solution.py:1210
  206.6 5.9 %collective-permute-start.64 = (bf16[528,256]{1,0:T(8,128)(2,1)S(1)}, bf16[528,256]{1,0:T(8,128)(2,1)S(1)}, u32[]{:S(2)}, u32[]{:S(2)}) collective-permute-start(bf16[528,256]{1,0:T(8,128)(2,1)S(1)} %get-tuple-element.253), channel_id=1, source_target_pairs={{0,16},{16,0},{1,17},{17,1},{2,18},{18,2},{3,19},{19,3},{4,20},{20... | collective-permute-start | bytes 811016 | tf_op jit(solution)/shard_map/ppermute | solution.py:868
  207.0 5.5 %collective-permute-start.65 = (bf16[528,256]{1,0:T(8,128)(2,1)S(1)}, bf16[528,256]{1,0:T(8,128)(2,1)S(1)}, u32[]{:S(2)}, u32[]{:S(2)}) collective-permute-start(bf16[528,256]{1,0:T(8,128)(2,1)S(1)} %get-tuple-element.254), channel_id=1, source_target_pairs={{0,16},{16,0},{1,17},{17,1},{2,18},{18,2},{3,19},{19,3},{4,20},{20... | collective-permute-start | bytes 811016 | tf_op jit(solution)/shard_map/ppermute | solution.py:868
  207.7 30.5 %collective-permute-start.70 = (bf16[272,768]{1,0:T(8,128)(2,1)S(1)}, bf16[272,768]{1,0:T(8,128)(2,1)S(1)}, u32[]{:S(2)}, u32[]{:S(2)}) collective-permute-start(bf16[272,768]{1,0:T(8,128)(2,1)S(1)} %get-tuple-element.269), channel_id=1, source_target_pairs={{0,8},{4,12},{8,0},{12,4},{1,9},{5,13},{9,1},{13,5},{2,10},{6,14},... | collective-permute-start | bytes 1253384 | tf_op jit(solution)/shard_map/ppermute | solution.py:1210
  210.8 31.7 %collective-permute-start.71 = (bf16[272,768]{1,0:T(8,128)(2,1)S(1)}, bf16[272,768]{1,0:T(8,128)(2,1)S(1)}, u32[]{:S(2)}, u32[]{:S(2)}) collective-permute-start(bf16[272,768]{1,0:T(8,128)(2,1)S(1)} %get-tuple-element.270), channel_id=1, source_target_pairs={{0,12},{4,0},{8,4},{12,8},{1,13},{5,1},{9,5},{13,9},{2,14},{6,2},{... | collective-permute-start | bytes 1253384 | tf_op jit(solution)/shard_map/ppermute | solution.py:1210
  213.7 28.8 %collective-permute-start.67 = (bf16[800,256]{1,0:T(8,128)(2,1)S(1)}, bf16[800,256]{1,0:T(8,128)(2,1)S(1)}, u32[]{:S(2)}, u32[]{:S(2)}) collective-permute-start(bf16[800,256]{1,0:T(8,128)(2,1)S(1)} %get-tuple-element.262), channel_id=1, source_target_pairs={{0,3},{1,2},{2,1},{3,0},{4,7},{5,6},{6,5},{7,4},{8,11},{9,10},{10,... | collective-permute-start | bytes 1228808 | tf_op jit(solution)/shard_map/ppermute | solution.py:875
  214.7 27.7 %collective-permute-start.68 = (bf16[800,256]{1,0:T(8,128)(2,1)S(1)}, bf16[800,256]{1,0:T(8,128)(2,1)S(1)}, u32[]{:S(2)}, u32[]{:S(2)}) collective-permute-start(bf16[800,256]{1,0:T(8,128)(2,1)S(1)} %get-tuple-element.263), channel_id=1, source_target_pairs={{0,2},{1,3},{2,0},{3,1},{4,6},{5,7},{6,4},{7,5},{8,10},{9,11},{10,... | collective-permute-start | bytes 1228808 | tf_op jit(solution)/shard_map/ppermute | solution.py:875
  215.9 26.6 %collective-permute-start.69 = (bf16[800,256]{1,0:T(8,128)(2,1)S(1)}, bf16[800,256]{1,0:T(8,128)(2,1)S(1)}, u32[]{:S(2)}, u32[]{:S(2)}) collective-permute-start(bf16[800,256]{1,0:T(8,128)(2,1)S(1)} %get-tuple-element.264), channel_id=1, source_target_pairs={{0,1},{1,0},{2,3},{3,2},{4,5},{5,4},{6,7},{7,6},{8,9},{9,8},{10,11... | collective-permute-start | bytes 1228808 | tf_op jit(solution)/shard_map/ppermute | solution.py:875
  247.6 17.6 %collective-permute-start.76 = (bf16[272,768]{1,0:T(8,128)(2,1)S(1)}, bf16[272,768]{1,0:T(8,128)(2,1)S(1)}, u32[]{:S(2)}, u32[]{:S(2)}) collective-permute-start(bf16[272,768]{1,0:T(8,128)(2,1)S(1)} %get-tuple-element.285), channel_id=1, source_target_pairs={{0,16},{16,0},{1,17},{17,1},{2,18},{18,2},{3,19},{19,3},{4,20},{20... | collective-permute-start | bytes 1253384 | tf_op jit(solution)/shard_map/ppermute | solution.py:868
  248.0 5.8 %collective-permute-start.73 = (bf16[336,256]{1,0:T(8,128)(2,1)S(1)}, bf16[336,256]{1,0:T(8,128)(2,1)S(1)}, u32[]{:S(2)}, u32[]{:S(2)}) collective-permute-start(bf16[336,256]{1,0:T(8,128)(2,1)S(1)} %get-tuple-element.277), channel_id=1, source_target_pairs={{0,4},{4,8},{8,12},{12,0},{1,5},{5,9},{9,13},{13,1},{2,6},{6,10},{... | collective-permute-start | bytes 516104 | tf_op jit(solution)/shard_map/ppermute | solution.py:872
  248.0 14.9 %collective-permute-start.74 = (bf16[336,256]{1,0:T(8,128)(2,1)S(1)}, bf16[336,256]{1,0:T(8,128)(2,1)S(1)}, u32[]{:S(2)}, u32[]{:S(2)}) collective-permute-start(bf16[336,256]{1,0:T(8,128)(2,1)S(1)} %get-tuple-element.278), channel_id=1, source_target_pairs={{0,8},{4,12},{8,0},{12,4},{1,9},{5,13},{9,1},{13,5},{2,10},{6,14},... | collective-permute-start | bytes 516104 | tf_op jit(solution)/shard_map/ppermute | solution.py:872
  248.0 15.2 %collective-permute-start.75 = (bf16[336,256]{1,0:T(8,128)(2,1)S(1)}, bf16[336,256]{1,0:T(8,128)(2,1)S(1)}, u32[]{:S(2)}, u32[]{:S(2)}) collective-permute-start(bf16[336,256]{1,0:T(8,128)(2,1)S(1)} %get-tuple-element.279), channel_id=1, source_target_pairs={{0,12},{4,0},{8,4},{12,8},{1,13},{5,1},{9,5},{13,9},{2,14},{6,2},{... | collective-permute-start | bytes 516104 | tf_op jit(solution)/shard_map/ppermute | solution.py:872
  (33 other events, 271.8 us)

commit v3 on v2

--- a/solution.py
+++ b/solution.py
@@ -17,7 +17,7 @@
 NN = ((1,), (0,))
 NT = ((1,), (1,))
 TN = ((0,), (0,))
-VMEM_BYTES = 28 * 1024 * 1024
+VMEM_BYTES = 22 * 1024 * 1024
 ALL_VMEM_BYTES = 63 * 1024 * 1024
 
 

time: 268 us -> 267 us (level)
  no operation moved by 1% of the time
where the time goes in v3:
time: 267 us; the launch traced here: 266 us
  waiting for transfers between devices  92.7 us (35%)
  Pallas kernels  89.6 us (34%)
  starting transfers between devices  78.3 us (29%)
  local copies, waits for them, and re-layouts  3.34 us (1%)
    ppermute x6, waiting for transfers between devices, shifted(): lax.ppermute(x, 'seq', [(i, (i + r) % seq) for i in range(seq)])  37.6 us
    ppermute x35, starting transfers between devices, cross(): return lax.ppermute(x, 'section', swap)  34.2 us
    ppermute x24, waiting for transfers between devices, over_heads(): lax.ppermute(x, 'head', [(i, i ^ d) for i in range(head_axis)])  23.7 us
    pallas_call x2, Pallas kernels, call(): pl.pallas_call(functools.partial(forward_kernel, sz, layer, slots), grid_...  23.6 us
    ppermute x12, waiting for transfers between devices, turn(): return lax.ppermute(x, 'seq', pairs) if r else x  22.1 us
    pallas_call x2, Pallas kernels, call(): pl.pallas_call(functools.partial(backward_kernel, sz, layer, len(deps)),...  21.9 us
    ppermute x24, starting transfers between devices, over_heads(): lax.ppermute(x, 'head', [(i, i ^ d) for i in range(head_axis)])  21.7 us
    ppermute x12, starting transfers between devices, turn(): return lax.ppermute(x, 'seq', pairs) if r else x  12.7 us
  transfers between devices with their start and end apart: 77, of which 25 were waited for; matrix products, arithmetic and copies ran while one was open for 0% of the time, Pallas kernels for 23%

profile of v3, /device:TPU:9, one launch (start us, length us, event | category | flops | bytes accessed | tf_op | source)
XLA Modules:
  0.0 265.7 jit_solution(15518514464345556650)
XLA Ops:
  1.2 3.0 %shard_map.212 = (bf16[144,1024]{1,0:T(8,128)(2,1)}, bf16[144,1024]{1,0:T(8,128)(2,1)}, bf16[144,1024]{1,0:T(8,128)(2,1)}, bf16[144,1024]{1,0:T(8,128)(2,1)}, s32[4]{0:T(128)}) custom-call(s32[4]{0:T(128)} %pad_add_fusion.sc, s32[4]{0:T(128)} %order.3, bf16[4,256,1024]{2,1,0:T(8,128)(2,1)} %tokens.1, f32[1,4,8,256]{3,2,1,0:T(8,128)} %rates.1), custom_call_target="tpu_custom_call" | custom-call | tf_op jit(solution)/shard_map/pallas_call | solution.py:899
  4.3 1.3 collective-permute-start
  6.7 4.1 %shard_map.213 = (bf16[1024,256]{1,0:T(8,128)(2,1)}, bf16[1024,256]{1,0:T(8,128)(2,1)}, bf16[256,1024]{1,0:T(8,128)(2,1)}, f32[16,1024]{1,0:T(8,128)}, f32[16,10...) custom-call(s32[4]{0:T(128)} %get-tuple-element.153.sc, ...), custom_call_target="tpu_custom_call" | custom-call | tf_op jit(solution)/shard_map/pallas_call | solution.py:911
  11.9 1.7 collective-permute-start.2
  14.3 12.6 %collective-permute-start.9 = (bf16[1024,256]{1,0:T(8,128)(2,1)}, bf16[1024,256]{1,0:T(8,128)(2,1)S(1)}, u32[]{:S(2)}, u32[]{:S(2)}) collective-permute-start(bf16[1024,256]{1,0:T(8,128)(2,1)} %get-tuple-element.161), channel_id=1, source_target_pairs={{0,16},{16,0},{1,17},{17,1},{2,18},{18,2},{3,19},{19,3},{4,20},{20... | collective-permute-start | bytes 1572872 | tf_op jit(solution)/shard_map/ppermute | solution.py:868
  26.9 3.6 %collective-permute-done.1.refs_2_ = bf16[144,1024]{1,0:T(8,128)(2,1)} collective-permute-done((bf16[144,1024]{1,0:T(8,128)(2,1)}, bf16[144,1024]{1,0:T(8,128)(2,1)}, u32[]{:S(2)}, u32[]{:S(2)}) %collective-permute-start.1) | collective-permute-done | bytes 294944 | tf_op jit(solution)/shard_map/ppermute | solution.py:872
  30.6 1.5 collective-permute-start.10
  32.1 1.2 collective-permute-done.2.refs_3_
  36.3 1.2 copy-done.1
  37.5 1.2 copy-done.3
  39.6 13.7 %shard_map.214 = (bf16[1024,1024]{1,0:T(8,128)(2,1)S(1)}, f32[1024,256]{1,0:T(8,128)S(1)}, bf16[1024,512]{1,0:T(8,128)(2,1)S(1)}, f32[1024,256]{1,0:T(8,128)S(1)...) custom-call(s32[4]{0:T(128)S(1)} %copy-done.8, ...), custom_call_target="tpu_custom_call" | custom-call | flops 12884901888 | bytes 16000000 | tf_op jit(solution)/shard_map/pallas_call | solution.py:962
  53.4 1.4 shard_map.215
  55.5 2.3 collective-permute-done.14.refs_0_
  58.9 2.2 collective-permute-start.15
  61.7 2.3 collective-permute-start.25
  64.0 1.5 collective-permute-start.26
  65.5 2.2 shard_map.217
  67.6 2.0 collective-permute-start.27
  69.6 4.5 %collective-permute-done.16.refs_2_ = bf16[528,256]{1,0:T(8,128)(2,1)S(1)} collective-permute-done((bf16[528,256]{1,0:T(8,128)(2,1)S(1)}, bf16[528,256]{1,0:T(8,128)(2,1)S(1)}, u32[]{:S(2)}, u32[]{:S(2)}) %collective-permute-start.16) | collective-permute-done | bytes 270368 | tf_op jit(solution)/shard_map/ppermute | solution.py:875
  75.7 1.5 collective-permute-start.18
  79.4 5.1 %collective-permute-done.18.refs_1_ = bf16[512,256]{1,0:T(8,128)(2,1)S(1)} collective-permute-done((bf16[512,256]{1,0:T(8,128)(2,1)S(1)}, bf16[512,256]{1,0:T(8,128)(2,1)S(1)}, u32[]{:S(2)}, u32[]{:S(2)}) %collective-permute-start.18) | collective-permute-done | bytes 262176 | tf_op jit(solution)/shard_map/ppermute | solution.py:875
  84.5 1.3 collective-permute-start.22
  85.9 4.6 %collective-permute-done.19.refs_2_ = bf16[512,256]{1,0:T(8,128)(2,1)S(1)} collective-permute-done((bf16[512,256]{1,0:T(8,128)(2,1)S(1)}, bf16[512,256]{1,0:T(8,128)(2,1)S(1)}, u32[]{:S(2)}, u32[]{:S(2)}) %collective-permute-start.19) | collective-permute-done | bytes 262176 | tf_op jit(solution)/shard_map/ppermute | solution.py:875
  92.5 9.9 %shard_map.219 = (bf16[1024,1024]{1,0:T(8,128)(2,1)S(1)}, f32[1024,256]{1,0:T(8,128)S(1)}, bf16[1024,512]{1,0:T(8,128)(2,1)S(1)}, f32[1024,256]{1,0:T(8,128)S(1)...) custom-call(s32[4]{0:T(128)S(1)} %copy-done.8, ...), custom_call_target="tpu_custom_call" | custom-call | flops 12884901888 | bytes 16000000 | tf_op jit(solution)/shard_map/pallas_call | solution.py:962
  102.5 1.6 shard_map.220
  104.7 2.2 collective-permute-done.31
  106.9 1.2 collective-permute-start.32
  109.5 1.1 shard_map.221
  110.7 1.5 collective-permute-start.35
  113.4 10.8 %shard_map.222 = (bf16[1024,768]{1,0:T(8,128)(2,1)S(1)}, bf16[1024,256]{1,0:T(8,128)(2,1)S(1)}, bf16[16,768]{1,0:T(8,128)(2,1)S(1)}, f32[8,512]{1,0:T(8,128)S(1)...) custom-call(s32[4]{0:T(128)S(1)} %get-tuple-element.189.sc, ...), custom_call_target="tpu_custom_call" | custom-call | flops 17179869184 | bytes 16000000 | tf_op jit(solution)/shard_map/pallas_call | solution.py:1038
  124.2 1.6 collective-permute-done.36.refs_2_
  125.8 3.1 %shard_map.223 = (bf16[4,528,256]{2,1,0:T(8,128)(2,1)S(1)}, bf16[528,256]{1,0:T(8,128)(2,1)S(1)}, bf16[528,256]{1,0:T(8,128)(2,1)S(1)}, bf16[528,256]{1,0:T(8,12...) custom-call(s32[4]{0:T(128)S(1)} %get-tuple-element.195.sc, ...), custom_call_target="tpu_custom_call" | custom-call | flops 2147483648 | bytes 8000000 | tf_op jit(solution)/shard_map/pallas_call | solution.py:1115
  130.2 3.4 %shard_map.224 = (s32[4]{0:T(128)S(1)}, bf16[272,768]{1,0:T(8,128)(2,1)S(1)}, bf16[272,768]{1,0:T(8,128)(2,1)S(1)}, bf16[272,768]{1,0:T(8,128)(2,1)S(1)}, bf16[2...) custom-call(s32[4]{0:T(128)S(1)} %get-tuple-element.202.sc, ...), custom_call_target="tpu_custom_call" | custom-call | flops 8589934592 | bytes 12000000 | tf_op jit(solution)/shard_map/pallas_call | solution.py:1196
  133.6 2.4 collective-permute-start.45
  136.0 1.3 shard_map.225
  137.3 1.4 collective-permute-start.42
  140.0 14.1 %collective-permute-done.45.refs_10_.refs_2_ = bf16[272,768]{1,0:T(8,128)(2,1)S(1)} collective-permute-done((bf16[272,768]{1,0:T(8,128)(2,1)S(1)}, bf16[272,768]{1,0:T(8,128)(2,1)S(1)}, u32[]{:S(2)}, u32[]{:S(2)}) %collective-permute-start.45) | collective-permute-done | bytes 417824 | tf_op jit(solution)/shard_map/ppermute | solution.py:1210
  154.1 2.2 shard_map.226
  156.3 1.4 collective-permute-start.50
  159.3 1.6 collective-permute-start.46
  160.9 3.7 %collective-permute-done.50.refs_1_ = bf16[528,256]{1,0:T(8,128)(2,1)S(1)} collective-permute-done((bf16[528,256]{1,0:T(8,128)(2,1)S(1)}, bf16[528,256]{1,0:T(8,128)(2,1)S(1)}, u32[]{:S(2)}, u32[]{:S(2)}) %collective-permute-start.50) | collective-permute-done | bytes 270368 | tf_op jit(solution)/shard_map/ppermute | solution.py:875
  164.6 2.7 %collective-permute-start.53 = (bf16[528,256]{1,0:T(8,128)(2,1)S(1)}, bf16[528,256]{1,0:T(8,128)(2,1)S(1)}, u32[]{:S(2)}, u32[]{:S(2)}) collective-permute-start(bf16[528,256]{1,0:T(8,128)(2,1)S(1)} %collective-permute-done.50.refs_1_), channel_id=1, source_target_pairs={{0,16},{16,0},{1,17},{17,1},{2,18},{18,2},{3,19},{19,3},{4,20},{20... | collective-permute-start | bytes 811016 | tf_op jit(solution)/shard_map/ppermute | solution.py:868
  167.4 4.1 %collective-permute-done.51.refs_2_ = bf16[528,256]{1,0:T(8,128)(2,1)S(1)} collective-permute-done((bf16[528,256]{1,0:T(8,128)(2,1)S(1)}, bf16[528,256]{1,0:T(8,128)(2,1)S(1)}, u32[]{:S(2)}, u32[]{:S(2)}) %collective-permute-start.51) | collective-permute-done | bytes 270368 | tf_op jit(solution)/shard_map/ppermute | solution.py:875
  173.6 2.2 collective-permute-start.58
  175.8 1.4 collective-permute-start.59
  177.2 4.2 %collective-permute-start.48 = (bf16[256,256]{1,0:T(8,128)(2,1)S(1)}, bf16[256,256]{1,0:T(8,128)(2,1)S(1)}, u32[]{:S(2)}, u32[]{:S(2)}) collective-permute-start(bf16[256,256]{1,0:T(8,128)(2,1)S(1)} %get-tuple-element.226), channel_id=1, source_target_pairs={{0,8},{4,12},{8,0},{12,4},{1,9},{5,13},{9,1},{13,5},{2,10},{6,14},... | collective-permute-start | bytes 393224 | tf_op jit(solution)/shard_map/ppermute | solution.py:872
  181.4 11.1 %shard_map.229 = (bf16[1024,768]{1,0:T(8,128)(2,1)S(1)}, bf16[1024,256]{1,0:T(8,128)(2,1)S(1)}, bf16[16,768]{1,0:T(8,128)(2,1)S(1)}, f32[8,512]{1,0:T(8,128)S(1)...) custom-call(s32[4]{0:T(128)S(1)} %copy-done.8, ...), custom_call_target="tpu_custom_call" | custom-call | flops 17179869184 | bytes 16000000 | tf_op jit(solution)/shard_map/pallas_call | solution.py:1038
  193.8 3.5 %collective-permute-done.48.refs_1_.refs_2_ = bf16[256,256]{1,0:T(8,128)(2,1)S(1)} collective-permute-done((bf16[256,256]{1,0:T(8,128)(2,1)S(1)}, bf16[256,256]{1,0:T(8,128)(2,1)S(1)}, u32[]{:S(2)}, u32[]{:S(2)}) %collective-permute-start.48) | collective-permute-done | bytes 131104 | tf_op jit(solution)/shard_map/ppermute | solution.py:872
  197.4 3.5 %shard_map.230 = (s32[4]{0:T(128)S(1)}, bf16[272,768]{1,0:T(8,128)(2,1)S(1)}, bf16[272,768]{1,0:T(8,128)(2,1)S(1)}, bf16[272,768]{1,0:T(8,128)(2,1)S(1)}, bf16[2...) custom-call(s32[4]{0:T(128)S(1)} %get-tuple-element.237.sc, ...), custom_call_target="tpu_custom_call" | custom-call | flops 8589934592 | bytes 12000000 | tf_op jit(solution)/shard_map/pallas_call | solution.py:1196
  201.0 3.1 %shard_map.231 = (bf16[4,528,256]{2,1,0:T(8,128)(2,1)S(1)}, bf16[528,256]{1,0:T(8,128)(2,1)S(1)}, bf16[528,256]{1,0:T(8,128)(2,1)S(1)}, bf16[528,256]{1,0:T(8,12...) custom-call(s32[4]{0:T(128)S(1)} %get-tuple-element.244.sc, ...), custom_call_target="tpu_custom_call" | custom-call | flops 2147483648 | bytes 8000000 | tf_op jit(solution)/shard_map/pallas_call | solution.py:1115
  206.2 3.1 %collective-permute-start.70 = (bf16[272,768]{1,0:T(8,128)(2,1)S(1)}, bf16[272,768]{1,0:T(8,128)(2,1)S(1)}, u32[]{:S(2)}, u32[]{:S(2)}) collective-permute-start(bf16[272,768]{1,0:T(8,128)(2,1)S(1)} %get-tuple-element.269), channel_id=1, source_target_pairs={{0,8},{4,12},{8,0},{12,4},{1,9},{5,13},{9,1},{13,5},{2,10},{6,14},... | collective-permute-start | bytes 1253384 | tf_op jit(solution)/shard_map/ppermute | solution.py:1210
  209.3 1.7 collective-permute-start.71
  213.3 1.2 collective-permute-start.68
  215.8 1.8 shard_map.228
  217.6 19.2 %collective-permute-done.70.refs_14_.refs_2_ = bf16[272,768]{1,0:T(8,128)(2,1)S(1)} collective-permute-done((bf16[272,768]{1,0:T(8,128)(2,1)S(1)}, bf16[272,768]{1,0:T(8,128)(2,1)S(1)}, u32[]{:S(2)}, u32[]{:S(2)}) %collective-permute-start.70) | collective-permute-done | bytes 417824 | tf_op jit(solution)/shard_map/ppermute | solution.py:1210
  236.8 4.3 %collective-permute-done.71.refs_15_.refs_3_ = bf16[272,768]{1,0:T(8,128)(2,1)S(1)} collective-permute-done((bf16[272,768]{1,0:T(8,128)(2,1)S(1)}, bf16[272,768]{1,0:T(8,128)(2,1)S(1)}, u32[]{:S(2)}, u32[]{:S(2)}) %collective-permute-start.71) | collective-permute-done | bytes 417824 | tf_op jit(solution)/shard_map/ppermute | solution.py:1210
  241.0 1.2 shard_map.234
  242.8 1.4 collective-permute-done.72.zero_other.one_other
  244.1 1.2 shard_map.235
  246.6 1.5 collective-permute-start.75
  248.1 4.4 %collective-permute-done.73.refs_5_.refs_1_ = bf16[336,256]{1,0:T(8,128)(2,1)S(1)} collective-permute-done((bf16[336,256]{1,0:T(8,128)(2,1)S(1)}, bf16[336,256]{1,0:T(8,128)(2,1)S(1)}, u32[]{:S(2)}, u32[]{:S(2)}) %collective-permute-start.73) | collective-permute-done | bytes 172064 | tf_op jit(solution)/shard_map/ppermute | solution.py:872
  252.4 9.1 %collective-permute-done.74.refs_6_.refs_2_ = bf16[336,256]{1,0:T(8,128)(2,1)S(1)} collective-permute-done((bf16[336,256]{1,0:T(8,128)(2,1)S(1)}, bf16[336,256]{1,0:T(8,128)(2,1)S(1)}, u32[]{:S(2)}, u32[]{:S(2)}) %collective-permute-start.74) | collective-permute-done | bytes 172064 | tf_op jit(solution)/shard_map/ppermute | solution.py:872
  261.8 2.0 shard_map.236
  263.8 1.9 shard_map.238
  (145 shorter events, 34.0 us)
Async XLA Ops:
  4.3 10.0 %collective-permute-start = (bf16[144,1024]{1,0:T(8,128)(2,1)}, bf16[144,1024]{1,0:T(8,128)(2,1)}, u32[]{:S(2)}, u32[]{:S(2)}) collective-permute-start(bf16[144,1024]{1,0:T(8,128)(2,1)} %get-tuple-element.155), channel_id=1, source_target_pairs={{0,4},{4,8},{8,12},{12,0},{1,5},{5,9},{9,13},{13,1},{2,6},{6,10},{... | collective-permute-start | bytes 884744 | tf_op jit(solution)/shard_map/ppermute | solution.py:872
  5.6 25.0 %collective-permute-start.1 = (bf16[144,1024]{1,0:T(8,128)(2,1)}, bf16[144,1024]{1,0:T(8,128)(2,1)}, u32[]{:S(2)}, u32[]{:S(2)}) collective-permute-start(bf16[144,1024]{1,0:T(8,128)(2,1)} %get-tuple-element.156), channel_id=1, source_target_pairs={{0,8},{4,12},{8,0},{12,4},{1,9},{5,13},{9,1},{13,5},{2,10},{6,14},... | collective-permute-start | bytes 884744 | tf_op jit(solution)/shard_map/ppermute | solution.py:872
  10.8 23.0 %collective-permute-start.8 = (bf16[1024,256]{1,0:T(8,128)(2,1)}, bf16[1024,256]{1,0:T(8,128)(2,1)S(1)}, u32[]{:S(2)}, u32[]{:S(2)}) collective-permute-start(bf16[1024,256]{1,0:T(8,128)(2,1)} %get-tuple-element.160), channel_id=1, source_target_pairs={{0,16},{16,0},{1,17},{17,1},{2,18},{18,2},{3,19},{19,3},{4,20},{20... | collective-permute-start | bytes 1572872 | tf_op jit(solution)/shard_map/ppermute | solution.py:868
  11.9 21.4 %collective-permute-start.2 = (bf16[144,1024]{1,0:T(8,128)(2,1)}, bf16[144,1024]{1,0:T(8,128)(2,1)S(1)}, u32[]{:S(2)}, u32[]{:S(2)}) collective-permute-start(bf16[144,1024]{1,0:T(8,128)(2,1)} %get-tuple-element.157), channel_id=1, source_target_pairs={{0,12},{4,0},{8,4},{12,8},{1,13},{5,1},{9,5},{13,9},{2,14},{6,2},{... | collective-permute-start | bytes 884744 | tf_op jit(solution)/shard_map/ppermute | solution.py:872
  13.7 20.1 %collective-permute-start.3 = (bf16[144,1024]{1,0:T(8,128)(2,1)S(1)}, bf16[144,1024]{1,0:T(8,128)(2,1)S(1)}, u32[]{:S(2)}, u32[]{:S(2)}) collective-permute-start(bf16[144,1024]{1,0:T(8,128)(2,1)S(1)} %copy-done.9), channel_id=1, source_target_pairs={{0,16},{16,0},{1,17},{17,1},{2,18},{18,2},{3,19},{19,3},{4,20},{20... | collective-permute-start | bytes 884744 | tf_op jit(solution)/shard_map/ppermute | solution.py:868
  14.3 20.0 %collective-permute-start.9 = (bf16[1024,256]{1,0:T(8,128)(2,1)}, bf16[1024,256]{1,0:T(8,128)(2,1)S(1)}, u32[]{:S(2)}, u32[]{:S(2)}) collective-permute-start(bf16[1024,256]{1,0:T(8,128)(2,1)} %get-tuple-element.161), channel_id=1, source_target_pairs={{0,16},{16,0},{1,17},{17,1},{2,18},{18,2},{3,19},{19,3},{4,20},{20... | collective-permute-start | bytes 1572872 | tf_op jit(solution)/shard_map/ppermute | solution.py:868
  34.3 19.0 %collective-permute-start.11 = (bf16[256,1024]{1,0:T(8,128)(2,1)}, bf16[256,1024]{1,0:T(8,128)(2,1)S(1)}, u32[]{:S(2)}, u32[]{:S(2)}) collective-permute-start(bf16[256,1024]{1,0:T(8,128)(2,1)} %get-tuple-element.165), channel_id=1, source_target_pairs={{0,16},{16,0},{1,17},{17,1},{2,18},{18,2},{3,19},{19,3},{4,20},{20... | collective-permute-start | bytes 1572872 | tf_op jit(solution)/shard_map/ppermute | solution.py:868
  34.4 18.9 %collective-permute-start.12 = (bf16[128,1024]{1,0:T(8,128)(2,1)}, bf16[128,1024]{1,0:T(8,128)(2,1)S(1)}, u32[]{:S(2)}, u32[]{:S(2)}) collective-permute-start(bf16[128,1024]{1,0:T(8,128)(2,1)} %get-tuple-element.166), channel_id=1, source_target_pairs={{0,4},{4,8},{8,12},{12,0},{1,5},{5,9},{9,13},{13,1},{2,6},{6,10},{... | collective-permute-start | bytes 786440 | tf_op jit(solution)/shard_map/ppermute | solution.py:872
  35.2 18.1 %collective-permute-start.13 = (bf16[128,1024]{1,0:T(8,128)(2,1)}, bf16[128,1024]{1,0:T(8,128)(2,1)S(1)}, u32[]{:S(2)}, u32[]{:S(2)}) collective-permute-start(bf16[128,1024]{1,0:T(8,128)(2,1)} %get-tuple-element.167), channel_id=1, source_target_pairs={{0,12},{4,0},{8,4},{12,8},{1,13},{5,1},{9,5},{13,9},{2,14},{6,2},{... | collective-permute-start | bytes 786440 | tf_op jit(solution)/shard_map/ppermute | solution.py:872
  58.9 8.7 %collective-permute-start.15 = (bf16[528,256]{1,0:T(8,128)(2,1)S(1)}, bf16[528,256]{1,0:T(8,128)(2,1)S(1)}, u32[]{:S(2)}, u32[]{:S(2)}) collective-permute-start(bf16[528,256]{1,0:T(8,128)(2,1)S(1)} %get-tuple-element.171), channel_id=1, source_target_pairs={{0,3},{1,2},{2,1},{3,0},{4,7},{5,6},{6,5},{7,4},{8,11},{9,10},{10,... | collective-permute-start | bytes 811016 | tf_op jit(solution)/shard_map/ppermute | solution.py:875
  61.2 12.9 %collective-permute-start.16 = (bf16[528,256]{1,0:T(8,128)(2,1)S(1)}, bf16[528,256]{1,0:T(8,128)(2,1)S(1)}, u32[]{:S(2)}, u32[]{:S(2)}) collective-permute-start(bf16[528,256]{1,0:T(8,128)(2,1)S(1)} %get-tuple-element.172), channel_id=1, source_target_pairs={{0,2},{1,3},{2,0},{3,1},{4,6},{5,7},{6,4},{7,5},{8,10},{9,11},{10,... | collective-permute-start | bytes 811016 | tf_op jit(solution)/shard_map/ppermute | solution.py:875
  61.4 13.2 %collective-permute-start.17 = (bf16[528,256]{1,0:T(8,128)(2,1)S(1)}, bf16[528,256]{1,0:T(8,128)(2,1)S(1)}, u32[]{:S(2)}, u32[]{:S(2)}) collective-permute-start(bf16[528,256]{1,0:T(8,128)(2,1)S(1)} %get-tuple-element.173), channel_id=1, source_target_pairs={{0,1},{1,0},{2,3},{3,2},{4,5},{5,4},{6,7},{7,6},{8,9},{9,8},{10,11... | collective-permute-start | bytes 811016 | tf_op jit(solution)/shard_map/ppermute | solution.py:875
  61.7 15.5 %collective-permute-start.25 = (bf16[128,1024]{1,0:T(8,128)(2,1)S(1)}, bf16[128,1024]{1,0:T(8,128)(2,1)S(1)}, u32[]{:S(2)}, u32[]{:S(2)}) collective-permute-start(bf16[128,1024]{1,0:T(8,128)(2,1)S(1)} %copy-done.11), channel_id=1, source_target_pairs={{0,8},{4,12},{8,0},{12,4},{1,9},{5,13},{9,1},{13,5},{2,10},{6,14},... | collective-permute-start | bytes 786440 | tf_op jit(solution)/shard_map/ppermute | solution.py:872
  64.0 14.2 %collective-permute-start.26 = (bf16[128,1024]{1,0:T(8,128)(2,1)S(1)}, bf16[128,1024]{1,0:T(8,128)(2,1)S(1)}, u32[]{:S(2)}, u32[]{:S(2)}) collective-permute-start(bf16[128,1024]{1,0:T(8,128)(2,1)S(1)} %copy-done.10), channel_id=1, source_target_pairs={{0,16},{16,0},{1,17},{17,1},{2,18},{18,2},{3,19},{19,3},{4,20},{20... | collective-permute-start | bytes 786440 | tf_op jit(solution)/shard_map/ppermute | solution.py:868
  67.6 10.8 %collective-permute-start.27 = (bf16[128,1024]{1,0:T(8,128)(2,1)S(1)}, bf16[128,1024]{1,0:T(8,128)(2,1)S(1)}, u32[]{:S(2)}, u32[]{:S(2)}) collective-permute-start(bf16[128,1024]{1,0:T(8,128)(2,1)S(1)} %collective-permute-done.12.refs_2_.refs_9_), channel_id=1, source_target_pairs={{0,16},{16,0},{1,17},{17,1},{2,18},{18,2},{3,19},{19,3},{4,20},{20... | collective-permute-start | bytes 786440 | tf_op jit(solution)/shard_map/ppermute | solution.py:868
  74.1 5.2 %collective-permute-start.29 = (bf16[128,1024]{1,0:T(8,128)(2,1)S(1)}, bf16[128,1024]{1,0:T(8,128)(2,1)S(1)}, u32[]{:S(2)}, u32[]{:S(2)}) collective-permute-start(bf16[128,1024]{1,0:T(8,128)(2,1)S(1)} %collective-permute-done.13.refs_3_.refs_11_), channel_id=1, source_target_pairs={{0,16},{16,0},{1,17},{17,1},{2,18},{18,2},{3,19},{19,3},{4,20},{20... | collective-permute-start | bytes 786440 | tf_op jit(solution)/shard_map/ppermute | solution.py:868
  75.7 8.9 %collective-permute-start.18 = (bf16[512,256]{1,0:T(8,128)(2,1)S(1)}, bf16[512,256]{1,0:T(8,128)(2,1)S(1)}, u32[]{:S(2)}, u32[]{:S(2)}) collective-permute-start(bf16[512,256]{1,0:T(8,128)(2,1)S(1)} %get-tuple-element.180.refs_0_.zero_own), channel_id=1, source_target_pairs={{0,3},{1,2},{2,1},{3,0},{4,7},{5,6},{6,5},{7,4},{8,11},{9,10},{10,... | collective-permute-start | bytes 786440 | tf_op jit(solution)/shard_map/ppermute | solution.py:875
  77.2 13.3 %collective-permute-start.19 = (bf16[512,256]{1,0:T(8,128)(2,1)S(1)}, bf16[512,256]{1,0:T(8,128)(2,1)S(1)}, u32[]{:S(2)}, u32[]{:S(2)}) collective-permute-start(bf16[512,256]{1,0:T(8,128)(2,1)S(1)} %get-tuple-element.180.refs_0_.zero_own), channel_id=1, source_target_pairs={{0,2},{1,3},{2,0},{3,1},{4,6},{5,7},{6,4},{7,5},{8,10},{9,11},{10,... | collective-permute-start | bytes 786440 | tf_op jit(solution)/shard_map/ppermute | solution.py:875
  78.2 12.8 %collective-permute-start.20 = (bf16[512,256]{1,0:T(8,128)(2,1)S(1)}, bf16[512,256]{1,0:T(8,128)(2,1)S(1)}, u32[]{:S(2)}, u32[]{:S(2)}) collective-permute-start(bf16[512,256]{1,0:T(8,128)(2,1)S(1)} %get-tuple-element.180.refs_0_.zero_own), channel_id=1, source_target_pairs={{0,1},{1,0},{2,3},{3,2},{4,5},{5,4},{6,7},{7,6},{8,9},{9,8},{10,11... | collective-permute-start | bytes 786440 | tf_op jit(solution)/shard_map/ppermute | solution.py:875
  78.4 12.7 %collective-permute-start.28 = (bf16[128,1024]{1,0:T(8,128)(2,1)S(1)}, bf16[128,1024]{1,0:T(8,128)(2,1)S(1)}, u32[]{:S(2)}, u32[]{:S(2)}) collective-permute-start(bf16[128,1024]{1,0:T(8,128)(2,1)S(1)} %collective-permute-done.25.refs_10_), channel_id=1, source_target_pairs={{0,16},{16,0},{1,17},{17,1},{2,18},{18,2},{3,19},{19,3},{4,20},{20... | collective-permute-start | bytes 786440 | tf_op jit(solution)/shard_map/ppermute | solution.py:868
  79.3 11.7 %collective-permute-start.21 = (bf16[512,256]{1,0:T(8,128)(2,1)S(1)}, bf16[512,256]{1,0:T(8,128)(2,1)S(1)}, u32[]{:S(2)}, u32[]{:S(2)}) collective-permute-start(bf16[512,256]{1,0:T(8,128)(2,1)S(1)} %get-tuple-element.180.refs_0_.zero_own), channel_id=1, source_target_pairs={{0,16},{16,0},{1,17},{17,1},{2,18},{18,2},{3,19},{19,3},{4,20},{20... | collective-permute-start | bytes 786440 | tf_op jit(solution)/shard_map/ppermute | solution.py:868
  84.5 6.5 %collective-permute-start.22 = (bf16[512,256]{1,0:T(8,128)(2,1)S(1)}, bf16[512,256]{1,0:T(8,128)(2,1)S(1)}, u32[]{:S(2)}, u32[]{:S(2)}) collective-permute-start(bf16[512,256]{1,0:T(8,128)(2,1)S(1)} %collective-permute-done.18.refs_1_), channel_id=1, source_target_pairs={{0,16},{16,0},{1,17},{17,1},{2,18},{18,2},{3,19},{19,3},{4,20},{20... | collective-permute-start | bytes 786440 | tf_op jit(solution)/shard_map/ppermute | solution.py:868
  104.1 5.4 %collective-permute-start.30 = (bf16[4,528,256]{2,1,0:T(8,128)(2,1)S(1)}, bf16[4,528,256]{2,1,0:T(8,128)(2,1)S(1)}, u32[]{:S(2)}, u32[]{:S(2)}) collective-permute-start(bf16[4,528,256]{2,1,0:T(8,128)(2,1)S(1)} %get-tuple-element.188), channel_id=1, source_target_pairs={{0,16},{16,0},{1,17},{17,1},{2,18},{18,2},{3,19},{19,3},{4,20},{20... | collective-permute-start | bytes 3244040 | tf_op jit(solution)/shard_map/ppermute | solution.py:868
  106.9 6.3 %collective-permute-start.32 = (f32[2,1024]{1,0:T(2,128)S(1)}, f32[2,1024]{1,0:T(2,128)S(1)}, u32[]{:S(2)}, u32[]{:S(2)}) collective-permute-start(f32[2,1024]{1,0:T(2,128)S(1)} %add.3.refs_1_), channel_id=1, source_target_pairs={{0,1},{1,0},{2,3},{3,2},{4,5},{5,4},{6,7},{7,6},{8,9},{9,8},{10,11... | collective-permute-start | bytes 24584 | tf_op jit(solution)/shard_map/ppermute | solution.py:875
  108.1 5.3 %collective-permute-start.33 = (f32[2,1024]{1,0:T(2,128)S(1)}, f32[2,1024]{1,0:T(2,128)S(1)}, u32[]{:S(2)}, u32[]{:S(2)}) collective-permute-start(f32[2,1024]{1,0:T(2,128)S(1)} %add.3.refs_1_), channel_id=1, source_target_pairs={{0,2},{1,3},{2,0},{3,1},{4,6},{5,7},{6,4},{7,5},{8,10},{9,11},{10,... | collective-permute-start | bytes 24584 | tf_op jit(solution)/shard_map/ppermute | solution.py:875
  108.6 4.8 %collective-permute-start.34 = (f32[2,1024]{1,0:T(2,128)S(1)}, f32[2,1024]{1,0:T(2,128)S(1)}, u32[]{:S(2)}, u32[]{:S(2)}) collective-permute-start(f32[2,1024]{1,0:T(2,128)S(1)} %add.3.refs_1_), channel_id=1, source_target_pairs={{0,3},{1,2},{2,1},{3,0},{4,7},{5,6},{6,5},{7,4},{8,11},{9,10},{10,... | collective-permute-start | bytes 24584 | tf_op jit(solution)/shard_map/ppermute | solution.py:875
  110.7 13.5 %collective-permute-start.35 = (bf16[528,256]{1,0:T(8,128)(2,1)S(1)}, bf16[528,256]{1,0:T(8,128)(2,1)S(1)}, u32[]{:S(2)}, u32[]{:S(2)}) collective-permute-start(bf16[528,256]{1,0:T(8,128)(2,1)S(1)} %get-tuple-element.199), channel_id=1, source_target_pairs={{0,3},{1,2},{2,1},{3,0},{4,7},{5,6},{6,5},{7,4},{8,11},{9,10},{10,... | collective-permute-start | bytes 811016 | tf_op jit(solution)/shard_map/ppermute | solution.py:875
  112.2 13.6 %collective-permute-start.36 = (bf16[528,256]{1,0:T(8,128)(2,1)S(1)}, bf16[528,256]{1,0:T(8,128)(2,1)S(1)}, u32[]{:S(2)}, u32[]{:S(2)}) collective-permute-start(bf16[528,256]{1,0:T(8,128)(2,1)S(1)} %get-tuple-element.200), channel_id=1, source_target_pairs={{0,2},{1,3},{2,0},{3,1},{4,6},{5,7},{6,4},{7,5},{8,10},{9,11},{10,... | collective-permute-start | bytes 811016 | tf_op jit(solution)/shard_map/ppermute | solution.py:875
  113.1 12.7 %collective-permute-start.37 = (bf16[528,256]{1,0:T(8,128)(2,1)S(1)}, bf16[528,256]{1,0:T(8,128)(2,1)S(1)}, u32[]{:S(2)}, u32[]{:S(2)}) collective-permute-start(bf16[528,256]{1,0:T(8,128)(2,1)S(1)} %get-tuple-element.201), channel_id=1, source_target_pairs={{0,1},{1,0},{2,3},{3,2},{4,5},{5,4},{6,7},{7,6},{8,9},{9,8},{10,11... | collective-permute-start | bytes 811016 | tf_op jit(solution)/shard_map/ppermute | solution.py:875
  128.9 7.0 %collective-permute-start.38 = (bf16[528,256]{1,0:T(8,128)(2,1)S(1)}, bf16[528,256]{1,0:T(8,128)(2,1)S(1)}, u32[]{:S(2)}, u32[]{:S(2)}) collective-permute-start(bf16[528,256]{1,0:T(8,128)(2,1)S(1)} %get-tuple-element.208), channel_id=1, source_target_pairs={{0,16},{16,0},{1,17},{17,1},{2,18},{18,2},{3,19},{19,3},{4,20},{20... | collective-permute-start | bytes 811016 | tf_op jit(solution)/shard_map/ppermute | solution.py:868
  129.6 6.4 %collective-permute-start.39 = (bf16[528,256]{1,0:T(8,128)(2,1)S(1)}, bf16[528,256]{1,0:T(8,128)(2,1)S(1)}, u32[]{:S(2)}, u32[]{:S(2)}) collective-permute-start(bf16[528,256]{1,0:T(8,128)(2,1)S(1)} %get-tuple-element.209), channel_id=1, source_target_pairs={{0,16},{16,0},{1,17},{17,1},{2,18},{18,2},{3,19},{19,3},{4,20},{20... | collective-permute-start | bytes 811016 | tf_op jit(solution)/shard_map/ppermute | solution.py:868
  129.7 6.3 %collective-permute-start.40 = (bf16[528,256]{1,0:T(8,128)(2,1)S(1)}, bf16[528,256]{1,0:T(8,128)(2,1)S(1)}, u32[]{:S(2)}, u32[]{:S(2)}) collective-permute-start(bf16[528,256]{1,0:T(8,128)(2,1)S(1)} %get-tuple-element.210), channel_id=1, source_target_pairs={{0,16},{16,0},{1,17},{17,1},{2,18},{18,2},{3,19},{19,3},{4,20},{20... | collective-permute-start | bytes 811016 | tf_op jit(solution)/shard_map/ppermute | solution.py:868
  130.1 5.9 %collective-permute-start.41 = (bf16[528,256]{1,0:T(8,128)(2,1)S(1)}, bf16[528,256]{1,0:T(8,128)(2,1)S(1)}, u32[]{:S(2)}, u32[]{:S(2)}) collective-permute-start(bf16[528,256]{1,0:T(8,128)(2,1)S(1)} %get-tuple-element.211), channel_id=1, source_target_pairs={{0,16},{16,0},{1,17},{17,1},{2,18},{18,2},{3,19},{19,3},{4,20},{20... | collective-permute-start | bytes 811016 | tf_op jit(solution)/shard_map/ppermute | solution.py:868
  133.6 20.5 %collective-permute-start.45 = (bf16[272,768]{1,0:T(8,128)(2,1)S(1)}, bf16[272,768]{1,0:T(8,128)(2,1)S(1)}, u32[]{:S(2)}, u32[]{:S(2)}) collective-permute-start(bf16[272,768]{1,0:T(8,128)(2,1)S(1)} %get-tuple-element.221), channel_id=1, source_target_pairs={{0,8},{4,12},{8,0},{12,4},{1,9},{5,13},{9,1},{13,5},{2,10},{6,14},... | collective-permute-start | bytes 1253384 | tf_op jit(solution)/shard_map/ppermute | solution.py:1210
  137.3 16.8 %collective-permute-start.42 = (bf16[528,256]{1,0:T(8,128)(2,1)S(1)}, bf16[528,256]{1,0:T(8,128)(2,1)S(1)}, u32[]{:S(2)}, u32[]{:S(2)}) collective-permute-start(bf16[528,256]{1,0:T(8,128)(2,1)S(1)} %get-tuple-element.214), channel_id=1, source_target_pairs={{0,3},{1,2},{2,1},{3,0},{4,7},{5,6},{6,5},{7,4},{8,11},{9,10},{10,... | collective-permute-start | bytes 811016 | tf_op jit(solution)/shard_map/ppermute | solution.py:875
  138.7 15.4 %collective-permute-start.43 = (bf16[528,256]{1,0:T(8,128)(2,1)S(1)}, bf16[528,256]{1,0:T(8,128)(2,1)S(1)}, u32[]{:S(2)}, u32[]{:S(2)}) collective-permute-start(bf16[528,256]{1,0:T(8,128)(2,1)S(1)} %get-tuple-element.215), channel_id=1, source_target_pairs={{0,2},{1,3},{2,0},{3,1},{4,6},{5,7},{6,4},{7,5},{8,10},{9,11},{10,... | collective-permute-start | bytes 811016 | tf_op jit(solution)/shard_map/ppermute | solution.py:875
  139.7 14.4 %collective-permute-start.44 = (bf16[528,256]{1,0:T(8,128)(2,1)S(1)}, bf16[528,256]{1,0:T(8,128)(2,1)S(1)}, u32[]{:S(2)}, u32[]{:S(2)}) collective-permute-start(bf16[528,256]{1,0:T(8,128)(2,1)S(1)} %get-tuple-element.216), channel_id=1, source_target_pairs={{0,1},{1,0},{2,3},{3,2},{4,5},{5,4},{6,7},{7,6},{8,9},{9,8},{10,11... | collective-permute-start | bytes 811016 | tf_op jit(solution)/shard_map/ppermute | solution.py:875
  156.3 8.3 %collective-permute-start.50 = (bf16[528,256]{1,0:T(8,128)(2,1)S(1)}, bf16[528,256]{1,0:T(8,128)(2,1)S(1)}, u32[]{:S(2)}, u32[]{:S(2)}) collective-permute-start(bf16[528,256]{1,0:T(8,128)(2,1)S(1)} %get-tuple-element.223.one_own.refs_0_), channel_id=1, source_target_pairs={{0,3},{1,2},{2,1},{3,0},{4,7},{5,6},{6,5},{7,4},{8,11},{9,10},{10,... | collective-permute-start | bytes 811016 | tf_op jit(solution)/shard_map/ppermute | solution.py:875
  157.7 13.7 %collective-permute-start.51 = (bf16[528,256]{1,0:T(8,128)(2,1)S(1)}, bf16[528,256]{1,0:T(8,128)(2,1)S(1)}, u32[]{:S(2)}, u32[]{:S(2)}) collective-permute-start(bf16[528,256]{1,0:T(8,128)(2,1)S(1)} %get-tuple-element.223.one_own.refs_0_), channel_id=1, source_target_pairs={{0,2},{1,3},{2,0},{3,1},{4,6},{5,7},{6,4},{7,5},{8,10},{9,11},{10,... | collective-permute-start | bytes 811016 | tf_op jit(solution)/shard_map/ppermute | solution.py:875
  158.7 13.2 %collective-permute-start.52 = (bf16[528,256]{1,0:T(8,128)(2,1)S(1)}, bf16[528,256]{1,0:T(8,128)(2,1)S(1)}, u32[]{:S(2)}, u32[]{:S(2)}) collective-permute-start(bf16[528,256]{1,0:T(8,128)(2,1)S(1)} %get-tuple-element.223.one_own.refs_0_), channel_id=1, source_target_pairs={{0,1},{1,0},{2,3},{3,2},{4,5},{5,4},{6,7},{7,6},{8,9},{9,8},{10,11... | collective-permute-start | bytes 811016 | tf_op jit(solution)/shard_map/ppermute | solution.py:875
  159.0 16.8 %collective-permute-start.57 = (bf16[272,768]{1,0:T(8,128)(2,1)S(1)}, bf16[272,768]{1,0:T(8,128)(2,1)S(1)}, u32[]{:S(2)}, u32[]{:S(2)}) collective-permute-start(bf16[272,768]{1,0:T(8,128)(2,1)S(1)} %get-tuple-element.236), channel_id=1, source_target_pairs={{0,4},{4,8},{8,12},{12,0},{1,5},{5,9},{9,13},{13,1},{2,6},{6,10},{... | collective-permute-start | bytes 1253384 | tf_op jit(solution)/shard_map/ppermute | solution.py:1210
  159.3 12.7 %collective-permute-start.46 = (bf16[528,256]{1,0:T(8,128)(2,1)S(1)}, bf16[528,256]{1,0:T(8,128)(2,1)S(1)}, u32[]{:S(2)}, u32[]{:S(2)}) collective-permute-start(bf16[528,256]{1,0:T(8,128)(2,1)S(1)} %get-tuple-element.223.one_own.refs_0_), channel_id=1, source_target_pairs={{0,16},{16,0},{1,17},{17,1},{2,18},{18,2},{3,19},{19,3},{4,20},{20... | collective-permute-start | bytes 811016 | tf_op jit(solution)/shard_map/ppermute | solution.py:868
  164.6 12.6 %collective-permute-start.53 = (bf16[528,256]{1,0:T(8,128)(2,1)S(1)}, bf16[528,256]{1,0:T(8,128)(2,1)S(1)}, u32[]{:S(2)}, u32[]{:S(2)}) collective-permute-start(bf16[528,256]{1,0:T(8,128)(2,1)S(1)} %collective-permute-done.50.refs_1_), channel_id=1, source_target_pairs={{0,16},{16,0},{1,17},{17,1},{2,18},{18,2},{3,19},{19,3},{4,20},{20... | collective-permute-start | bytes 811016 | tf_op jit(solution)/shard_map/ppermute | solution.py:868
  171.5 5.7 %collective-permute-start.54 = (bf16[528,256]{1,0:T(8,128)(2,1)S(1)}, bf16[528,256]{1,0:T(8,128)(2,1)S(1)}, u32[]{:S(2)}, u32[]{:S(2)}) collective-permute-start(bf16[528,256]{1,0:T(8,128)(2,1)S(1)} %collective-permute-done.51.refs_2_), channel_id=1, source_target_pairs={{0,16},{16,0},{1,17},{17,1},{2,18},{18,2},{3,19},{19,3},{4,20},{20... | collective-permute-start | bytes 811016 | tf_op jit(solution)/shard_map/ppermute | solution.py:868
  172.0 9.4 %collective-permute-start.55 = (bf16[528,256]{1,0:T(8,128)(2,1)S(1)}, bf16[528,256]{1,0:T(8,128)(2,1)S(1)}, u32[]{:S(2)}, u32[]{:S(2)}) collective-permute-start(bf16[528,256]{1,0:T(8,128)(2,1)S(1)} %collective-permute-done.52.refs_3_), channel_id=1, source_target_pairs={{0,16},{16,0},{1,17},{17,1},{2,18},{18,2},{3,19},{19,3},{4,20},{20... | collective-permute-start | bytes 811016 | tf_op jit(solution)/shard_map/ppermute | solution.py:868
  173.6 18.9 %collective-permute-start.58 = (bf16[272,768]{1,0:T(8,128)(2,1)S(1)}, bf16[272,768]{1,0:T(8,128)(2,1)S(1)}, u32[]{:S(2)}, u32[]{:S(2)}) collective-permute-start(bf16[272,768]{1,0:T(8,128)(2,1)S(1)} %get-tuple-element.243), channel_id=1, source_target_pairs={{0,12},{4,0},{8,4},{12,8},{1,13},{5,1},{9,5},{13,9},{2,14},{6,2},{... | collective-permute-start | bytes 1253384 | tf_op jit(solution)/shard_map/ppermute | solution.py:1210
  175.8 25.1 %collective-permute-start.59 = (bf16[272,256]{1,0:T(8,128)(2,1)S(1)}, bf16[272,256]{1,0:T(8,128)(2,1)S(1)}, u32[]{:S(2)}, u32[]{:S(2)}) collective-permute-start(bf16[272,256]{1,0:T(8,128)(2,1)S(1)} %get-tuple-element.246), channel_id=1, source_target_pairs={{0,3},{1,2},{2,1},{3,0},{4,7},{5,6},{6,5},{7,4},{8,11},{9,10},{10,... | collective-permute-start | bytes 417800 | tf_op jit(solution)/shard_map/ppermute | solution.py:875
  177.2 16.3 %collective-permute-start.47 = (bf16[256,256]{1,0:T(8,128)(2,1)S(1)}, bf16[256,256]{1,0:T(8,128)(2,1)S(1)}, u32[]{:S(2)}, u32[]{:S(2)}) collective-permute-start(bf16[256,256]{1,0:T(8,128)(2,1)S(1)} %get-tuple-element.225), channel_id=1, source_target_pairs={{0,4},{4,8},{8,12},{12,0},{1,5},{5,9},{9,13},{13,1},{2,6},{6,10},{... | collective-permute-start | bytes 393224 | tf_op jit(solution)/shard_map/ppermute | solution.py:872
  177.2 20.2 %collective-permute-start.48 = (bf16[256,256]{1,0:T(8,128)(2,1)S(1)}, bf16[256,256]{1,0:T(8,128)(2,1)S(1)}, u32[]{:S(2)}, u32[]{:S(2)}) collective-permute-start(bf16[256,256]{1,0:T(8,128)(2,1)S(1)} %get-tuple-element.226), channel_id=1, source_target_pairs={{0,8},{4,12},{8,0},{12,4},{1,9},{5,13},{9,1},{13,5},{2,10},{6,14},... | collective-permute-start | bytes 393224 | tf_op jit(solution)/shard_map/ppermute | solution.py:872
  181.4 16.0 %collective-permute-start.49 = (bf16[256,256]{1,0:T(8,128)(2,1)S(1)}, bf16[256,256]{1,0:T(8,128)(2,1)S(1)}, u32[]{:S(2)}, u32[]{:S(2)}) collective-permute-start(bf16[256,256]{1,0:T(8,128)(2,1)S(1)} %get-tuple-element.227), channel_id=1, source_target_pairs={{0,12},{4,0},{8,4},{12,8},{1,13},{5,1},{9,5},{13,9},{2,14},{6,2},{... | collective-permute-start | bytes 393224 | tf_op jit(solution)/shard_map/ppermute | solution.py:872
  192.5 8.4 %collective-permute-start.60 = (bf16[272,256]{1,0:T(8,128)(2,1)S(1)}, bf16[272,256]{1,0:T(8,128)(2,1)S(1)}, u32[]{:S(2)}, u32[]{:S(2)}) collective-permute-start(bf16[272,256]{1,0:T(8,128)(2,1)S(1)} %get-tuple-element.247), channel_id=1, source_target_pairs={{0,2},{1,3},{2,0},{3,1},{4,6},{5,7},{6,4},{7,5},{8,10},{9,11},{10,... | collective-permute-start | bytes 417800 | tf_op jit(solution)/shard_map/ppermute | solution.py:875
  193.5 7.4 %collective-permute-start.61 = (bf16[272,256]{1,0:T(8,128)(2,1)S(1)}, bf16[272,256]{1,0:T(8,128)(2,1)S(1)}, u32[]{:S(2)}, u32[]{:S(2)}) collective-permute-start(bf16[272,256]{1,0:T(8,128)(2,1)S(1)} %get-tuple-element.248), channel_id=1, source_target_pairs={{0,1},{1,0},{2,3},{3,2},{4,5},{5,4},{6,7},{7,6},{8,9},{9,8},{10,11... | collective-permute-start | bytes 417800 | tf_op jit(solution)/shard_map/ppermute | solution.py:875
  200.9 10.3 %collective-permute-start.66 = (bf16[272,768]{1,0:T(8,128)(2,1)S(1)}, bf16[272,768]{1,0:T(8,128)(2,1)S(1)}, u32[]{:S(2)}, u32[]{:S(2)}) collective-permute-start(bf16[272,768]{1,0:T(8,128)(2,1)S(1)} %get-tuple-element.260), channel_id=1, source_target_pairs={{0,4},{4,8},{8,12},{12,0},{1,5},{5,9},{9,13},{13,1},{2,6},{6,10},{... | collective-permute-start | bytes 1253384 | tf_op jit(solution)/shard_map/ppermute | solution.py:1210
  205.1 5.9 %collective-permute-start.64 = (bf16[528,256]{1,0:T(8,128)(2,1)S(1)}, bf16[528,256]{1,0:T(8,128)(2,1)S(1)}, u32[]{:S(2)}, u32[]{:S(2)}) collective-permute-start(bf16[528,256]{1,0:T(8,128)(2,1)S(1)} %get-tuple-element.253), channel_id=1, source_target_pairs={{0,16},{16,0},{1,17},{17,1},{2,18},{18,2},{3,19},{19,3},{4,20},{20... | collective-permute-start | bytes 811016 | tf_op jit(solution)/shard_map/ppermute | solution.py:868
  205.6 5.5 %collective-permute-start.65 = (bf16[528,256]{1,0:T(8,128)(2,1)S(1)}, bf16[528,256]{1,0:T(8,128)(2,1)S(1)}, u32[]{:S(2)}, u32[]{:S(2)}) collective-permute-start(bf16[528,256]{1,0:T(8,128)(2,1)S(1)} %get-tuple-element.254), channel_id=1, source_target_pairs={{0,16},{16,0},{1,17},{17,1},{2,18},{18,2},{3,19},{19,3},{4,20},{20... | collective-permute-start | bytes 811016 | tf_op jit(solution)/shard_map/ppermute | solution.py:868
  206.2 30.5 %collective-permute-start.70 = (bf16[272,768]{1,0:T(8,128)(2,1)S(1)}, bf16[272,768]{1,0:T(8,128)(2,1)S(1)}, u32[]{:S(2)}, u32[]{:S(2)}) collective-permute-start(bf16[272,768]{1,0:T(8,128)(2,1)S(1)} %get-tuple-element.269), channel_id=1, source_target_pairs={{0,8},{4,12},{8,0},{12,4},{1,9},{5,13},{9,1},{13,5},{2,10},{6,14},... | collective-permute-start | bytes 1253384 | tf_op jit(solution)/shard_map/ppermute | solution.py:1210
  209.3 31.7 %collective-permute-start.71 = (bf16[272,768]{1,0:T(8,128)(2,1)S(1)}, bf16[272,768]{1,0:T(8,128)(2,1)S(1)}, u32[]{:S(2)}, u32[]{:S(2)}) collective-permute-start(bf16[272,768]{1,0:T(8,128)(2,1)S(1)} %get-tuple-element.270), channel_id=1, source_target_pairs={{0,12},{4,0},{8,4},{12,8},{1,13},{5,1},{9,5},{13,9},{2,14},{6,2},{... | collective-permute-start | bytes 1253384 | tf_op jit(solution)/shard_map/ppermute | solution.py:1210
  212.3 28.8 %collective-permute-start.67 = (bf16[800,256]{1,0:T(8,128)(2,1)S(1)}, bf16[800,256]{1,0:T(8,128)(2,1)S(1)}, u32[]{:S(2)}, u32[]{:S(2)}) collective-permute-start(bf16[800,256]{1,0:T(8,128)(2,1)S(1)} %get-tuple-element.262), channel_id=1, source_target_pairs={{0,3},{1,2},{2,1},{3,0},{4,7},{5,6},{6,5},{7,4},{8,11},{9,10},{10,... | collective-permute-start | bytes 1228808 | tf_op jit(solution)/shard_map/ppermute | solution.py:875
  213.3 27.8 %collective-permute-start.68 = (bf16[800,256]{1,0:T(8,128)(2,1)S(1)}, bf16[800,256]{1,0:T(8,128)(2,1)S(1)}, u32[]{:S(2)}, u32[]{:S(2)}) collective-permute-start(bf16[800,256]{1,0:T(8,128)(2,1)S(1)} %get-tuple-element.263), channel_id=1, source_target_pairs={{0,2},{1,3},{2,0},{3,1},{4,6},{5,7},{6,4},{7,5},{8,10},{9,11},{10,... | collective-permute-start | bytes 1228808 | tf_op jit(solution)/shard_map/ppermute | solution.py:875
  214.4 26.6 %collective-permute-start.69 = (bf16[800,256]{1,0:T(8,128)(2,1)S(1)}, bf16[800,256]{1,0:T(8,128)(2,1)S(1)}, u32[]{:S(2)}, u32[]{:S(2)}) collective-permute-start(bf16[800,256]{1,0:T(8,128)(2,1)S(1)} %get-tuple-element.264), channel_id=1, source_target_pairs={{0,1},{1,0},{2,3},{3,2},{4,5},{5,4},{6,7},{7,6},{8,9},{9,8},{10,11... | collective-permute-start | bytes 1228808 | tf_op jit(solution)/shard_map/ppermute | solution.py:875
  246.1 17.6 %collective-permute-start.76 = (bf16[272,768]{1,0:T(8,128)(2,1)S(1)}, bf16[272,768]{1,0:T(8,128)(2,1)S(1)}, u32[]{:S(2)}, u32[]{:S(2)}) collective-permute-start(bf16[272,768]{1,0:T(8,128)(2,1)S(1)} %get-tuple-element.285), channel_id=1, source_target_pairs={{0,16},{16,0},{1,17},{17,1},{2,18},{18,2},{3,19},{19,3},{4,20},{20... | collective-permute-start | bytes 1253384 | tf_op jit(solution)/shard_map/ppermute | solution.py:868
  246.6 5.8 %collective-permute-start.73 = (bf16[336,256]{1,0:T(8,128)(2,1)S(1)}, bf16[336,256]{1,0:T(8,128)(2,1)S(1)}, u32[]{:S(2)}, u32[]{:S(2)}) collective-permute-start(bf16[336,256]{1,0:T(8,128)(2,1)S(1)} %get-tuple-element.277), channel_id=1, source_target_pairs={{0,4},{4,8},{8,12},{12,0},{1,5},{5,9},{9,13},{13,1},{2,6},{6,10},{... | collective-permute-start | bytes 516104 | tf_op jit(solution)/shard_map/ppermute | solution.py:872
  246.6 14.9 %collective-permute-start.74 = (bf16[336,256]{1,0:T(8,128)(2,1)S(1)}, bf16[336,256]{1,0:T(8,128)(2,1)S(1)}, u32[]{:S(2)}, u32[]{:S(2)}) collective-permute-start(bf16[336,256]{1,0:T(8,128)(2,1)S(1)} %get-tuple-element.278), channel_id=1, source_target_pairs={{0,8},{4,12},{8,0},{12,4},{1,9},{5,13},{9,1},{13,5},{2,10},{6,14},... | collective-permute-start | bytes 516104 | tf_op jit(solution)/shard_map/ppermute | solution.py:872
  246.6 15.2 %collective-permute-start.75 = (bf16[336,256]{1,0:T(8,128)(2,1)S(1)}, bf16[336,256]{1,0:T(8,128)(2,1)S(1)}, u32[]{:S(2)}, u32[]{:S(2)}) collective-permute-start(bf16[336,256]{1,0:T(8,128)(2,1)S(1)} %get-tuple-element.279), channel_id=1, source_target_pairs={{0,12},{4,0},{8,4},{12,8},{1,13},{5,1},{9,5},{13,9},{2,14},{6,2},{... | collective-permute-start | bytes 516104 | tf_op jit(solution)/shard_map/ppermute | solution.py:872
  (25 other events, 166.2 us)
